TPU v7x, 32 devices: a whole 2x2x4 slice. The times are simulated.
32 devices in a mesh: grp: 2 (over y), lat: 4 (over z), lon: 4 (over x, core).
Axes of the slice: x: 2, y: 2, z: 4, core: 2. Of those that a mesh axis runs over, the one named last changes fastest.
Arguments:
- state: bfloat16 [2, 64, 512, 512], P('grp', 'lat', 'lon'), may hold values from -6 to 6
- intersection_lists: int32 [2, 4, 4, 3, 16], P('grp', 'lat', 'lon'), may hold values from 0 to 31, as said below
- intersection_matrices: bfloat16 [2, 4, 4, 16, 128, 128], P('grp', 'lat', 'lon'), may hold values from -0.5 to 0.5
- water_indicator: int32 [64, 1024], P('lat', 'lon'), may hold values from 0 to 1, as said below
- atmosphere_kernels: bfloat16 [2, 3, 3, 512, 512], replicated, may hold values from -0.09375 to 0.09375
- ocean_kernels: bfloat16 [2, 3, 3, 256, 256], replicated, may hold values from -0.125 to 0.125
- flux_projection: bfloat16 [512, 256], replicated, may hold values from -0.25 to 0.25
- coupling_matrix: bfloat16 [256, 512], replicated, may hold values from -0.375 to 0.375
Outputs:
- new_state: bfloat16 [2, 64, 512, 512], P('grp', 'lat', 'lon')
Inputs may be any that keep to these rules, and one draw needn't show every extreme that they name: intersection_lists[g, i, j] lists the 16 intersections whose source block lies on tile (i, j) of component g (0 atmosphere, 1 ocean). Row 0 is the tile number of the receiving tile of the other component; row 1 the source block, below 16 for atmosphere sources and below 32 for ocean sources; row 2 the receiving block, below 32 on ocean tiles and below 16 on atmosphere tiles. A source tile names one receiving tile at most 2 times, and every source tile names some receiving tile exactly 2 times. `water_indicator`: the share of land differs from tile to tile.
All inputs are finite; a program needn't handle non-finite values.
Results may differ from a plain program's by a relative error of at most 0.01.
Values may be sent and summed in bfloat16 or wider, within the bound.
No kernel may reach another device: no remote copies, remote signals or barrier semaphores. Data moves between devices by JAX's collectives and lax.ppermute only.
A program may use at most 192 MiB of HBM per device.

v0:
```python
import functools

import jax
import jax.numpy as jnp
from jax import lax
from jax.experimental import pallas as pl
from jax.experimental.pallas import tpu as pltpu
from jax.sharding import PartitionSpec as P

LAYERS = 2
BLOCK_ROWS = 8
BLOCK_COLS = 16
BLOCK = BLOCK_ROWS * BLOCK_COLS
SLOTS = 2
HALF = BLOCK // 2
HALF_ROWS = BLOCK_ROWS // 2
VMEM_BYTES = 48 * 2**20

F32 = jnp.float32
BF16 = jnp.bfloat16

VMEM = pl.BlockSpec(memory_space=pltpu.VMEM)
SMEM = pl.BlockSpec(memory_space=pltpu.SMEM)
ANY = pl.BlockSpec(memory_space=pl.ANY)


def silu(v):
    return v / (1.0 + jnp.exp(-v))


def iota(shape, dim):
    return lax.broadcasted_iota(jnp.int32, shape, dim)


def dot(a, b):
    return jnp.dot(a, b, preferred_element_type=F32)


def params(**kwargs):
    return pltpu.CompilerParams(vmem_limit_bytes=VMEM_BYTES, **kwargs)


def on_ocean():
    return lax.axis_index("grp") == 1


def fill_water(water_ref, turned_ref):
    count, cols = water_ref.shape
    turned_ref[:, 0:count] = water_ref[...].astype(F32).T


def water_of_row(turned_ref, rows, r, width, start, size):
    parts = [
        jnp.broadcast_to(turned_ref[start : start + size, p * rows + r : p * rows + r + 1], (size, width))
        for p in range(2)
    ]
    return jnp.concatenate(parts, axis=1)


def payload_kernel(
    lists_ref, state_ref, matrices_ref, water_ref, flux_ref, first_ref, second_ref, flux, surface, turned, count
):
    rows, cols, width = state_ref.shape
    half = width // 2
    entries = matrices_ref.shape[0]
    tiles = first_ref.shape[0] // SLOTS
    ocean = on_ocean()

    def clear(t, _):
        count[t] = 0
        return 0

    lax.fori_loop(0, tiles, clear, 0)
    i = iota((BLOCK, BLOCK), 0)
    j = iota((BLOCK, BLOCK), 1)

    def put(e, payload):
        owner = lists_ref[0, e]
        rank = count[owner]
        count[owner] = rank + 1
        slot = owner * SLOTS + rank
        first_ref[slot] = payload[:HALF]
        second_ref[slot] = payload[HALF:]

    @pl.when(jnp.logical_not(ocean))
    def _():
        p, r, c = (i // 32) % 2, (i // 64) * 4 + (i // 8) % 4, i % 8
        turn = (j == r * BLOCK_COLS + 2 * c + p).astype(BF16)
        step = 4
        for r0 in range(0, rows, step):
            block = state_ref[r0 : r0 + step].reshape(step * cols, width)
            flux[r0 : r0 + step] = dot(block, flux_ref[...]).astype(BF16).reshape(step, cols, half)
        across = cols // BLOCK_COLS

        def entry(e, _):
            source = lists_ref[1, e]
            r0 = (source // across) * BLOCK_ROWS
            c0 = pl.multiple_of((source % across) * BLOCK_COLS, BLOCK_COLS)
            chosen = flux[pl.ds(r0, BLOCK_ROWS), pl.ds(c0, BLOCK_COLS), :].reshape(BLOCK, half)
            weight = dot(turn, matrices_ref[e]).astype(BF16)
            put(e, dot(weight, chosen).astype(BF16))
            return 0

        lax.fori_loop(0, entries, entry, 0, unroll=2)

    @pl.when(ocean)
    def _():
        p, r, c = j // 64, (j // 8) % 8, j % 8
        turn = (i == r * BLOCK_COLS + 2 * c + p).astype(BF16)
        fill_water(water_ref, turned)
        for r0 in range(rows):
            surface[r0] = state_ref[r0].astype(F32) * water_of_row(turned, rows, r0, half, 0, cols)
        wide = BLOCK_COLS // 2
        across = cols // wide

        def entry(e, _):
            source = lists_ref[1, e]
            r0 = (source // across) * BLOCK_ROWS
            c0 = pl.multiple_of((source % across) * wide, wide)
            block = surface[pl.ds(r0, BLOCK_ROWS), pl.ds(c0, wide), :]
            chosen = jnp.concatenate(
                [block[:, :, q * half : (q + 1) * half].reshape(BLOCK // 2, half) for q in range(2)], axis=0
            ).astype(BF16)
            weight = dot(matrices_ref[e], turn).astype(BF16)
            put(e, dot(weight, chosen).astype(BF16))
            return 0

        lax.fori_loop(0, entries, entry, 0, unroll=2)


def payloads(lists, state, matrices, water, flux_projection, tiles):
    rows, cols, width = state.shape
    half = width // 2
    slots = jax.ShapeDtypeStruct((tiles * SLOTS, HALF, half), BF16)
    return pl.pallas_call(
        payload_kernel,
        out_shape=(slots, slots),
        in_specs=[SMEM, VMEM, VMEM, VMEM, VMEM],
        out_specs=(VMEM, VMEM),
        scratch_shapes=[
            pltpu.VMEM((rows, cols, half), BF16),
            pltpu.VMEM((rows, cols, width), F32),
            pltpu.VMEM((cols, 128), F32),
            pltpu.SMEM((tiles,), jnp.int32),
        ],
        compiler_params=params(),
        name="payload",
    )(lists, state, matrices, water, flux_projection)


GROUP = 4


def weight_copies(layer, kernels_ref, held, sems):
    return [
        pltpu.make_async_copy(kernels_ref.at[layer, d], held.at[d], sems.at[d]) for d in range(3)
    ]


def set_columns(line, before, after):
    cols = line.shape[0]
    at = iota(line.shape, 0)
    left = jnp.where(at == 0, before, pltpu.roll(line, 1, 0))
    right = jnp.where(at == cols - 1, after, pltpu.roll(line, cols - 1, 0))
    return left, right


def air_line(h, before, after):
    left, right = set_columns(h, before, after)
    return jnp.concatenate([left, h, right], axis=1).astype(BF16)


def sea_line(h, before, after):
    half = h.shape[1] // 2
    left, _ = set_columns(h[:, half:], before[:, half:], after[:, half:])
    _, right = set_columns(h[:, :half], before[:, :half], after[:, :half])
    return jnp.concatenate([left, h, right], axis=1).astype(BF16)


def air_product(block, kernel):
    return dot(block, kernel.reshape(-1, kernel.shape[-1]))


def sea_product(block, kernel):
    width = kernel.shape[-1]
    flat = kernel.reshape(-1, width)
    return jnp.concatenate(
        [dot(block[:, : 3 * width], flat), dot(block[:, width : 4 * width], flat)], axis=1
    )


def conv_kernel(layer, halo, *refs):
    if halo:
        (x_ref, top_ref, bottom_ref, left_ref, right_ref, air_ref, sea_ref, sum_ref) = refs[:8]
        (lined, air_held, sea_held, sems) = refs[8:]
    else:
        (x_ref, water_ref, air_ref, sea_ref, out_ref, lines_ref, sides_ref) = refs[:7]
        (lined, air_held, sea_held, turned, sems) = refs[7:]
    rows, cols, width = x_ref.shape
    half = width // 2
    ocean = on_ocean()

    def run(kernels_ref, held, make_line, product, masked):
        copies = weight_copies(layer, kernels_ref, held, sems)
        for copy in copies:
            copy.start()
        wide = 3 * width if not masked else 2 * width
        none = jnp.zeros((1, width), F32)

        def put(r, line, before, after):
            lined[r, :, 0:wide] = make_line(silu(line.astype(F32)), before, after)

        if halo:
            before_all = silu(left_ref[...].astype(F32))
            after_all = silu(right_ref[...].astype(F32))
            for r in range(rows + 2):
                line = top_ref[...] if r == 0 else bottom_ref[...] if r == rows + 1 else x_ref[r - 1]
                put(r, line, before_all[r : r + 1], after_all[r : r + 1])
        else:
            for r in (0, rows + 1):
                lined[r, :, 0:wide] = jnp.zeros((cols, wide), BF16)
            for r in range(rows):
                put(r + 1, x_ref[r], none, none)
        for copy in copies:
            copy.wait()
        if masked and not halo:
            fill_water(water_ref, turned)

        def products(r0):
            total = x_ref[pl.ds(r0, GROUP)].astype(F32).reshape(GROUP * cols, width)
            for d in range(3):
                block = lined[pl.ds(r0 + d, GROUP), :, 0:wide].reshape(GROUP * cols, wide)
                total = total + product(block, held[d])
            return total.reshape(GROUP, cols, width)

        if halo:

            @pl.loop(0, rows // GROUP)
            def _(g):
                sum_ref[pl.ds(g * GROUP, GROUP)] = products(g * GROUP)
        else:
            for r0 in range(0, rows, GROUP):
                total = products(r0)
                for k in range(GROUP):
                    r = r0 + k
                    if r == 0 or r == rows - 1:
                        lines_ref[0 if r == 0 else 1] = total[k]
                    sides_ref[0, r] = total[k, :BLOCK_COLS]
                    sides_ref[1, r] = total[k, cols - BLOCK_COLS :]
                    line = total[k]
                    if masked:
                        line = line * water_of_row(turned, rows, r, half, 0, cols)
                    out_ref[r] = line.astype(BF16)

    @pl.when(jnp.logical_not(ocean))
    def _():
        run(air_ref, air_held, air_line, air_product, False)

    @pl.when(ocean)
    def _():
        run(sea_ref, sea_held, sea_line, sea_product, True)


def conv_scratch(state, air_kernels, sea_kernels):
    rows, cols, width = state.shape
    return [
        pltpu.VMEM((rows + 2, cols, 3 * width), BF16),
        pltpu.VMEM(air_kernels.shape[1:], BF16),
        pltpu.VMEM(sea_kernels.shape[1:], BF16),
    ]


def conv_cost(state, air_kernels):
    cells = state.shape[0] * state.shape[1]
    width = state.shape[2]
    return pl.CostEstimate(
        flops=2 * 9 * cells * width * width,
        bytes_accessed=air_kernels[0].size * 2 + state.size * 6,
        transcendentals=state.size,
    )


def conv_with_halo(layer, state, halo, air_kernels, sea_kernels):
    return pl.pallas_call(
        functools.partial(conv_kernel, layer, True),
        out_shape=jax.ShapeDtypeStruct(state.shape, F32),
        in_specs=[VMEM] * 5 + [ANY] * 2,
        out_specs=VMEM,
        scratch_shapes=conv_scratch(state, air_kernels, sea_kernels) + [pltpu.SemaphoreType.DMA((3,))],
        compiler_params=params(),
        cost_estimate=conv_cost(state, air_kernels),
        name="conv_halo",
    )(state, *halo, air_kernels, sea_kernels)


def conv_inside(layer, state, water, air_kernels, sea_kernels):
    rows, cols, width = state.shape
    return pl.pallas_call(
        functools.partial(conv_kernel, layer, False),
        out_shape=(
            jax.ShapeDtypeStruct(state.shape, BF16),
            jax.ShapeDtypeStruct((2, cols, width), F32),
            jax.ShapeDtypeStruct((2, rows, BLOCK_COLS, width), F32),
        ),
        in_specs=[VMEM] * 2 + [ANY] * 2,
        out_specs=(VMEM,) * 3,
        scratch_shapes=conv_scratch(state, air_kernels, sea_kernels)
        + [pltpu.VMEM((cols, 128), F32), pltpu.SemaphoreType.DMA((3,))],
        compiler_params=params(),
        cost_estimate=conv_cost(state, air_kernels),
        name="conv_inside",
    )(state, water, air_kernels, sea_kernels)


def edge_kernel(
    layer,
    out_in_ref,
    lines_ref,
    sides_ref,
    top_ref,
    bottom_ref,
    left_ref,
    right_ref,
    water_ref,
    air_ref,
    sea_ref,
    out_ref,
    air_held,
    sea_held,
    turned,
    line_out,
    side_out,
    sems,
    out_sems,
):
    del out_in_ref
    _, rows, _, width = sides_ref.shape
    cols = lines_ref.shape[1]
    half = width // 2
    ocean = on_ocean()

    def run(kernels_ref, held, make_line, product, masked):
        copies = weight_copies(layer, kernels_ref, held, sems)
        for copy in copies:
            copy.start()
        none = jnp.zeros((1, width), F32)
        top = make_line(silu(top_ref[...].astype(F32)), none, none)
        bottom = make_line(silu(bottom_ref[...].astype(F32)), none, none)
        before = silu(left_ref[...].astype(F32))
        after = silu(right_ref[...].astype(F32))
        if masked:
            before, after = before[:, half:], after[:, :half]
            fill_water(water_ref, turned)
        size = before.shape[1]
        for copy in copies:
            copy.wait()
        west = jnp.zeros((rows, size), F32)
        east = jnp.zeros((rows, size), F32)
        for d in range(3):
            west = west + dot(before[d : d + rows].astype(BF16), held[d, 0])
            east = east + dot(after[d : d + rows].astype(BF16), held[d, 2])
        if masked:
            blank = jnp.zeros((rows, half), F32)
            west = jnp.concatenate([west, blank], axis=1)
            east = jnp.concatenate([blank, east], axis=1)

        def finish(value, r, start, size):
            if masked:
                value = value * water_of_row(turned, rows, r, half, start, size)
            return value.astype(BF16)

        at = iota((cols, width), 0)
        for k, (line, d) in enumerate(((top, 0), (bottom, 2))):
            r = 0 if k == 0 else rows - 1
            total = lines_ref[k] + product(line, held[d])
            total = total + jnp.where(at == 0, west[r : r + 1], 0.0)
            total = total + jnp.where(at == cols - 1, east[r : r + 1], 0.0)
            line_out[k] = finish(total, r, 0, cols)
        at = iota((BLOCK_COLS, width), 0)
        for r in range(1, rows - 1):
            total = sides_ref[0, r] + jnp.where(at == 0, west[r : r + 1], 0.0)
            side_out[0, r - 1] = finish(total, r, 0, BLOCK_COLS)
            total = sides_ref[1, r] + jnp.where(at == BLOCK_COLS - 1, east[r : r + 1], 0.0)
            side_out[1, r - 1] = finish(total, r, cols - BLOCK_COLS, BLOCK_COLS)

    @pl.when(jnp.logical_not(ocean))
    def _():
        run(air_ref, air_held, air_line, air_product, False)

    @pl.when(ocean)
    def _():
        run(sea_ref, sea_held, sea_line, sea_product, True)

    inner = pl.ds(1, rows - 2)
    copies = [
        pltpu.make_async_copy(line_out.at[0], out_ref.at[0], out_sems.at[0]),
        pltpu.make_async_copy(line_out.at[1], out_ref.at[rows - 1], out_sems.at[1]),
        pltpu.make_async_copy(side_out.at[0], out_ref.at[inner, pl.ds(0, BLOCK_COLS)], out_sems.at[2]),
        pltpu.make_async_copy(
            side_out.at[1], out_ref.at[inner, pl.ds(cols - BLOCK_COLS, BLOCK_COLS)], out_sems.at[3]
        ),
    ]
    for copy in copies:
        copy.start()
    for copy in copies:
        copy.wait()


def fix_edges(layer, out, lines, sides, halo, water, air_kernels, sea_kernels):
    rows, cols, width = out.shape
    return pl.pallas_call(
        functools.partial(edge_kernel, layer),
        out_shape=jax.ShapeDtypeStruct(out.shape, BF16),
        in_specs=[ANY] + [VMEM] * 7 + [ANY] * 2,
        out_specs=ANY,
        scratch_shapes=[
            pltpu.VMEM(air_kernels.shape[1:], BF16),
            pltpu.VMEM(sea_kernels.shape[1:], BF16),
            pltpu.VMEM((cols, 128), F32),
            pltpu.VMEM((2, cols, width), BF16),
            pltpu.VMEM((2, rows - 2, BLOCK_COLS, width), BF16),
            pltpu.SemaphoreType.DMA((3,)),
            pltpu.SemaphoreType.DMA((4,)),
        ],
        input_output_aliases={0: 0},
        compiler_params=params(),
        name="fix_edges",
    )(out, lines, sides, *halo, water, air_kernels, sea_kernels)


def update_kernel(
    labels_ref,
    first_ref,
    second_ref,
    sum_hbm,
    water_ref,
    coupling_ref,
    new_ref,
    top_ref,
    bottom_ref,
    left_ref,
    right_ref,
    total,
    sum_ref,
    turned,
    sems,
):
    rows, cols, width = new_ref.shape
    half = width // 2
    tiles = first_ref.shape[0] // SLOTS
    ocean = on_ocean()
    me = lax.axis_index("lat") * lax.axis_size("lon") + lax.axis_index("lon")
    quarter = rows // 4
    copies = [
        pltpu.make_async_copy(
            sum_hbm.at[pl.ds(k * quarter, quarter)], sum_ref.at[pl.ds(k * quarter, quarter)], sems.at[k]
        )
        for k in range(4)
    ]
    for copy in copies:
        copy.start()

    def gather(add):
        def slot(s, _):
            label = labels_ref[(jnp.bitwise_xor(s // SLOTS, me)) * SLOTS + s % SLOTS]

            @pl.when(label >= 0)
            def _():
                add(s, label)

            return 0

        lax.fori_loop(0, tiles * SLOTS, slot, 0)

    def store(r, line):
        low = line.astype(BF16)
        new_ref[r] = low
        exact = low.astype(F32)
        left_ref[r : r + 1] = exact[0:1]
        right_ref[r : r + 1] = exact[cols - 1 : cols]
        if r == 0:
            top_ref[...] = low
        if r == rows - 1:
            bottom_ref[...] = low

    @pl.when(jnp.logical_not(ocean))
    def _():
        total[:, :, 0:half] = jnp.zeros((rows, cols, half), F32)
        across = cols // BLOCK_COLS

        def add(s, label):
            r0 = (label // across) * BLOCK_ROWS
            c0 = pl.multiple_of((label % across) * BLOCK_COLS, BLOCK_COLS)
            for h, ref in enumerate((first_ref, second_ref)):
                value = ref[s].astype(F32).reshape(HALF_ROWS, BLOCK_COLS, half)
                total[pl.ds(r0 + h * HALF_ROWS, HALF_ROWS), pl.ds(c0, BLOCK_COLS), 0:half] += value

        gather(add)
        for k in range(4):
            r0 = k * quarter
            block = total[r0 : r0 + quarter, :, 0:half].astype(BF16).reshape(quarter * cols, half)
            force = dot(block, coupling_ref[...]).reshape(quarter, cols, width)
            copies[k].wait()
            for q in range(quarter):
                store(r0 + q, sum_ref[r0 + q] + force[q])

    @pl.when(ocean)
    def _():
        total[...] = jnp.zeros_like(total)
        fill_water(water_ref, turned)
        wide = BLOCK_COLS // 2
        across = cols // wide

        def add(s, label):
            r0 = (label // across) * BLOCK_ROWS
            c0 = pl.multiple_of((label % across) * wide, wide)
            for h, ref in enumerate((first_ref, second_ref)):
                value = ref[s].astype(F32).reshape(2, HALF_ROWS, wide, half)
                for p in range(2):
                    total[
                        pl.ds(r0 + h * HALF_ROWS, HALF_ROWS), pl.ds(c0, wide), p * half : (p + 1) * half
                    ] += value[p]

        gather(add)
        for k in range(4):
            copies[k].wait()
            for q in range(quarter):
                r = k * quarter + q
                store(r, (sum_ref[r] + total[r]) * water_of_row(turned, rows, r, half, 0, cols))


def update(labels, first, second, summed, water, coupling_matrix):
    rows, cols, width = summed.shape
    return pl.pallas_call(
        update_kernel,
        out_shape=(
            jax.ShapeDtypeStruct((rows, cols, width), BF16),
            jax.ShapeDtypeStruct((cols, width), BF16),
            jax.ShapeDtypeStruct((cols, width), BF16),
            jax.ShapeDtypeStruct((rows, width), F32),
            jax.ShapeDtypeStruct((rows, width), F32),
        ),
        in_specs=[SMEM, VMEM, VMEM, ANY, VMEM, VMEM],
        out_specs=(VMEM,) * 5,
        scratch_shapes=[
            pltpu.VMEM((rows, cols, width), F32),
            pltpu.VMEM((rows, cols, width), F32),
            pltpu.VMEM((cols, 128), F32),
            pltpu.SemaphoreType.DMA((4,)),
        ],
        compiler_params=params(),
        name="update",
    )(labels, first, second, summed, water, coupling_matrix)


def exchange(value, axis, bit):
    return lax.ppermute(value, axis, [(i, i ^ bit) for i in range(lax.axis_size(axis))])


def across_groups(value):
    return exchange(value, "grp", 1)


def to_owners(value):
    return lax.all_to_all(value, ("lat", "lon"), split_axis=0, concat_axis=0, tiled=True)


def all_lists(lists):
    held = across_groups(lists)[None]
    for axis in ("lon", "lat"):
        bit = 1
        while bit < lax.axis_size(axis):
            held = jnp.concatenate([held, exchange(held, axis, bit)], axis=0)
            bit *= 2
    return held


def slot_labels(held):
    me = lax.axis_index("lat") * lax.axis_size("lon") + lax.axis_index("lon")
    mine = (held[:, 0] == me).astype(jnp.int32)
    rank = jnp.cumsum(mine, axis=1) - mine
    labels = [
        jnp.sum(mine * (rank == slot) * (held[:, 2] + 1), axis=1) - 1 for slot in range(SLOTS)
    ]
    return jnp.stack(labels, axis=1).reshape(-1)


def halo_of(top, bottom, left, right):
    lats, lons = lax.axis_size("lat"), lax.axis_size("lon")
    down = [(i, i + 1) for i in range(lats - 1)]
    up = [(i + 1, i) for i in range(lats - 1)]
    east = [(i, (i + 1) % lons) for i in range(lons)]
    west = [((i + 1) % lons, i) for i in range(lons)]
    above = lax.ppermute(bottom, "lat", down)
    below = lax.ppermute(top, "lat", up)
    first = jnp.concatenate([above[:1], left.astype(BF16), below[:1]], axis=0)
    last = jnp.concatenate([above[-1:], right.astype(BF16), below[-1:]], axis=0)
    before = lax.ppermute(last, "lon", east)
    after = lax.ppermute(first, "lon", west)
    return above, below, before, after


def body(
    state,
    intersection_lists,
    intersection_matrices,
    water_indicator,
    atmosphere_kernels,
    ocean_kernels,
    flux_projection,
    coupling_matrix,
):
    current = state[0]
    rows, cols, width = current.shape
    tiles = lax.axis_size("lat") * lax.axis_size("lon")
    entries = intersection_lists.shape[-1]
    lists = intersection_lists.reshape(3, entries)
    matrices = intersection_matrices.reshape(entries, BLOCK, BLOCK)
    water = water_indicator.reshape(rows, cols, 2).transpose(2, 0, 1).reshape(2 * rows, cols)

    first, second = payloads(lists, current, matrices, water, flux_projection, tiles)
    first = across_groups(first)
    second = to_owners(second)
    first = to_owners(first)
    second = across_groups(second)
    labels = slot_labels(all_lists(lists))

    halo = halo_of(current[0], current[-1], current[:, 0], current[:, -1])
    summed = conv_with_halo(0, current, halo, atmosphere_kernels, ocean_kernels)
    current, *rim = update(labels, first, second, summed, water, coupling_matrix)
    for layer in range(1, LAYERS):
        halo = halo_of(*rim)
        out, lines, sides = conv_inside(layer, current, water, atmosphere_kernels, ocean_kernels)
        current = fix_edges(layer, out, lines, sides, halo, water, atmosphere_kernels, ocean_kernels)
    return current[None]


def solution(mesh):
    placed = (
        P("grp", "lat", "lon", None),
        P("grp", "lat", "lon", None, None),
        P("grp", "lat", "lon", None, None, None),
        P("lat", "lon"),
        P(),
        P(),
        P(),
        P(),
    )
    return jax.shard_map(
        body, mesh=mesh, in_specs=placed, out_specs=P("grp", "lat", "lon", None), check_vma=False
    )
```

profile of v0, /device:TPU:0, one launch (start us, length us, event | category | flops | bytes accessed | tf_op | source)
XLA Modules:
  0.0 134.1 jit_solution(11865265651422246974)
XLA Ops:
  0.0 0.7 copy.36
  0.7 0.8 copy.27
  1.6 1.6 %copy-done = bf16[1,16,128,512]{3,2,1,0:T(8,128)(2,1)S(1)} copy-done((bf16[1,16,128,512]{3,2,1,0:T(8,128)(2,1)S(1)}, bf16[1,16,128,512]{3,2,1,0:T(8,128)(2,1)}, u32[]{:S(2)}) %copy-start) | copy-done | bytes 2097176
  3.2 1.0 copy-done.4
  4.2 0.9 copy-done.5
  5.2 5.1 %payload.1 = (bf16[32,64,256]{2,1,0:T(8,128)(2,1)}, bf16[32,64,256]{2,1,0:T(8,128)(2,1)}) custom-call(s32[3,16]{1,0:T(4,128)S(1)} %bitcast.59, bf16[16,128,512]{2,1,0:T(8,128)(2,1)S(1)} %bitcast.52, bf16[16,128,128]{2,1,0:T(8,128)(2,1)S(1)} %bitcast.54, s32[32,128]{1,0:T(8,128)S(1)} %bitcast.55, bf16[512,256]{1,0:T(8,128)(2,1)S(1)} %copy-done.5), custom_call_target="tpu_custom_call" | custom-call | tf_op jit(solution)/shard_map/payload/pallas_call | solution.py:135
  10.3 7.4 %all-to-all-start.1 = ((bf16[32,64,256]{2,1,0:T(8,128)(2,1)}), bf16[32,64,256]{2,1,0:T(8,128)(2,1)}, u32[]{:S(2)}, u32[]{:S(2)}) async-start(bf16[32,64,256]{2,1,0:T(8,128)(2,1)} %get-tuple-element.16), calls=%async_computation.1 | async-start | bytes 2097152 | tf_op jit(solution)/shard_map/all_to_all | solution.py:565
  17.7 1.7 %collective-permute-start.5 = (bf16[32,64,256]{2,1,0:T(8,128)(2,1)}, bf16[32,64,256]{2,1,0:T(8,128)(2,1)}, u32[]{:S(2)}, u32[]{:S(2)}) collective-permute-start(bf16[32,64,256]{2,1,0:T(8,128)(2,1)} %get-tuple-element.15), channel_id=1, source_target_pairs={{0,16},{16,0},{1,17},{17,1},{2,18},{18,2},{3,19},{19,3},{4,20},{20... | collective-permute-start | bytes 3145736 | tf_op jit(solution)/shard_map/ppermute | solution.py:557
  19.3 0.4 collective-permute-start
  19.8 23.7 %collective-permute-done = s32[3,16]{1,0:T(4,128)S(1)} collective-permute-done((s32[3,16]{1,0:T(4,128)S(1)}, s32[3,16]{1,0:T(4,128)S(1)}, u32[]{:S(2)}, u32[]{:S(2)}) %collective-permute-start) | collective-permute-done | bytes 224 | tf_op jit(solution)/shard_map/ppermute | solution.py:557
  43.4 1.1 collective-permute-done.1
  44.6 1.7 %collective-permute-start.2 = (s32[2,3,16]{2,0,1:T(2,128)S(1)}, s32[2,3,16]{2,0,1:T(2,128)S(1)}, u32[]{:S(2)}, u32[]{:S(2)}) collective-permute-start(s32[2,3,16]{2,0,1:T(2,128)S(1)} %pad_add_fusion.2), channel_id=1, source_target_pairs={{0,2},{1,3},{2,0},{3,1},{4,6},{5,7},{6,4},{7,5},{8,10},{9,11},{10,... | collective-permute-start | bytes 1160 | tf_op jit(solution)/shard_map/ppermute | solution.py:557
  46.3 1.9 %collective-permute-done.2 = s32[2,3,16]{2,0,1:T(2,128)S(1)} collective-permute-done((s32[2,3,16]{2,0,1:T(2,128)S(1)}, s32[2,3,16]{2,0,1:T(2,128)S(1)}, u32[]{:S(2)}, u32[]{:S(2)}) %collective-permute-start.2) | collective-permute-done | bytes 416 | tf_op jit(solution)/shard_map/ppermute | solution.py:557
  48.3 1.7 %collective-permute-start.3 = (s32[4,3,16]{2,0,1:T(4,128)S(1)}, s32[4,3,16]{2,0,1:T(4,128)S(1)}, u32[]{:S(2)}, u32[]{:S(2)}) collective-permute-start(s32[4,3,16]{2,0,1:T(4,128)S(1)} %pad_add_fusion.1), channel_id=1, source_target_pairs={{0,4},{4,0},{8,12},{12,8},{1,5},{5,1},{9,13},{13,9},{2,6},{6,2},{1... | collective-permute-start | bytes 2312 | tf_op jit(solution)/shard_map/ppermute | solution.py:557
  50.0 0.7 slice_bitcast_fusion
  50.7 1.3 collective-permute-start.8
  52.0 4.6 %collective-permute-start.7 = (bf16[128,512]{1,0:T(8,128)(2,1)S(1)}, bf16[128,512]{1,0:T(8,128)(2,1)S(1)}, u32[]{:S(2)}, u32[]{:S(2)}) collective-permute-start(bf16[128,512]{1,0:T(8,128)(2,1)S(1)} %get-tuple-element.32), channel_id=1, source_target_pairs={{0,4},{4,8},{8,12},{1,5},{5,9},{9,13},{2,6},{6,10},{10,14},{3,7},{... | collective-permute-start | bytes 393224 | tf_op jit(solution)/shard_map/ppermute | solution.py:594
  56.5 1.2 copy.35
  57.7 2.4 %collective-permute-start.4 = (s32[8,3,16]{2,0,1:T(8,128)S(1)}, s32[8,3,16]{2,0,1:T(8,128)S(1)}, u32[]{:S(2)}, u32[]{:S(2)}) collective-permute-start(s32[8,3,16]{2,0,1:T(8,128)S(1)} %pad_add_fusion), channel_id=1, source_target_pairs={{0,8},{4,12},{8,0},{12,4},{1,9},{5,13},{9,1},{13,5},{2,10},{6,14},... | collective-permute-start | bytes 4616 | tf_op jit(solution)/shard_map/ppermute | solution.py:557
  60.2 0.6 slice_bitcast_fusion.2
  60.8 1.6 %collective-permute-done.4 = s32[8,3,16]{2,0,1:T(8,128)S(1)} collective-permute-done((s32[8,3,16]{2,0,1:T(8,128)S(1)}, s32[8,3,16]{2,0,1:T(8,128)S(1)}, u32[]{:S(2)}, u32[]{:S(2)}) %collective-permute-start.4) | collective-permute-done | bytes 1568 | tf_op jit(solution)/shard_map/ppermute | solution.py:557
  62.4 0.6 convert_bitcast_fusion
  63.1 0.8 reduce_window_sum.11
  63.8 4.7 %all-to-all-start = ((bf16[32,64,256]{2,1,0:T(8,128)(2,1)}), bf16[32,64,256]{2,1,0:T(8,128)(2,1)S(1)}, u32[]{:S(2)}, u32[]{:S(2)}) async-start(bf16[32,64,256]{2,1,0:T(8,128)(2,1)} %collective-permute-done.5), calls=%async_computation | async-start | bytes 2097152 | tf_op jit(solution)/shard_map/all_to_all | solution.py:565
  68.5 0.8 fusion.5
  69.4 0.6 copy-done.9
  70.1 0.7 pad_maximum_fusion
  70.8 0.5 collective-permute-start.9
  71.2 1.6 %collective-permute-start.6 = (bf16[32,64,256]{2,1,0:T(8,128)(2,1)}, bf16[32,64,256]{2,1,0:T(8,128)(2,1)}, u32[]{:S(2)}, u32[]{:S(2)}) collective-permute-start(bf16[32,64,256]{2,1,0:T(8,128)(2,1)} %all-to-all-done.1), channel_id=1, source_target_pairs={{0,16},{16,0},{1,17},{17,1},{2,18},{18,2},{3,19},{19,3},{4,20},{20... | collective-permute-start | bytes 3145736 | tf_op jit(solution)/shard_map/ppermute | solution.py:557
  72.8 0.7 pad_maximum_fusion.1
  73.6 1.1 collective-permute-start.10
  74.7 0.1 copy.25
  74.8 0.1 reshape.44.labels_ref
  74.9 2.0 %collective-permute-done.9.refs_3_ = bf16[18,512]{1,0:T(8,128)(2,1)S(1)} collective-permute-done((bf16[18,512]{1,0:T(8,128)(2,1)S(1)}, bf16[18,512]{1,0:T(8,128)(2,1)S(1)}, u32[]{:S(2)}, u32[]{:S(2)}) %collective-permute-start.9) | collective-permute-done | bytes 18464 | tf_op jit(solution)/shard_map/ppermute | solution.py:598
  76.9 1.7 %copy-done.2 = bf16[2,3,3,256,256]{4,3,2,1,0:T(8,128)(2,1)S(1)} copy-done((bf16[2,3,3,256,256]{4,3,2,1,0:T(8,128)(2,1)S(1)}, bf16[2,3,3,256,256]{4,3,2,1,0:T(8,128)(2,1)}, u32[]{:S(2)}) %copy-start.2) | copy-done | bytes 2359320
  78.5 0.9 copy-done.8
  79.4 0.9 copy-done.10
  80.3 14.8 %conv_halo.1.sum_hbm = f32[16,128,512]{2,1,0:T(8,128)} custom-call(bf16[16,128,512]{2,1,0:T(8,128)(2,1)S(1)} %bitcast.53, bf16[128,512]{1,0:T(8,128)(2,1)S(1)} %copy-done.10, bf16[128,512]{1,0:T(8,128)(2,1)S(1)} %copy-done.8, bf16[18,512]{1,0:T(8,128)(2,1)S(1)} %collective-permute-done.9.refs_3_, bf16[18,512]{1,0:T(8,128)(2,1)S(1)} %collective-permute-done.10.refs_4_, ...), custom_call_target="tpu_custom_call" | custom-call | flops 9663676416 | bytes 11010048 | tf_op jit(solution)/shard_map/conv_halo/pallas_call | solution.py:284
  95.1 1.9 %collective-permute-done.6.second_ref = bf16[32,64,256]{2,1,0:T(8,128)(2,1)} collective-permute-done((bf16[32,64,256]{2,1,0:T(8,128)(2,1)}, bf16[32,64,256]{2,1,0:T(8,128)(2,1)}, u32[]{:S(2)}, u32[]{:S(2)}) %collective-permute-start.6) | collective-permute-done | bytes 1048608 | tf_op jit(solution)/shard_map/ppermute | solution.py:557
  97.0 4.1 %update.1 = (bf16[16,128,512]{2,1,0:T(8,128)(2,1)S(1)}, bf16[128,512]{1,0:T(8,128)(2,1)S(1)}, bf16[128,512]{1,0:T(8,128)(2,1)S(1)}, f32[16,512]{1,0:T(8,128)S(1)}, f32[16,512]{1,0:T(8,128)S(1)}) custom-call(s32[32]{0:T(128)S(1)} %reshape.44.labels_ref, bf16[32,64,256]{2,1,0:T(8,128)(2,1)S(1)} %all-to-all-done.first_ref, ...), custom_call_target="tpu_custom_call" | custom-call | tf_op jit(solution)/shard_map/update/pallas_call | solution.py:534
  101.1 3.9 %collective-permute-start.11 = (bf16[128,512]{1,0:T(8,128)(2,1)S(1)}, bf16[128,512]{1,0:T(8,128)(2,1)S(1)}, u32[]{:S(2)}, u32[]{:S(2)}) collective-permute-start(bf16[128,512]{1,0:T(8,128)(2,1)S(1)} %get-tuple-element.21), channel_id=1, source_target_pairs={{0,4},{4,8},{8,12},{1,5},{5,9},{9,13},{2,6},{6,10},{10,14},{3,7},{... | collective-permute-start | bytes 393224 | tf_op jit(solution)/shard_map/ppermute | solution.py:594
  105.0 1.3 collective-permute-start.12
  106.3 1.7 %collective-permute-done.11.top_ref = bf16[128,512]{1,0:T(8,128)(2,1)S(1)} collective-permute-done((bf16[128,512]{1,0:T(8,128)(2,1)S(1)}, bf16[128,512]{1,0:T(8,128)(2,1)S(1)}, u32[]{:S(2)}, u32[]{:S(2)}) %collective-permute-start.11) | collective-permute-done | bytes 131104 | tf_op jit(solution)/shard_map/ppermute | solution.py:594
  108.0 4.1 %collective-permute-done.12.bottom_ref = bf16[128,512]{1,0:T(8,128)(2,1)S(1)} collective-permute-done((bf16[128,512]{1,0:T(8,128)(2,1)S(1)}, bf16[128,512]{1,0:T(8,128)(2,1)S(1)}, u32[]{:S(2)}, u32[]{:S(2)}) %collective-permute-start.12) | collective-permute-done | bytes 131104 | tf_op jit(solution)/shard_map/ppermute | solution.py:595
  112.3 1.8 %collective-permute-start.14 = (bf16[18,512]{1,0:T(8,128)(2,1)S(1)}, bf16[18,512]{1,0:T(8,128)(2,1)S(1)}, u32[]{:S(2)}, u32[]{:S(2)}) collective-permute-start(bf16[18,512]{1,0:T(8,128)(2,1)S(1)} %pad_maximum_fusion.3), channel_id=1, source_target_pairs={{1,0},{2,1},{3,2},{0,3},{5,4},{6,5},{7,6},{4,7},{9,8},{10,9},{11,1... | collective-permute-start | bytes 55304 | tf_op jit(solution)/shard_map/ppermute | solution.py:599
  114.1 1.7 %copy-done.3 = bf16[2,3,3,256,256]{4,3,2,1,0:T(8,128)(2,1)S(1)} copy-done((bf16[2,3,3,256,256]{4,3,2,1,0:T(8,128)(2,1)S(1)}, bf16[2,3,3,256,256]{4,3,2,1,0:T(8,128)(2,1)}, u32[]{:S(2)}) %copy-start.3) | copy-done | bytes 2359320
  115.7 13.8 %conv_inside.1 = (bf16[16,128,512]{2,1,0:T(8,128)(2,1)}, f32[2,128,512]{2,1,0:T(8,128)S(1)}, f32[2,16,16,512]{3,2,1,0:T(8,128)S(1)}) custom-call(bf16[16,128,512]{2,1,0:T(8,128)(2,1)S(1)} %get-tuple-element.17.refs_0_, s32[32,128]{1,0:T(8,128)S(1)} %bitcast.57, bf16[2,3,3,512,512]{4,3,2,1,0:T(8,128)(2,1)} %air_ref.1, bf16[2,3,3,256,256]{4,3,2,1,0:T(8,128)(2,1)S(1)} %copy-done.3), custom_call_target="tpu_custom_call" | custom-call | flops 9663676416 | bytes 11010048 | tf_op jit(solution)/shard_map/conv_inside/pallas_call | solution.py:298
  129.6 4.3 %fix_edges.1 = bf16[16,128,512]{2,1,0:T(8,128)(2,1)} custom-call(bf16[16,128,512]{2,1,0:T(8,128)(2,1)} %get-tuple-element.18.out_in_ref, f32[2,128,512]{2,1,0:T(8,128)S(1)} %get-tuple-element.19.lines_ref, f32[2,16,16,512]{3,2,1,0:T(8,128)S(1)} %get-tuple-element.20.sides_ref, ...), custom_call_target="tpu_custom_call", output_to_operand_aliasing={{}: (0, {})} | custom-call | tf_op jit(solution)/shard_map/fix_edges/pallas_call | solution.py:411
  (43 shorter events, 0.3 us)
Async XLA Ops:
  1.6 1.6 %copy-start = (bf16[1,16,128,512]{3,2,1,0:T(8,128)(2,1)S(1)}, bf16[1,16,128,512]{3,2,1,0:T(8,128)(2,1)}, u32[]{:S(2)}) copy-start(bf16[1,16,128,512]{3,2,1,0:T(8,128)(2,1)} %param.8) | copy-start | bytes 6291460
  3.2 1.0 copy-start.4
  4.2 0.9 copy-start.5
  5.2 44.8 %copy-start.1 = (bf16[1,16,128,512]{3,2,1,0:T(8,128)(2,1)S(1)}, bf16[1,16,128,512]{3,2,1,0:T(8,128)(2,1)}, u32[]{:S(2)}) copy-start(bf16[1,16,128,512]{3,2,1,0:T(8,128)(2,1)} %param.8) | copy-start | bytes 6291460
  10.3 53.6 %all-to-all-start.1 = ((bf16[32,64,256]{2,1,0:T(8,128)(2,1)}), bf16[32,64,256]{2,1,0:T(8,128)(2,1)}, u32[]{:S(2)}, u32[]{:S(2)}) async-start(bf16[32,64,256]{2,1,0:T(8,128)(2,1)} %get-tuple-element.16), calls=%async_computation.1 | async-start | bytes 2097152 | tf_op jit(solution)/shard_map/all_to_all | solution.py:565
  17.7 46.1 %collective-permute-start.5 = (bf16[32,64,256]{2,1,0:T(8,128)(2,1)}, bf16[32,64,256]{2,1,0:T(8,128)(2,1)}, u32[]{:S(2)}, u32[]{:S(2)}) collective-permute-start(bf16[32,64,256]{2,1,0:T(8,128)(2,1)} %get-tuple-element.15), channel_id=1, source_target_pairs={{0,16},{16,0},{1,17},{17,1},{2,18},{18,2},{3,19},{19,3},{4,20},{20... | collective-permute-start | bytes 3145736 | tf_op jit(solution)/shard_map/ppermute | solution.py:557
  19.3 24.1 %collective-permute-start = (s32[3,16]{1,0:T(4,128)S(1)}, s32[3,16]{1,0:T(4,128)S(1)}, u32[]{:S(2)}, u32[]{:S(2)}) collective-permute-start(s32[3,16]{1,0:T(4,128)S(1)} %bitcast.60), channel_id=1, source_target_pairs={{0,16},{16,0},{1,17},{17,1},{2,18},{18,2},{3,19},{19,3},{4,20},{20... | collective-permute-start | bytes 584 | tf_op jit(solution)/shard_map/ppermute | solution.py:557
  43.4 1.2 collective-permute-start.1
  44.6 3.7 %collective-permute-start.2 = (s32[2,3,16]{2,0,1:T(2,128)S(1)}, s32[2,3,16]{2,0,1:T(2,128)S(1)}, u32[]{:S(2)}, u32[]{:S(2)}) collective-permute-start(s32[2,3,16]{2,0,1:T(2,128)S(1)} %pad_add_fusion.2), channel_id=1, source_target_pairs={{0,2},{1,3},{2,0},{3,1},{4,6},{5,7},{6,4},{7,5},{8,10},{9,11},{10,... | collective-permute-start | bytes 1160 | tf_op jit(solution)/shard_map/ppermute | solution.py:557
  48.3 9.4 %collective-permute-start.3 = (s32[4,3,16]{2,0,1:T(4,128)S(1)}, s32[4,3,16]{2,0,1:T(4,128)S(1)}, u32[]{:S(2)}, u32[]{:S(2)}) collective-permute-start(s32[4,3,16]{2,0,1:T(4,128)S(1)} %pad_add_fusion.1), channel_id=1, source_target_pairs={{0,4},{4,0},{8,12},{12,8},{1,5},{5,1},{9,13},{13,9},{2,6},{6,2},{1... | collective-permute-start | bytes 2312 | tf_op jit(solution)/shard_map/ppermute | solution.py:557
  50.7 18.7 %collective-permute-start.8 = (bf16[128,512]{1,0:T(8,128)(2,1)}, bf16[128,512]{1,0:T(8,128)(2,1)S(1)}, u32[]{:S(2)}, u32[]{:S(2)}) collective-permute-start(bf16[128,512]{1,0:T(8,128)(2,1)} %get-tuple-element.31), channel_id=1, source_target_pairs={{4,0},{8,4},{12,8},{5,1},{9,5},{13,9},{6,2},{10,6},{14,10},{7,3},{... | collective-permute-start | bytes 393224 | tf_op jit(solution)/shard_map/ppermute | solution.py:595
  52.0 17.4 %collective-permute-start.7 = (bf16[128,512]{1,0:T(8,128)(2,1)S(1)}, bf16[128,512]{1,0:T(8,128)(2,1)S(1)}, u32[]{:S(2)}, u32[]{:S(2)}) collective-permute-start(bf16[128,512]{1,0:T(8,128)(2,1)S(1)} %get-tuple-element.32), channel_id=1, source_target_pairs={{0,4},{4,8},{8,12},{1,5},{5,9},{9,13},{2,6},{6,10},{10,14},{3,7},{... | collective-permute-start | bytes 393224 | tf_op jit(solution)/shard_map/ppermute | solution.py:594
  57.7 4.7 %collective-permute-start.4 = (s32[8,3,16]{2,0,1:T(8,128)S(1)}, s32[8,3,16]{2,0,1:T(8,128)S(1)}, u32[]{:S(2)}, u32[]{:S(2)}) collective-permute-start(s32[8,3,16]{2,0,1:T(8,128)S(1)} %pad_add_fusion), channel_id=1, source_target_pairs={{0,8},{4,12},{8,0},{12,4},{1,9},{5,13},{9,1},{13,5},{2,10},{6,14},... | collective-permute-start | bytes 4616 | tf_op jit(solution)/shard_map/ppermute | solution.py:557
  62.4 1.4 %copy-start.11 = (s32[16,3,16]{2,0,1:T(8,128)}, s32[16,3,16]{2,0,1:T(8,128)S(1)}, u32[]{:S(2)}) copy-start(s32[16,3,16]{2,0,1:T(8,128)S(1)} %concatenate.30) | copy-start | bytes 9220
  63.8 33.2 %all-to-all-start = ((bf16[32,64,256]{2,1,0:T(8,128)(2,1)}), bf16[32,64,256]{2,1,0:T(8,128)(2,1)S(1)}, u32[]{:S(2)}, u32[]{:S(2)}) async-start(bf16[32,64,256]{2,1,0:T(8,128)(2,1)} %collective-permute-done.5), calls=%async_computation | async-start | bytes 2097152 | tf_op jit(solution)/shard_map/all_to_all | solution.py:565
  69.3 7.5 %copy-start.7 = (bf16[128,512]{1,0:T(8,128)(2,1)}, bf16[128,512]{1,0:T(8,128)(2,1)S(1)}, u32[]{:S(2)}) copy-start(bf16[128,512]{1,0:T(8,128)(2,1)S(1)} %collective-permute-done.8.refs_2_) | copy-start | bytes 393220
  69.4 0.7 copy-start.9
  70.8 6.1 %collective-permute-start.9 = (bf16[18,512]{1,0:T(8,128)(2,1)S(1)}, bf16[18,512]{1,0:T(8,128)(2,1)S(1)}, u32[]{:S(2)}, u32[]{:S(2)}) collective-permute-start(bf16[18,512]{1,0:T(8,128)(2,1)S(1)} %pad_maximum_fusion), channel_id=1, source_target_pairs={{0,1},{1,2},{2,3},{3,0},{4,5},{5,6},{6,7},{7,4},{8,9},{9,10},{10,1... | collective-permute-start | bytes 55304 | tf_op jit(solution)/shard_map/ppermute | solution.py:598
  71.2 25.7 %collective-permute-start.6 = (bf16[32,64,256]{2,1,0:T(8,128)(2,1)}, bf16[32,64,256]{2,1,0:T(8,128)(2,1)}, u32[]{:S(2)}, u32[]{:S(2)}) collective-permute-start(bf16[32,64,256]{2,1,0:T(8,128)(2,1)} %all-to-all-done.1), channel_id=1, source_target_pairs={{0,16},{16,0},{1,17},{17,1},{2,18},{18,2},{3,19},{19,3},{4,20},{20... | collective-permute-start | bytes 3145736 | tf_op jit(solution)/shard_map/ppermute | solution.py:557
  73.6 3.3 %collective-permute-start.10 = (bf16[18,512]{1,0:T(8,128)(2,1)S(1)}, bf16[18,512]{1,0:T(8,128)(2,1)S(1)}, u32[]{:S(2)}, u32[]{:S(2)}) collective-permute-start(bf16[18,512]{1,0:T(8,128)(2,1)S(1)} %pad_maximum_fusion.1), channel_id=1, source_target_pairs={{1,0},{2,1},{3,2},{0,3},{5,4},{6,5},{7,6},{4,7},{9,8},{10,9},{11,1... | collective-permute-start | bytes 55304 | tf_op jit(solution)/shard_map/ppermute | solution.py:599
  76.9 1.7 %copy-start.2 = (bf16[2,3,3,256,256]{4,3,2,1,0:T(8,128)(2,1)S(1)}, bf16[2,3,3,256,256]{4,3,2,1,0:T(8,128)(2,1)}, u32[]{:S(2)}) copy-start(bf16[2,3,3,256,256]{4,3,2,1,0:T(8,128)(2,1)} %sea_ref.1) | copy-start | bytes 7077892
  78.5 0.9 copy-start.8
  79.4 0.9 copy-start.10
  80.3 16.7 %copy-start.6 = (bf16[256,512]{1,0:T(8,128)(2,1)S(1)}, bf16[256,512]{1,0:T(8,128)(2,1)}, u32[]{:S(2)}) copy-start(bf16[256,512]{1,0:T(8,128)(2,1)} %coupling_ref.1) | copy-start | bytes 786436
  101.1 6.9 %collective-permute-start.11 = (bf16[128,512]{1,0:T(8,128)(2,1)S(1)}, bf16[128,512]{1,0:T(8,128)(2,1)S(1)}, u32[]{:S(2)}, u32[]{:S(2)}) collective-permute-start(bf16[128,512]{1,0:T(8,128)(2,1)S(1)} %get-tuple-element.21), channel_id=1, source_target_pairs={{0,4},{4,8},{8,12},{1,5},{5,9},{9,13},{2,6},{6,10},{10,14},{3,7},{... | collective-permute-start | bytes 393224 | tf_op jit(solution)/shard_map/ppermute | solution.py:594
  105.0 7.2 %collective-permute-start.12 = (bf16[128,512]{1,0:T(8,128)(2,1)S(1)}, bf16[128,512]{1,0:T(8,128)(2,1)S(1)}, u32[]{:S(2)}, u32[]{:S(2)}) collective-permute-start(bf16[128,512]{1,0:T(8,128)(2,1)S(1)} %get-tuple-element.22), channel_id=1, source_target_pairs={{4,0},{8,4},{12,8},{5,1},{9,5},{13,9},{6,2},{10,6},{14,10},{7,3},{... | collective-permute-start | bytes 393224 | tf_op jit(solution)/shard_map/ppermute | solution.py:595
  112.2 17.3 %collective-permute-start.13 = (bf16[18,512]{1,0:T(8,128)(2,1)S(1)}, bf16[18,512]{1,0:T(8,128)(2,1)S(1)}, u32[]{:S(2)}, u32[]{:S(2)}) collective-permute-start(bf16[18,512]{1,0:T(8,128)(2,1)S(1)} %pad_maximum_fusion.2), channel_id=1, source_target_pairs={{0,1},{1,2},{2,3},{3,0},{4,5},{5,6},{6,7},{7,4},{8,9},{9,10},{10,1... | collective-permute-start | bytes 55304 | tf_op jit(solution)/shard_map/ppermute | solution.py:598
  112.3 17.3 %collective-permute-start.14 = (bf16[18,512]{1,0:T(8,128)(2,1)S(1)}, bf16[18,512]{1,0:T(8,128)(2,1)S(1)}, u32[]{:S(2)}, u32[]{:S(2)}) collective-permute-start(bf16[18,512]{1,0:T(8,128)(2,1)S(1)} %pad_maximum_fusion.3), channel_id=1, source_target_pairs={{1,0},{2,1},{3,2},{0,3},{5,4},{6,5},{7,6},{4,7},{9,8},{10,9},{11,1... | collective-permute-start | bytes 55304 | tf_op jit(solution)/shard_map/ppermute | solution.py:599
  114.1 1.7 %copy-start.3 = (bf16[2,3,3,256,256]{4,3,2,1,0:T(8,128)(2,1)S(1)}, bf16[2,3,3,256,256]{4,3,2,1,0:T(8,128)(2,1)}, u32[]{:S(2)}) copy-start(bf16[2,3,3,256,256]{4,3,2,1,0:T(8,128)(2,1)} %sea_ref.1) | copy-start | bytes 7077892
where the time goes:
time: 135 us; the launch traced here: 134 us
  Pallas kernels  42.1 us (31%)
  waiting for transfers between devices  38.1 us (28%)
  starting transfers between devices  36 us (27%)
  local copies, waits for them, and re-layouts  13.6 us (10%)
  other arithmetic  3.78 us (3%)
    ppermute x7, waiting for transfers between devices, exchange(): lax.ppermute(value, axis, [(i, i ^ bit) for i in range(lax.axis_size(axis...  30.2 us
    pallas_call x1, Pallas kernels, conv_with_halo(): pl.pallas_call(functools.partial(conv_kernel, layer, True), out_shape=jax...  14.8 us
    pallas_call x1, Pallas kernels, conv_inside(): pl.pallas_call(functools.partial(conv_kernel, layer, False), out_shape=(j...  13.8 us
    all_to_all x2, starting transfers between devices, to_owners(): lax.all_to_all(value, ('lat', 'lon'), split_axis=0, concat_axis=0, tiled=...  12.1 us
    unnamed x27, local copies, waits for them, and re-layouts  12.1 us
    ppermute x7, starting transfers between devices, exchange(): lax.ppermute(value, axis, [(i, i ^ bit) for i in range(lax.axis_size(axis...  9.58 us
    ppermute x2, starting transfers between devices, halo_of(): above = lax.ppermute(bottom, 'lat', down)  8.42 us
    pallas_call x1, Pallas kernels, payloads(): pl.pallas_call(payload_kernel, out_shape=(slots, slots), in_specs=[SMEM,...  5.09 us
  transfers between devices with their start and end apart: 17, of which 8 were waited for; matrix products, arithmetic and copies ran while one was open for 5% of the time, Pallas kernels for 21%

commit v1 on v0

v1 whole, which is shorter than its diff:
```python
import functools

import jax
import jax.numpy as jnp
from jax import lax
from jax.experimental import pallas as pl
from jax.experimental.pallas import tpu as pltpu
from jax.sharding import PartitionSpec as P

BLOCK_ROWS = 8
BLOCK_COLS = 16
BLOCK = BLOCK_ROWS * BLOCK_COLS
SLOTS = 2
HALF = BLOCK // 2
HALF_ROWS = BLOCK_ROWS // 2
VMEM_BYTES = 28 * 2**20

F32 = jnp.float32
BF16 = jnp.bfloat16

VMEM = pl.BlockSpec(memory_space=pltpu.VMEM)
SMEM = pl.BlockSpec(memory_space=pltpu.SMEM)
HBM = pl.BlockSpec(memory_space=pltpu.HBM)


def silu(v):
    return v / (1.0 + jnp.exp(-v))


def iota(shape, dim):
    return lax.broadcasted_iota(jnp.int32, shape, dim)


def dot(a, b):
    return jnp.dot(a, b, preferred_element_type=F32)


def params(**kwargs):
    return pltpu.CompilerParams(vmem_limit_bytes=VMEM_BYTES, **kwargs)


def on_ocean():
    return lax.axis_index("grp") == 1


def fill_water(water_ref, wide_ref, turned_ref):
    rows, longitudes = water_ref.shape
    wide_ref[:, 0:rows] = water_ref[...].astype(F32).T
    for p in range(2):
        turned_ref[:, p * rows : (p + 1) * rows] = wide_ref[pl.ds(p, longitudes // 2, stride=2), :][:, 0:rows]


def water_scratch(cols):
    return [pltpu.VMEM((2 * cols, 128), F32), pltpu.VMEM((cols, 128), F32)]


def water_of_row(turned_ref, rows, r, width, start, size):
    parts = [
        jnp.broadcast_to(turned_ref[start : start + size, p * rows + r : p * rows + r + 1], (size, width))
        for p in range(2)
    ]
    return jnp.concatenate(parts, axis=1)


def rim_shapes(rows, cols, width):
    line = jax.ShapeDtypeStruct((cols, width), BF16)
    side = jax.ShapeDtypeStruct((rows, width), F32)
    return (line, line, side, side)


def put_rim(rim, r, rows, line):
    top_ref, bottom_ref, left_ref, right_ref = rim
    cols = line.shape[0]
    exact = line.astype(F32)
    left_ref[r : r + 1] = exact[0:1]
    right_ref[r : r + 1] = exact[cols - 1 : cols]
    if r == 0:
        top_ref[...] = line
    if r == rows - 1:
        bottom_ref[...] = line


def payload_kernel(
    lists_ref, state_hbm, matrices_hbm, water_ref, flux_hbm,
    first_ref, second_ref, lists_out, top_ref, bottom_ref, left_ref, right_ref,
    state_ref, matrices_ref, flux_ref, flux, surface, wide_water, turned, count, sems,
):
    rows, cols, width = state_ref.shape
    half = width // 2
    entries = matrices_ref.shape[0]
    tiles = second_ref.shape[0] // SLOTS
    ocean = on_ocean()
    pieces = 4
    step = rows // pieces
    flux_copy = pltpu.make_async_copy(flux_hbm, flux_ref, sems.at[pieces])
    matrices_copy = pltpu.make_async_copy(matrices_hbm, matrices_ref, sems.at[pieces + 1])
    state_copies = [
        pltpu.make_async_copy(state_hbm.at[pl.ds(k * step, step)], state_ref.at[pl.ds(k * step, step)], sems.at[k])
        for k in range(pieces)
    ]
    flux_copy.start()
    for copy in state_copies:
        copy.start()
    matrices_copy.start()

    def clear(t, _):
        count[t] = 0
        return 0

    lax.fori_loop(0, tiles, clear, 0)

    def keep(e, _):
        for k in range(3):
            lists_out[k, e] = lists_ref[k, e]
        return 0

    lax.fori_loop(0, entries, keep, 0)
    i = iota((BLOCK, BLOCK), 0)
    j = iota((BLOCK, BLOCK), 1)

    def put(e, payload):
        owner = lists_ref[0, e]
        rank = count[owner]
        count[owner] = rank + 1
        first_ref[e] = payload[:HALF]
        second_ref[owner * SLOTS + rank] = payload[HALF:]

    flux_copy.wait()

    @pl.when(jnp.logical_not(ocean))
    def _():
        p, r, c = (i // 32) % 2, (i // 64) * 4 + (i // 8) % 4, i % 8
        turn = (j == r * BLOCK_COLS + 2 * c + p).astype(BF16)
        for k in range(pieces):
            state_copies[k].wait()
            block = state_ref[k * step : (k + 1) * step].reshape(step * cols, width)
            flux[k * step : (k + 1) * step] = (
                dot(block, flux_ref[...]).astype(BF16).reshape(step, cols, half)
            )
        matrices_copy.wait()
        across = cols // BLOCK_COLS

        def entry(e, _):
            source = lists_ref[1, e]
            r0 = (source // across) * BLOCK_ROWS
            c0 = pl.multiple_of((source % across) * BLOCK_COLS, BLOCK_COLS)
            chosen = flux[pl.ds(r0, BLOCK_ROWS), pl.ds(c0, BLOCK_COLS), :].reshape(BLOCK, half)
            weight = dot(turn, matrices_ref[e]).astype(BF16)
            put(e, dot(weight, chosen).astype(BF16))
            return 0

        lax.fori_loop(0, entries, entry, 0, unroll=8)

    @pl.when(ocean)
    def _():
        p, r, c = j // 64, (j // 8) % 8, j % 8
        turn = (i == r * BLOCK_COLS + 2 * c + p).astype(BF16)
        fill_water(water_ref, wide_water, turned)
        for k in range(pieces):
            state_copies[k].wait()
            for r0 in range(k * step, (k + 1) * step):
                surface[r0] = state_ref[r0].astype(F32) * water_of_row(turned, rows, r0, half, 0, cols)
        matrices_copy.wait()
        wide = BLOCK_COLS // 2
        across = cols // wide

        def entry(e, _):
            source = lists_ref[1, e]
            r0 = (source // across) * BLOCK_ROWS
            c0 = pl.multiple_of((source % across) * wide, wide)
            block = surface[pl.ds(r0, BLOCK_ROWS), pl.ds(c0, wide), :]
            chosen = jnp.concatenate(
                [block[:, :, q * half : (q + 1) * half].reshape(BLOCK // 2, half) for q in range(2)], axis=0
            ).astype(BF16)
            weight = dot(matrices_ref[e], turn).astype(BF16)
            put(e, dot(weight, chosen).astype(BF16))
            return 0

        lax.fori_loop(0, entries, entry, 0, unroll=8)

    for r in range(rows):
        put_rim((top_ref, bottom_ref, left_ref, right_ref), r, rows, state_ref[r])


def payloads(lists, state, matrices, water, flux_projection, tiles):
    rows, cols, width = state.shape
    half = width // 2
    entries = lists.shape[1]
    return pl.pallas_call(
        payload_kernel,
        out_shape=(
            jax.ShapeDtypeStruct((entries, HALF, half), BF16),
            jax.ShapeDtypeStruct((tiles * SLOTS, HALF, half), BF16),
            jax.ShapeDtypeStruct(lists.shape, jnp.int32),
        )
        + rim_shapes(rows, cols, width),
        in_specs=[SMEM, HBM, HBM, VMEM, HBM],
        out_specs=(VMEM, VMEM, SMEM) + (VMEM,) * 4,
        scratch_shapes=[
            pltpu.VMEM(state.shape, BF16),
            pltpu.VMEM(matrices.shape, BF16),
            pltpu.VMEM(flux_projection.shape, BF16),
            pltpu.VMEM((rows, cols, half), BF16),
            pltpu.VMEM((rows, cols, width), F32),
        ]
        + water_scratch(cols)
        + [pltpu.SMEM((tiles,), jnp.int32), pltpu.SemaphoreType.DMA((6,))],
        compiler_params=params(),
        name="payload",
    )(lists, state, matrices, water, flux_projection)


def pack_kernel(
    lists_ref, dense_ref, above_ref, below_ref, left_ref, right_ref,
    slots_ref, labels_ref, west_ref, east_ref, count,
):
    tiles, _, entries = lists_ref.shape
    rows = left_ref.shape[0]
    cols = above_ref.shape[0]
    me = lax.axis_index("lat") * lax.axis_size("lon") + lax.axis_index("lon")

    def clear(t, _):
        count[t] = 0
        for slot in range(SLOTS):
            labels_ref[t * SLOTS + slot] = -1
        return 0

    lax.fori_loop(0, tiles, clear, 0)

    def place(e, _):
        owner = lists_ref[0, 0, e]
        rank = count[owner]
        count[owner] = rank + 1
        slots_ref[owner * SLOTS + rank] = dense_ref[e]
        return 0

    lax.fori_loop(0, entries, place, 0)

    def source(t, _):
        def entry(e, rank):
            hit = lists_ref[t, 0, e] == me

            @pl.when(hit)
            def _():
                labels_ref[jnp.bitwise_xor(t, me) * SLOTS + rank] = lists_ref[t, 2, e]

            return rank + hit.astype(jnp.int32)

        lax.fori_loop(0, entries, entry, 0, unroll=8)
        return 0

    lax.fori_loop(0, tiles, source, 0)
    side_message(above_ref, below_ref, left_ref, right_ref, west_ref, east_ref, rows, cols)


def side_message(above_ref, below_ref, left_ref, right_ref, west_ref, east_ref, rows, cols):
    for ref, side, at in ((west_ref, left_ref, 0), (east_ref, right_ref, cols - 1)):
        ref[0:1] = above_ref[at : at + 1].astype(F32)
        ref[1 : rows + 1] = side[...]
        ref[rows + 1 : rows + 2] = below_ref[at : at + 1].astype(F32)


def pack(held, dense, above, below, left, right):
    tiles = held.shape[0]
    rows, width = left.shape
    side = jax.ShapeDtypeStruct((rows + 2, width), F32)
    return pl.pallas_call(
        pack_kernel,
        out_shape=(
            jax.ShapeDtypeStruct((tiles * SLOTS,) + dense.shape[1:], BF16),
            jax.ShapeDtypeStruct((tiles * SLOTS,), jnp.int32),
            side,
            side,
        ),
        in_specs=[SMEM] + [VMEM] * 5,
        out_specs=(VMEM, SMEM, VMEM, VMEM),
        scratch_shapes=[pltpu.SMEM((tiles,), jnp.int32)],
        compiler_params=params(),
        name="pack",
    )(held, dense, above, below, left, right)


GROUP = 4


def set_columns(line, before, after):
    cols = line.shape[0]
    at = iota(line.shape, 0)
    left = jnp.where(at == 0, before, pltpu.roll(line, 1, 0))
    right = jnp.where(at == cols - 1, after, pltpu.roll(line, cols - 1, 0))
    return left, right


def air_line(h, before, after):
    left, right = set_columns(h, before, after)
    return jnp.concatenate([left, h, right], axis=1).astype(BF16)


def sea_line(h, before, after):
    half = h.shape[1] // 2
    left, _ = set_columns(h[:, half:], before[:, half:], after[:, half:])
    _, right = set_columns(h[:, :half], before[:, :half], after[:, :half])
    return jnp.concatenate([left, h, right], axis=1).astype(BF16)


def air_product(block, kernel):
    return dot(block, kernel.reshape(-1, kernel.shape[-1]))


def sea_product(block, kernel):
    width = kernel.shape[-1]
    flat = kernel.reshape(-1, width)
    return jnp.concatenate(
        [dot(block[:, : 3 * width], flat), dot(block[:, width : 4 * width], flat)], axis=1
    )


def each_component(run, air_ref, sea_ref):
    ocean = on_ocean()

    @pl.when(jnp.logical_not(ocean))
    def _():
        run(air_ref, air_line, air_product, False)

    @pl.when(ocean)
    def _():
        run(sea_ref, sea_line, sea_product, True)


def halo_conv_kernel(
    layer, x_ref, top_ref, bottom_ref, left_ref, right_ref, air_ref, sea_ref, sum_ref, lined
):
    rows, cols, width = x_ref.shape

    def run(kernels_ref, make_line, product, masked):
        wide = (2 if masked else 3) * width
        before_all = silu(left_ref[...])
        after_all = silu(right_ref[...])

        def put(r):
            line = top_ref[...] if r == 0 else bottom_ref[...] if r == rows + 1 else x_ref[r - 1]
            lined[r, :, 0:wide] = make_line(
                silu(line.astype(F32)), before_all[r : r + 1], after_all[r : r + 1]
            )

        put(0)
        put(1)
        for r0 in range(0, rows, GROUP):
            for k in range(GROUP):
                put(r0 + k + 2)
            total = x_ref[r0 : r0 + GROUP].astype(F32).reshape(GROUP * cols, width)
            for d in range(3):
                block = lined[r0 + d : r0 + d + GROUP, :, 0:wide].reshape(GROUP * cols, wide)
                total = total + product(block, kernels_ref[layer, d])
            sum_ref[r0 : r0 + GROUP] = total.reshape(GROUP, cols, width)

    each_component(run, air_ref, sea_ref)


def inside_conv_kernel(
    layer, begin, end, *refs
):
    if begin:
        refs = refs[1:]
    x_ref, water_ref, air_ref, sea_ref, out_hbm, line_ref, sides_ref, token_ref = refs[:8]
    lined, out, wide_water, turned, sems = refs[8:]
    rows, cols, width = x_ref.shape
    half = width // 2
    token_ref[...] = jnp.zeros_like(token_ref)

    def write(g):
        at = g * GROUP
        return pltpu.make_async_copy(
            out.at[pl.ds(at, GROUP)], out_hbm.at[pl.ds(begin + at, GROUP)], sems.at[g]
        )

    def run(kernels_ref, make_line, product, masked):
        wide = (2 if masked else 3) * width
        none = jnp.zeros((1, width), F32)

        def put(r):
            if 0 <= r < rows:
                line = make_line(silu(x_ref[r].astype(F32)), none, none)
            else:
                line = jnp.zeros((cols, wide), BF16)
            lined[r - begin + 1, :, 0:wide] = line

        if masked:
            fill_water(water_ref, wide_water, turned)
        put(begin - 1)
        put(begin)
        for r0 in range(begin, end, GROUP):
            for k in range(GROUP):
                put(r0 + k + 1)
            total = x_ref[r0 : r0 + GROUP].astype(F32).reshape(GROUP * cols, width)
            for d in range(3):
                at = r0 - begin + d
                block = lined[at : at + GROUP, :, 0:wide].reshape(GROUP * cols, wide)
                total = total + product(block, kernels_ref[layer, d])
            total = total.reshape(GROUP, cols, width)
            for k in range(GROUP):
                r = r0 + k
                line = total[k]
                if r == 0 or r == rows - 1:
                    line_ref[...] = line
                sides_ref[0, r - begin] = line[:BLOCK_COLS]
                sides_ref[1, r - begin] = line[cols - BLOCK_COLS :]
                if masked:
                    line = line * water_of_row(turned, rows, r, half, 0, cols)
                out[r - begin] = line.astype(BF16)
            write((r0 - begin) // GROUP).start()

    each_component(run, air_ref, sea_ref)
    for g in range((end - begin) // GROUP):
        write(g).wait()


def conv_cost(state, rows):
    cells = rows * state.shape[1]
    width = state.shape[2]
    return pl.CostEstimate(
        flops=2 * 9 * cells * width * width,
        bytes_accessed=cells * width * 6,
        transcendentals=cells * width,
    )


def conv_with_halo(layer, state, halo, air_kernels, sea_kernels):
    rows, cols, width = state.shape
    return pl.pallas_call(
        functools.partial(halo_conv_kernel, layer),
        out_shape=jax.ShapeDtypeStruct(state.shape, F32),
        in_specs=[VMEM] * 7,
        out_specs=VMEM,
        scratch_shapes=[pltpu.VMEM((rows + 2, cols, 3 * width), BF16)],
        compiler_params=params(),
        cost_estimate=conv_cost(state, rows),
        name="conv_halo",
    )(state, *halo, air_kernels, sea_kernels)


def conv_inside(layer, part, state, water, air_kernels, sea_kernels, out=None):
    rows, cols, width = state.shape
    count = rows // 2
    begin = part * count
    before = [] if out is None else [out]
    return pl.pallas_call(
        functools.partial(inside_conv_kernel, layer, begin, begin + count),
        out_shape=(
            jax.ShapeDtypeStruct(state.shape, BF16),
            jax.ShapeDtypeStruct((cols, width), F32),
            jax.ShapeDtypeStruct((2, count, BLOCK_COLS, width), F32),
            jax.ShapeDtypeStruct((8, 128), F32),
        ),
        in_specs=[HBM] * len(before) + [VMEM] * 4,
        out_specs=(HBM, VMEM, VMEM, VMEM),
        scratch_shapes=[
            pltpu.VMEM((count + 2, cols, 3 * width), BF16),
            pltpu.VMEM((count, cols, width), BF16),
        ]
        + water_scratch(cols)
        + [pltpu.SemaphoreType.DMA((count // GROUP,))],
        input_output_aliases={0: 0} if before else {},
        compiler_params=params(),
        cost_estimate=conv_cost(state, count),
        name="conv_inside",
    )(*before, state, water, air_kernels, sea_kernels)


def edge_kernel(
    layer, out_in_hbm, first_ref, last_ref, upper_ref, lower_ref, top_ref, bottom_ref, left_ref, right_ref,
    water_ref, air_ref, sea_ref, out_hbm, line_out, side_out, wide_water, turned, sems,
):
    del out_in_hbm
    rows = upper_ref.shape[1] + lower_ref.shape[1]
    cols, width = first_ref.shape
    half = width // 2
    inner = pl.ds(1, rows - 2)
    writes = [
        pltpu.make_async_copy(line_out.at[0], out_hbm.at[0], sems.at[0]),
        pltpu.make_async_copy(line_out.at[1], out_hbm.at[rows - 1], sems.at[1]),
        pltpu.make_async_copy(side_out.at[0], out_hbm.at[inner, pl.ds(0, BLOCK_COLS)], sems.at[2]),
        pltpu.make_async_copy(
            side_out.at[1], out_hbm.at[inner, pl.ds(cols - BLOCK_COLS, BLOCK_COLS)], sems.at[3]
        ),
    ]

    def run(kernels_ref, make_line, product, masked):
        none = jnp.zeros((1, width), F32)
        before = silu(left_ref[...])
        after = silu(right_ref[...])
        if masked:
            before, after = before[:, half:], after[:, :half]
            fill_water(water_ref, wide_water, turned)
        size = before.shape[1]
        west = jnp.zeros((rows, size), F32)
        east = jnp.zeros((rows, size), F32)
        for d in range(3):
            west = west + dot(before[d : d + rows].astype(BF16), kernels_ref[layer, d, 0])
            east = east + dot(after[d : d + rows].astype(BF16), kernels_ref[layer, d, 2])
        if masked:
            blank = jnp.zeros((rows, half), F32)
            west = jnp.concatenate([west, blank], axis=1)
            east = jnp.concatenate([blank, east], axis=1)

        def finish(value, r, start, size):
            if masked:
                value = value * water_of_row(turned, rows, r, half, start, size)
            return value.astype(BF16)

        at = iota((BLOCK_COLS, width), 0)
        for r in range(1, rows - 1):
            sides, k = (upper_ref, r) if r < rows // 2 else (lower_ref, r - rows // 2)
            total = sides[0, k] + jnp.where(at == 0, west[r : r + 1], 0.0)
            side_out[0, r - 1] = finish(total, r, 0, BLOCK_COLS)
            total = sides[1, k] + jnp.where(at == BLOCK_COLS - 1, east[r : r + 1], 0.0)
            side_out[1, r - 1] = finish(total, r, cols - BLOCK_COLS, BLOCK_COLS)
        writes[2].start()
        writes[3].start()
        at = iota((cols, width), 0)
        for k, (partial, line, d) in enumerate(((first_ref, top_ref, 0), (last_ref, bottom_ref, 2))):
            r = 0 if k == 0 else rows - 1
            lined = make_line(silu(line[...].astype(F32)), none, none)
            total = partial[...] + product(lined, kernels_ref[layer, d])
            total = total + jnp.where(at == 0, west[r : r + 1], 0.0)
            total = total + jnp.where(at == cols - 1, east[r : r + 1], 0.0)
            line_out[k] = finish(total, r, 0, cols)
            writes[k].start()

    each_component(run, air_ref, sea_ref)
    for copy in writes:
        copy.wait()


def fix_edges(layer, out, first, last, upper, lower, halo, water, air_kernels, sea_kernels):
    rows, cols, width = out.shape
    return pl.pallas_call(
        functools.partial(edge_kernel, layer),
        out_shape=jax.ShapeDtypeStruct(out.shape, BF16),
        in_specs=[HBM] + [VMEM] * 11,
        out_specs=HBM,
        scratch_shapes=[
            pltpu.VMEM((2, cols, width), BF16),
            pltpu.VMEM((2, rows - 2, BLOCK_COLS, width), BF16),
        ]
        + water_scratch(cols)
        + [pltpu.SemaphoreType.DMA((4,))],
        input_output_aliases={0: 0},
        compiler_params=params(),
        name="fix_edges",
    )(out, first, last, upper, lower, *halo, water, air_kernels, sea_kernels)


def update_kernel(
    labels_ref, first_hbm, second_hbm, sum_ref, water_ref, coupling_ref,
    new_ref, top_ref, bottom_ref, left_ref, right_ref,
    total, arrived, wide_water, turned, sems,
):
    rows, cols, width = new_ref.shape
    half = width // 2
    slots = first_hbm.shape[0]
    ocean = on_ocean()
    quarter = rows // 4
    halves = (first_hbm, second_hbm)

    def copy_of(h, s):
        return pltpu.make_async_copy(halves[h].at[s], arrived.at[h, s], sems.at[h, s])

    def each_slot(act):
        def one(s, _):
            label = labels_ref[s]

            @pl.when(label >= 0)
            def _():
                act(s, label)

            return 0

        lax.fori_loop(0, slots, one, 0)

    def fetch(s, label):
        copy_of(0, s).start()
        copy_of(1, s).start()

    each_slot(fetch)

    def store(r, line):
        low = line.astype(BF16)
        new_ref[r] = low
        put_rim((top_ref, bottom_ref, left_ref, right_ref), r, rows, low)

    @pl.when(jnp.logical_not(ocean))
    def _():
        total[:, :, 0:half] = jnp.zeros((rows, cols, half), F32)
        across = cols // BLOCK_COLS

        def add(s, label):
            r0 = (label // across) * BLOCK_ROWS
            c0 = pl.multiple_of((label % across) * BLOCK_COLS, BLOCK_COLS)
            for h in range(2):
                copy_of(h, s).wait()
                value = arrived[h, s].astype(F32).reshape(HALF_ROWS, BLOCK_COLS, half)
                total[pl.ds(r0 + h * HALF_ROWS, HALF_ROWS), pl.ds(c0, BLOCK_COLS), 0:half] += value

        each_slot(add)
        for k in range(4):
            r0 = k * quarter
            block = total[r0 : r0 + quarter, :, 0:half].astype(BF16).reshape(quarter * cols, half)
            force = dot(block, coupling_ref[...]).reshape(quarter, cols, width)
            for q in range(quarter):
                store(r0 + q, sum_ref[r0 + q] + force[q])

    @pl.when(ocean)
    def _():
        total[...] = jnp.zeros_like(total)
        fill_water(water_ref, wide_water, turned)
        wide = BLOCK_COLS // 2
        across = cols // wide

        def add(s, label):
            r0 = (label // across) * BLOCK_ROWS
            c0 = pl.multiple_of((label % across) * wide, wide)
            for h in range(2):
                copy_of(h, s).wait()
                value = arrived[h, s].astype(F32).reshape(2, HALF_ROWS, wide, half)
                for p in range(2):
                    total[
                        pl.ds(r0 + h * HALF_ROWS, HALF_ROWS), pl.ds(c0, wide), p * half : (p + 1) * half
                    ] += value[p]

        each_slot(add)
        for r in range(rows):
            store(r, (sum_ref[r] + total[r]) * water_of_row(turned, rows, r, half, 0, cols))


def update(labels, first, second, summed, water, coupling_matrix):
    rows, cols, width = summed.shape
    return pl.pallas_call(
        update_kernel,
        out_shape=(jax.ShapeDtypeStruct((rows, cols, width), BF16),) + rim_shapes(rows, cols, width),
        in_specs=[SMEM, HBM, HBM, VMEM, VMEM, VMEM],
        out_specs=(VMEM,) * 5,
        scratch_shapes=[
            pltpu.VMEM((rows, cols, width), F32),
            pltpu.VMEM((2,) + first.shape, BF16),
        ]
        + water_scratch(cols)
        + [pltpu.SemaphoreType.DMA((2, first.shape[0]))],
        compiler_params=params(),
        name="update",
    )(labels, first, second, summed, water, coupling_matrix)


def exchange(value, axis, bit):
    return lax.ppermute(value, axis, [(i, i ^ bit) for i in range(lax.axis_size(axis))])


def across_groups(value):
    return exchange(value, "grp", 1)


def to_owners(value):
    return lax.all_to_all(value, ("lat", "lon"), split_axis=0, concat_axis=0, tiled=True)


def all_lists(lists):
    held = across_groups(lists)[None]
    for axis in ("lon", "lat"):
        bit = 1
        while bit < lax.axis_size(axis):
            held = jnp.concatenate([held, exchange(held, axis, bit)], axis=0)
            bit *= 2
    return held


def rows_beside(top, bottom):
    lats = lax.axis_size("lat")
    above = lax.ppermute(bottom, "lat", [(i, i + 1) for i in range(lats - 1)])
    below = lax.ppermute(top, "lat", [(i + 1, i) for i in range(lats - 1)])
    return above, below


def columns_beside(west, east):
    lons = lax.axis_size("lon")
    before = lax.ppermute(east, "lon", [(i, (i + 1) % lons) for i in range(lons)])
    after = lax.ppermute(west, "lon", [((i + 1) % lons, i) for i in range(lons)])
    return before, after


def body(
    state,
    intersection_lists,
    intersection_matrices,
    water,
    air_kernels,
    sea_kernels,
    flux_projection,
    coupling_matrix,
):
    current = state[0]
    tiles = lax.axis_size("lat") * lax.axis_size("lon")
    entries = intersection_lists.shape[-1]
    lists = intersection_lists.reshape(3, entries)
    matrices = intersection_matrices.reshape(entries, BLOCK, BLOCK)

    first, second, lists, top, bottom, left, right = payloads(
        lists, current, matrices, water, flux_projection, tiles
    )
    first = across_groups(first)
    second = to_owners(second)
    above, below = rows_beside(top, bottom)
    first, labels, west, east = pack(all_lists(lists), first, above, below, left, right)
    second = across_groups(second)
    first = to_owners(first)
    before, after = columns_beside(west, east)
    summed = conv_with_halo(0, current, (above, below, before, after), air_kernels, sea_kernels)
    current, top, bottom, left, right = update(labels, first, second, summed, water, coupling_matrix)

    above, below = rows_beside(top, bottom)
    out, first, upper, token = conv_inside(1, 0, current, water, air_kernels, sea_kernels)
    corner = token[0, 0]
    west = jnp.concatenate([above[:1].astype(F32), left, below[:1].astype(F32)], axis=0) + corner
    east = jnp.concatenate([above[-1:].astype(F32), right, below[-1:].astype(F32)], axis=0) + corner
    before, after = columns_beside(west, east)
    out, last, lower, _ = conv_inside(1, 1, current, water, air_kernels, sea_kernels, out)
    out = fix_edges(
        1, out, first, last, upper, lower, (above, below, before, after), water, air_kernels, sea_kernels
    )
    return out[None]


def solution(mesh):
    placed = (
        P("grp", "lat", "lon", None),
        P("grp", "lat", "lon", None, None),
        P("grp", "lat", "lon", None, None, None),
        P("lat", "lon"),
        P(),
        P(),
        P(),
        P(),
    )
    return jax.shard_map(
        body, mesh=mesh, in_specs=placed, out_specs=P("grp", "lat", "lon", None), check_vma=False
    )
```

time: 135 us -> 122 us (0.904)
  the two profiles are of different devices: /device:TPU:0 before, /device:TPU:24 now
where the time goes in v1:
time: 122 us; the launch traced here: 121 us
  Pallas kernels  37.7 us (31%)
  starting transfers between devices  33.9 us (28%)
  local copies, waits for them, and re-layouts  24.6 us (20%)
  waiting for transfers between devices  23.2 us (19%)
  other arithmetic  1.29 us (1%)
    unnamed x43, local copies, waits for them, and re-layouts  24.1 us
    ppermute x7, waiting for transfers between devices, exchange(): lax.ppermute(value, axis, [(i, i ^ bit) for i in range(lax.axis_size(axis...  16.4 us
    pallas_call x2, Pallas kernels, conv_inside(): pl.pallas_call(functools.partial(inside_conv_kernel, layer, begin, begin...  12.6 us
    all_to_all x2, starting transfers between devices, to_owners(): lax.all_to_all(value, ('lat', 'lon'), split_axis=0, concat_axis=0, tiled=...  12.2 us
    pallas_call x1, Pallas kernels, conv_with_halo(): pl.pallas_call(functools.partial(halo_conv_kernel, layer), out_shape=jax....  10.4 us
    ppermute x2, starting transfers between devices, rows_beside(): below = lax.ppermute(top, 'lat', [(i + 1, i) for i in range(lats - 1)])  9.11 us
    ppermute x2, waiting for transfers between devices, columns_beside(): lax.ppermute(east, 'lon', [(i, (i + 1) % lons) for i in range(lons)])  6.76 us
    ppermute x7, starting transfers between devices, exchange(): lax.ppermute(value, axis, [(i, i ^ bit) for i in range(lax.axis_size(axis...  6.37 us
  transfers between devices with their start and end apart: 17, of which 5 were waited for; matrix products, arithmetic and copies ran while one was open for 1% of the time, Pallas kernels for 22%

profile of v1, /device:TPU:24, one launch (start us, length us, event | category | flops | bytes accessed | tf_op | source)
XLA Modules:
  0.0 121.0 jit_solution(11811587180366762615)
XLA Ops:
  0.0 0.7 copy.13
  0.7 1.6 %copy-done.5 = bf16[1,16,128,512]{3,2,1,0:T(8,128)(2,1)S(1)} copy-done((bf16[1,16,128,512]{3,2,1,0:T(8,128)(2,1)S(1)}, bf16[1,16,128,512]{3,2,1,0:T(8,128)(2,1)}, u32[]{:S(2)}) %copy-start.5) | copy-done | bytes 2097176
  2.3 1.0 copy-done.8
  3.3 0.9 copy-done.9
  4.3 0.7 copy-done.11
  5.0 5.4 %payload.1 = (bf16[16,64,256]{2,1,0:T(8,128)(2,1)S(1)}, bf16[32,64,256]{2,1,0:T(8,128)(2,1)}, s32[3,16]{1,0:T(4,128)S(1)}, bf16[128,512]{1,0:T(8,128)(2,1)S(1)},...) custom-call(s32[3,16]{1,0:T(4,128)S(1)} %bitcast.12, ...), custom_call_target="tpu_custom_call" | custom-call | tf_op jit(solution)/shard_map/payload/pallas_call | solution.py:189
  10.4 6.2 %all-to-all-start.1 = ((bf16[32,64,256]{2,1,0:T(8,128)(2,1)}), bf16[32,64,256]{2,1,0:T(8,128)(2,1)}, u32[]{:S(2)}, u32[]{:S(2)}) async-start(bf16[32,64,256]{2,1,0:T(8,128)(2,1)} %get-tuple-element.36), calls=%async_computation.1 | async-start | bytes 2097152 | tf_op jit(solution)/shard_map/all_to_all | solution.py:663
  16.6 0.8 collective-permute-start
  17.4 1.3 %collective-permute-start.6 = (bf16[128,512]{1,0:T(8,128)(2,1)S(1)}, bf16[128,512]{1,0:T(8,128)(2,1)S(1)}, u32[]{:S(2)}, u32[]{:S(2)}) collective-permute-start(bf16[128,512]{1,0:T(8,128)(2,1)S(1)} %get-tuple-element.30), channel_id=1, source_target_pairs={{0,4},{4,8},{8,12},{1,5},{5,9},{9,13},{2,6},{6,10},{10,14},{3,7},{... | collective-permute-start | bytes 393224 | tf_op jit(solution)/shard_map/ppermute | solution.py:678
  18.7 4.6 %collective-permute-start.7 = (bf16[128,512]{1,0:T(8,128)(2,1)S(1)}, bf16[128,512]{1,0:T(8,128)(2,1)S(1)}, u32[]{:S(2)}, u32[]{:S(2)}) collective-permute-start(bf16[128,512]{1,0:T(8,128)(2,1)S(1)} %get-tuple-element.31), channel_id=1, source_target_pairs={{4,0},{8,4},{12,8},{5,1},{9,5},{13,9},{6,2},{10,6},{14,10},{7,3},{... | collective-permute-start | bytes 393224 | tf_op jit(solution)/shard_map/ppermute | solution.py:679
  23.3 1.3 %collective-permute-start.5 = (bf16[16,64,256]{2,1,0:T(8,128)(2,1)S(1)}, bf16[16,64,256]{2,1,0:T(8,128)(2,1)S(1)}, u32[]{:S(2)}, u32[]{:S(2)}) collective-permute-start(bf16[16,64,256]{2,1,0:T(8,128)(2,1)S(1)} %get-tuple-element.29), channel_id=1, source_target_pairs={{0,16},{16,0},{1,17},{17,1},{2,18},{18,2},{3,19},{19,3},{4,20},{20... | collective-permute-start | bytes 1572872 | tf_op jit(solution)/shard_map/ppermute | solution.py:655
  24.5 1.1 collective-permute-done.1
  25.7 1.5 %collective-permute-start.2 = (s32[2,3,16]{2,1,0:T(4,128)S(1)}, s32[2,3,16]{2,1,0:T(4,128)S(1)}, u32[]{:S(2)}, u32[]{:S(2)}) collective-permute-start(s32[2,3,16]{2,1,0:T(4,128)S(1)} %pad_add_fusion.2), channel_id=1, source_target_pairs={{0,2},{1,3},{2,0},{3,1},{4,6},{5,7},{6,4},{7,5},{8,10},{9,11},{10,... | collective-permute-start | bytes 1160 | tf_op jit(solution)/shard_map/ppermute | solution.py:655
  27.2 2.1 %collective-permute-done.2 = s32[2,3,16]{2,1,0:T(4,128)S(1)} collective-permute-done((s32[2,3,16]{2,1,0:T(4,128)S(1)}, s32[2,3,16]{2,1,0:T(4,128)S(1)}, u32[]{:S(2)}, u32[]{:S(2)}) %collective-permute-start.2) | collective-permute-done | bytes 416 | tf_op jit(solution)/shard_map/ppermute | solution.py:655
  29.3 0.6 collective-permute-start.3
  29.9 7.4 %collective-permute-done.3 = s32[4,3,16]{2,1,0:T(4,128)S(1)} collective-permute-done((s32[4,3,16]{2,1,0:T(4,128)S(1)}, s32[4,3,16]{2,1,0:T(4,128)S(1)}, u32[]{:S(2)}, u32[]{:S(2)}) %collective-permute-start.3) | collective-permute-done | bytes 800 | tf_op jit(solution)/shard_map/ppermute | solution.py:655
  37.3 1.4 %collective-permute-start.4 = (s32[8,3,16]{2,1,0:T(4,128)S(1)}, s32[8,3,16]{2,1,0:T(4,128)S(1)}, u32[]{:S(2)}, u32[]{:S(2)}) collective-permute-start(s32[8,3,16]{2,1,0:T(4,128)S(1)} %pad_add_fusion), channel_id=1, source_target_pairs={{0,8},{4,12},{8,0},{12,4},{1,9},{5,13},{9,1},{13,5},{2,10},{6,14},... | collective-permute-start | bytes 4616 | tf_op jit(solution)/shard_map/ppermute | solution.py:655
  38.7 5.7 %collective-permute-done.4 = s32[8,3,16]{2,1,0:T(4,128)S(1)} collective-permute-done((s32[8,3,16]{2,1,0:T(4,128)S(1)}, s32[8,3,16]{2,1,0:T(4,128)S(1)}, u32[]{:S(2)}, u32[]{:S(2)}) %collective-permute-start.4) | collective-permute-done | bytes 1568 | tf_op jit(solution)/shard_map/ppermute | solution.py:655
  44.4 3.7 %pack.1 = (bf16[32,64,256]{2,1,0:T(8,128)(2,1)S(1)}, s32[32]{0:T(128)S(1)}, f32[18,512]{1,0:T(8,128)S(1)}, f32[18,512]{1,0:T(8,128)S(1)}) custom-call(s32[16,3,16]{2,1,0:T(4,128)S(1)} %constant_dynamic-update-slice_fusion.lists_ref, bf16[16,64,256]{2,1,0:T(8,128)(2,1)S(1)} %collective-permute-done.5.dense_ref, ...), custom_call_target="tpu_custom_call" | custom-call | tf_op jit(solution)/shard_map/pack/pallas_call | solution.py:267
  48.1 1.0 copy-done.7
  49.1 0.6 copy-done.13
  49.8 0.6 copy-done.15
  50.4 0.6 copy-done.17
  51.0 0.6 copy-done.18
  51.6 6.0 %all-to-all-start = ((bf16[32,64,256]{2,1,0:T(8,128)(2,1)}), bf16[32,64,256]{2,1,0:T(8,128)(2,1)S(1)}, u32[]{:S(2)}, u32[]{:S(2)}) async-start(bf16[32,64,256]{2,1,0:T(8,128)(2,1)} %copy-done.7), calls=%async_computation | async-start | bytes 2097152 | tf_op jit(solution)/shard_map/all_to_all | solution.py:663
  57.6 0.8 collective-permute-start.8
  58.5 1.7 %collective-permute-start.10 = (f32[18,512]{1,0:T(8,128)}, f32[18,512]{1,0:T(8,128)S(1)}, u32[]{:S(2)}, u32[]{:S(2)}) collective-permute-start(f32[18,512]{1,0:T(8,128)} %copy-done.17), channel_id=1, source_target_pairs={{1,0},{2,1},{3,2},{0,3},{5,4},{6,5},{7,6},{4,7},{9,8},{10,9},{11,1... | collective-permute-start | bytes 110600 | tf_op jit(solution)/shard_map/ppermute | solution.py:686
  60.2 6.8 %collective-permute-done.9.left_ref = f32[18,512]{1,0:T(8,128)S(1)} collective-permute-done((f32[18,512]{1,0:T(8,128)}, f32[18,512]{1,0:T(8,128)S(1)}, u32[]{:S(2)}, u32[]{:S(2)}) %collective-permute-start.9) | collective-permute-done | bytes 36896 | tf_op jit(solution)/shard_map/ppermute | solution.py:685
  67.0 3.7 %copy-done = bf16[2,3,3,512,512]{4,3,2,1,0:T(8,128)(2,1)S(1)} copy-done((bf16[2,3,3,512,512]{4,3,2,1,0:T(8,128)(2,1)S(1)}, bf16[2,3,3,512,512]{4,3,2,1,0:T(8,128)(2,1)}, u32[]{:S(2)}) %copy-start) | copy-done | bytes 9437208
  70.7 1.6 %copy-done.6 = bf16[1,16,128,512]{3,2,1,0:T(8,128)(2,1)S(1)} copy-done((bf16[1,16,128,512]{3,2,1,0:T(8,128)(2,1)S(1)}, bf16[1,16,128,512]{3,2,1,0:T(8,128)(2,1)}, u32[]{:S(2)}) %copy-start.6) | copy-done | bytes 2097176
  72.3 0.9 copy-done.14
  73.2 10.4 %conv_halo.1.sum_ref = f32[16,128,512]{2,1,0:T(8,128)S(1)} custom-call(bf16[16,128,512]{2,1,0:T(8,128)(2,1)S(1)} %bitcast.10, bf16[128,512]{1,0:T(8,128)(2,1)S(1)} %collective-permute-done.6.above_ref.top_ref, bf16[128,512]{1,0:T(8,128)(2,1)S(1)} %copy-done.14, f32[18,512]{1,0:T(8,128)S(1)} %collective-permute-done.9.left_ref, ...), custom_call_target="tpu_custom_call" | custom-call | flops 9663676416 | bytes 6291456 | tf_op jit(solution)/shard_map/conv_halo/pallas_call | solution.py:430
  83.5 2.0 %copy-done.2 = f32[16,128,512]{2,1,0:T(8,128)} copy-done((f32[16,128,512]{2,1,0:T(8,128)}, f32[16,128,512]{2,1,0:T(8,128)S(1)}, u32[]{:S(2)}) %copy-start.2) | copy-done | bytes 4194328
  85.5 2.2 %copy-done.3 = f32[16,128,512]{2,1,0:T(8,128)S(1)} copy-done((f32[16,128,512]{2,1,0:T(8,128)S(1)}, f32[16,128,512]{2,1,0:T(8,128)}, u32[]{:S(2)}) %copy-start.3) | copy-done | bytes 4194328
  87.7 0.9 copy-done.10
  88.7 0.7 copy-done.16
  89.3 3.8 %update.1 = (bf16[16,128,512]{2,1,0:T(8,128)(2,1)S(1)}, bf16[128,512]{1,0:T(8,128)(2,1)S(1)}, bf16[128,512]{1,0:T(8,128)(2,1)S(1)}, f32[16,512]{1,0:T(8,128)S(1)}, f32[16,512]{1,0:T(8,128)S(1)}) custom-call(s32[32]{0:T(128)S(1)} %copy-done.16, bf16[32,64,256]{2,1,0:T(8,128)(2,1)S(1)} %all-to-all-done.first_hbm, ...), custom_call_target="tpu_custom_call" | custom-call | tf_op jit(solution)/shard_map/update/pallas_call | solution.py:638
  93.1 1.3 %collective-permute-start.11 = (bf16[128,512]{1,0:T(8,128)(2,1)S(1)}, bf16[128,512]{1,0:T(8,128)(2,1)S(1)}, u32[]{:S(2)}, u32[]{:S(2)}) collective-permute-start(bf16[128,512]{1,0:T(8,128)(2,1)S(1)} %get-tuple-element.46), channel_id=1, source_target_pairs={{0,4},{4,8},{8,12},{1,5},{5,9},{9,13},{2,6},{6,10},{10,14},{3,7},{... | collective-permute-start | bytes 393224 | tf_op jit(solution)/shard_map/ppermute | solution.py:678
  94.4 4.6 %collective-permute-start.12 = (bf16[128,512]{1,0:T(8,128)(2,1)S(1)}, bf16[128,512]{1,0:T(8,128)(2,1)S(1)}, u32[]{:S(2)}, u32[]{:S(2)}) collective-permute-start(bf16[128,512]{1,0:T(8,128)(2,1)S(1)} %get-tuple-element.47), channel_id=1, source_target_pairs={{4,0},{8,4},{12,8},{5,1},{9,5},{13,9},{6,2},{10,6},{14,10},{7,3},{... | collective-permute-start | bytes 393224 | tf_op jit(solution)/shard_map/ppermute | solution.py:679
  99.0 3.7 %copy-done.1 = bf16[2,3,3,512,512]{4,3,2,1,0:T(8,128)(2,1)S(1)} copy-done((bf16[2,3,3,512,512]{4,3,2,1,0:T(8,128)(2,1)S(1)}, bf16[2,3,3,512,512]{4,3,2,1,0:T(8,128)(2,1)}, u32[]{:S(2)}) %copy-start.1) | copy-done | bytes 9437208
  102.7 6.0 %conv_inside.2 = (bf16[16,128,512]{2,1,0:T(8,128)(2,1)}, f32[128,512]{1,0:T(8,128)S(1)}, f32[2,8,16,512]{3,2,1,0:T(8,128)S(1)}, f32[8,128]{1,0:T(8,128)S(1)}) custom-call(bf16[16,128,512]{2,1,0:T(8,128)(2,1)S(1)} %get-tuple-element.39.refs_0_.refs_1_, s32[16,256]{1,0:T(8,128)S(1)} %copy-done.12, bf16[2,3,3,512,512]{4,3,2,1,0:T(8,128)(2,1)S(1)} %copy-done.1, ...), custom_call_target="tpu_custom_call" | custom-call | flops 4831838208 | bytes 3145728 | tf_op jit(solution)/shard_map/conv_inside/pallas_call | solution.py:447
  108.7 0.5 slice.17
  109.2 0.6 maximum_add_fusion
  109.9 0.4 collective-permute-start.13
  110.2 0.6 maximum_add_fusion.1
  110.9 1.5 %collective-permute-start.14 = (f32[18,512]{1,0:T(8,128)S(1)}, f32[18,512]{1,0:T(8,128)S(1)}, u32[]{:S(2)}, u32[]{:S(2)}) collective-permute-start(f32[18,512]{1,0:T(8,128)S(1)} %maximum_add_fusion.1), channel_id=1, source_target_pairs={{1,0},{2,1},{3,2},{0,3},{5,4},{6,5},{7,6},{4,7},{9,8},{10,9},{11,1... | collective-permute-start | bytes 110600 | tf_op jit(solution)/shard_map/ppermute | solution.py:686
  112.4 6.7 %conv_inside.3 = (bf16[16,128,512]{2,1,0:T(8,128)(2,1)}, f32[128,512]{1,0:T(8,128)S(1)}, f32[2,8,16,512]{3,2,1,0:T(8,128)S(1)}, f32[8,128]{1,0:T(8,128)}) custom-call(bf16[16,128,512]{2,1,0:T(8,128)(2,1)} %get-tuple-element.40.refs_0_, bf16[16,128,512]{2,1,0:T(8,128)(2,1)S(1)} %get-tuple-element.39.refs_0_.refs_1_, ...), custom_call_target="tpu_custom_call", output_to_operand_aliasing={{0}: (0, {})} | custom-call | flops 4831838208 | bytes 3145728 | tf_op jit(solution)/shard_map/conv_inside/pallas_call | solution.py:447
  119.0 1.8 %fix_edges.1 = bf16[16,128,512]{2,1,0:T(8,128)(2,1)} custom-call(bf16[16,128,512]{2,1,0:T(8,128)(2,1)} %get-tuple-element.41.out_in_hbm, f32[128,512]{1,0:T(8,128)S(1)} %get-tuple-element.42.first_ref, f32[128,512]{1,0:T(8,128)S(1)} %get-tuple-element.43.last_ref, f32[2,8,16,512]{3,2,1,0:T(8,128)S(1)} %get-tuple-element.44.upper_ref, ...), custom_call_target="tpu_custom_call", output_to_operand_aliasing={{}: (0, {})} | custom-call | tf_op jit(solution)/shard_map/fix_edges/pallas_call | solution.py:537
  (45 shorter events, 0.1 us)
Async XLA Ops:
  0.7 1.6 %copy-start.5 = (bf16[1,16,128,512]{3,2,1,0:T(8,128)(2,1)S(1)}, bf16[1,16,128,512]{3,2,1,0:T(8,128)(2,1)}, u32[]{:S(2)}) copy-start(bf16[1,16,128,512]{3,2,1,0:T(8,128)(2,1)} %param.8) | copy-start | bytes 6291460
  2.3 1.0 copy-start.8
  3.3 0.9 copy-start.9
  4.3 0.7 copy-start.11
  10.4 56.6 %copy-start.4 = (bf16[2,3,3,256,256]{4,3,2,1,0:T(8,128)(2,1)S(1)}, bf16[2,3,3,256,256]{4,3,2,1,0:T(8,128)(2,1)}, u32[]{:S(2)}) copy-start(bf16[2,3,3,256,256]{4,3,2,1,0:T(8,128)(2,1)} %sea_ref.3) | copy-start | bytes 7077892
  10.4 41.2 %all-to-all-start.1 = ((bf16[32,64,256]{2,1,0:T(8,128)(2,1)}), bf16[32,64,256]{2,1,0:T(8,128)(2,1)}, u32[]{:S(2)}, u32[]{:S(2)}) async-start(bf16[32,64,256]{2,1,0:T(8,128)(2,1)} %get-tuple-element.36), calls=%async_computation.1 | async-start | bytes 2097152 | tf_op jit(solution)/shard_map/all_to_all | solution.py:663
  16.6 7.9 %collective-permute-start = (s32[3,16]{1,0:T(4,128)S(1)}, s32[3,16]{1,0:T(4,128)S(1)}, u32[]{:S(2)}, u32[]{:S(2)}) collective-permute-start(s32[3,16]{1,0:T(4,128)S(1)} %get-tuple-element.28), channel_id=1, source_target_pairs={{0,16},{16,0},{1,17},{17,1},{2,18},{18,2},{3,19},{19,3},{4,20},{20... | collective-permute-start | bytes 584 | tf_op jit(solution)/shard_map/ppermute | solution.py:655
  17.4 27.0 %collective-permute-start.6 = (bf16[128,512]{1,0:T(8,128)(2,1)S(1)}, bf16[128,512]{1,0:T(8,128)(2,1)S(1)}, u32[]{:S(2)}, u32[]{:S(2)}) collective-permute-start(bf16[128,512]{1,0:T(8,128)(2,1)S(1)} %get-tuple-element.30), channel_id=1, source_target_pairs={{0,4},{4,8},{8,12},{1,5},{5,9},{9,13},{2,6},{6,10},{10,14},{3,7},{... | collective-permute-start | bytes 393224 | tf_op jit(solution)/shard_map/ppermute | solution.py:678
  18.7 25.7 %collective-permute-start.7 = (bf16[128,512]{1,0:T(8,128)(2,1)S(1)}, bf16[128,512]{1,0:T(8,128)(2,1)S(1)}, u32[]{:S(2)}, u32[]{:S(2)}) collective-permute-start(bf16[128,512]{1,0:T(8,128)(2,1)S(1)} %get-tuple-element.31), channel_id=1, source_target_pairs={{4,0},{8,4},{12,8},{5,1},{9,5},{13,9},{6,2},{10,6},{14,10},{7,3},{... | collective-permute-start | bytes 393224 | tf_op jit(solution)/shard_map/ppermute | solution.py:679
  23.3 21.2 %collective-permute-start.5 = (bf16[16,64,256]{2,1,0:T(8,128)(2,1)S(1)}, bf16[16,64,256]{2,1,0:T(8,128)(2,1)S(1)}, u32[]{:S(2)}, u32[]{:S(2)}) collective-permute-start(bf16[16,64,256]{2,1,0:T(8,128)(2,1)S(1)} %get-tuple-element.29), channel_id=1, source_target_pairs={{0,16},{16,0},{1,17},{17,1},{2,18},{18,2},{3,19},{19,3},{4,20},{20... | collective-permute-start | bytes 1572872 | tf_op jit(solution)/shard_map/ppermute | solution.py:655
  24.5 1.2 collective-permute-start.1
  25.7 3.6 %collective-permute-start.2 = (s32[2,3,16]{2,1,0:T(4,128)S(1)}, s32[2,3,16]{2,1,0:T(4,128)S(1)}, u32[]{:S(2)}, u32[]{:S(2)}) collective-permute-start(s32[2,3,16]{2,1,0:T(4,128)S(1)} %pad_add_fusion.2), channel_id=1, source_target_pairs={{0,2},{1,3},{2,0},{3,1},{4,6},{5,7},{6,4},{7,5},{8,10},{9,11},{10,... | collective-permute-start | bytes 1160 | tf_op jit(solution)/shard_map/ppermute | solution.py:655
  29.3 8.0 %collective-permute-start.3 = (s32[4,3,16]{2,1,0:T(4,128)S(1)}, s32[4,3,16]{2,1,0:T(4,128)S(1)}, u32[]{:S(2)}, u32[]{:S(2)}) collective-permute-start(s32[4,3,16]{2,1,0:T(4,128)S(1)} %pad_add_fusion.1), channel_id=1, source_target_pairs={{0,4},{4,0},{8,12},{12,8},{1,5},{5,1},{9,13},{13,9},{2,6},{6,2},{1... | collective-permute-start | bytes 2312 | tf_op jit(solution)/shard_map/ppermute | solution.py:655
  37.3 7.1 %collective-permute-start.4 = (s32[8,3,16]{2,1,0:T(4,128)S(1)}, s32[8,3,16]{2,1,0:T(4,128)S(1)}, u32[]{:S(2)}, u32[]{:S(2)}) collective-permute-start(s32[8,3,16]{2,1,0:T(4,128)S(1)} %pad_add_fusion), channel_id=1, source_target_pairs={{0,8},{4,12},{8,0},{12,4},{1,9},{5,13},{9,1},{13,5},{2,10},{6,14},... | collective-permute-start | bytes 4616 | tf_op jit(solution)/shard_map/ppermute | solution.py:655
  48.1 1.0 copy-start.7
  49.1 0.7 copy-start.13
  49.8 0.6 copy-start.15
  50.4 0.6 copy-start.17
  51.0 0.6 copy-start.18
  51.6 33.9 %all-to-all-start = ((bf16[32,64,256]{2,1,0:T(8,128)(2,1)}), bf16[32,64,256]{2,1,0:T(8,128)(2,1)S(1)}, u32[]{:S(2)}, u32[]{:S(2)}) async-start(bf16[32,64,256]{2,1,0:T(8,128)(2,1)} %copy-done.7), calls=%async_computation | async-start | bytes 2097152 | tf_op jit(solution)/shard_map/all_to_all | solution.py:663
  57.6 27.9 %collective-permute-start.8 = (bf16[32,64,256]{2,1,0:T(8,128)(2,1)}, bf16[32,64,256]{2,1,0:T(8,128)(2,1)}, u32[]{:S(2)}, u32[]{:S(2)}) collective-permute-start(bf16[32,64,256]{2,1,0:T(8,128)(2,1)} %all-to-all-done.1), channel_id=1, source_target_pairs={{0,16},{16,0},{1,17},{17,1},{2,18},{18,2},{3,19},{19,3},{4,20},{20... | collective-permute-start | bytes 3145736 | tf_op jit(solution)/shard_map/ppermute | solution.py:655
  58.5 8.5 %collective-permute-start.9 = (f32[18,512]{1,0:T(8,128)}, f32[18,512]{1,0:T(8,128)S(1)}, u32[]{:S(2)}, u32[]{:S(2)}) collective-permute-start(f32[18,512]{1,0:T(8,128)} %copy-done.18), channel_id=1, source_target_pairs={{0,1},{1,2},{2,3},{3,0},{4,5},{5,6},{6,7},{7,4},{8,9},{9,10},{10,1... | collective-permute-start | bytes 110600 | tf_op jit(solution)/shard_map/ppermute | solution.py:685
  58.5 8.5 %collective-permute-start.10 = (f32[18,512]{1,0:T(8,128)}, f32[18,512]{1,0:T(8,128)S(1)}, u32[]{:S(2)}, u32[]{:S(2)}) collective-permute-start(f32[18,512]{1,0:T(8,128)} %copy-done.17), channel_id=1, source_target_pairs={{1,0},{2,1},{3,2},{0,3},{5,4},{6,5},{7,6},{4,7},{9,8},{10,9},{11,1... | collective-permute-start | bytes 110600 | tf_op jit(solution)/shard_map/ppermute | solution.py:686
  67.0 3.7 %copy-start = (bf16[2,3,3,512,512]{4,3,2,1,0:T(8,128)(2,1)S(1)}, bf16[2,3,3,512,512]{4,3,2,1,0:T(8,128)(2,1)}, u32[]{:S(2)}) copy-start(bf16[2,3,3,512,512]{4,3,2,1,0:T(8,128)(2,1)} %air_ref.3) | copy-start | bytes 28311556
  70.7 1.6 %copy-start.6 = (bf16[1,16,128,512]{3,2,1,0:T(8,128)(2,1)S(1)}, bf16[1,16,128,512]{3,2,1,0:T(8,128)(2,1)}, u32[]{:S(2)}) copy-start(bf16[1,16,128,512]{3,2,1,0:T(8,128)(2,1)} %param.8) | copy-start | bytes 6291460
  72.3 0.9 copy-start.14
  73.2 12.4 %copy-start.12 = (s32[16,256]{1,0:T(8,128)S(1)}, s32[16,256]{1,0:T(8,128)}, u32[]{:S(2)}) copy-start(s32[16,256]{1,0:T(8,128)} %water_ref.5) | copy-start | bytes 49156
  83.5 2.0 %copy-start.2 = (f32[16,128,512]{2,1,0:T(8,128)}, f32[16,128,512]{2,1,0:T(8,128)S(1)}, u32[]{:S(2)}) copy-start(f32[16,128,512]{2,1,0:T(8,128)S(1)} %conv_halo.1.sum_ref) | copy-start | bytes 12582916
  85.5 2.2 %copy-start.3 = (f32[16,128,512]{2,1,0:T(8,128)S(1)}, f32[16,128,512]{2,1,0:T(8,128)}, u32[]{:S(2)}) copy-start(f32[16,128,512]{2,1,0:T(8,128)} %copy-done.2) | copy-start | bytes 12582916
  87.7 0.9 copy-start.10
  88.7 0.7 copy-start.16
  93.1 16.1 %collective-permute-start.11 = (bf16[128,512]{1,0:T(8,128)(2,1)S(1)}, bf16[128,512]{1,0:T(8,128)(2,1)S(1)}, u32[]{:S(2)}, u32[]{:S(2)}) collective-permute-start(bf16[128,512]{1,0:T(8,128)(2,1)S(1)} %get-tuple-element.46), channel_id=1, source_target_pairs={{0,4},{4,8},{8,12},{1,5},{5,9},{9,13},{2,6},{6,10},{10,14},{3,7},{... | collective-permute-start | bytes 393224 | tf_op jit(solution)/shard_map/ppermute | solution.py:678
  94.4 14.8 %collective-permute-start.12 = (bf16[128,512]{1,0:T(8,128)(2,1)S(1)}, bf16[128,512]{1,0:T(8,128)(2,1)S(1)}, u32[]{:S(2)}, u32[]{:S(2)}) collective-permute-start(bf16[128,512]{1,0:T(8,128)(2,1)S(1)} %get-tuple-element.47), channel_id=1, source_target_pairs={{4,0},{8,4},{12,8},{5,1},{9,5},{13,9},{6,2},{10,6},{14,10},{7,3},{... | collective-permute-start | bytes 393224 | tf_op jit(solution)/shard_map/ppermute | solution.py:679
  99.0 3.7 %copy-start.1 = (bf16[2,3,3,512,512]{4,3,2,1,0:T(8,128)(2,1)S(1)}, bf16[2,3,3,512,512]{4,3,2,1,0:T(8,128)(2,1)}, u32[]{:S(2)}) copy-start(bf16[2,3,3,512,512]{4,3,2,1,0:T(8,128)(2,1)} %air_ref.3) | copy-start | bytes 28311556
  109.9 9.1 %collective-permute-start.13 = (f32[18,512]{1,0:T(8,128)S(1)}, f32[18,512]{1,0:T(8,128)S(1)}, u32[]{:S(2)}, u32[]{:S(2)}) collective-permute-start(f32[18,512]{1,0:T(8,128)S(1)} %maximum_add_fusion), channel_id=1, source_target_pairs={{0,1},{1,2},{2,3},{3,0},{4,5},{5,6},{6,7},{7,4},{8,9},{9,10},{10,1... | collective-permute-start | bytes 110600 | tf_op jit(solution)/shard_map/ppermute | solution.py:685
  110.9 8.2 %collective-permute-start.14 = (f32[18,512]{1,0:T(8,128)S(1)}, f32[18,512]{1,0:T(8,128)S(1)}, u32[]{:S(2)}, u32[]{:S(2)}) collective-permute-start(f32[18,512]{1,0:T(8,128)S(1)} %maximum_add_fusion.1), channel_id=1, source_target_pairs={{1,0},{2,1},{3,2},{0,3},{5,4},{6,5},{7,6},{4,7},{9,8},{10,9},{11,1... | collective-permute-start | bytes 110600 | tf_op jit(solution)/shard_map/ppermute | solution.py:686

commit v2 on v1

v2 whole, which is shorter than its diff:
```python
import functools

import jax
import jax.numpy as jnp
from jax import lax
from jax.experimental import pallas as pl
from jax.experimental.pallas import tpu as pltpu
from jax.sharding import PartitionSpec as P

BLOCK_ROWS = 8
BLOCK_COLS = 16
BLOCK = BLOCK_ROWS * BLOCK_COLS
SLOTS = 2
FIRST = (1, 2, 3, 4, 5, 6)
SECOND = (0, 7)
FIRST_CELLS = len(FIRST) * BLOCK_COLS
SECOND_CELLS = len(SECOND) * BLOCK_COLS
LABEL_ROWS = 16
LANES = 128
VMEM_BYTES = 62 * 2**20
LATE_BYTES = 36 * 2**20
UPDATE_BYTES = 36 * 2**20

F32 = jnp.float32
BF16 = jnp.bfloat16

VMEM = pl.BlockSpec(memory_space=pltpu.VMEM)
SMEM = pl.BlockSpec(memory_space=pltpu.SMEM)
HBM = pl.BlockSpec(memory_space=pltpu.HBM)


def silu(v):
    h = 0.5 * v
    return h + h * jnp.tanh(h)


def iota(shape, dim):
    return lax.broadcasted_iota(jnp.int32, shape, dim)


def dot(a, b):
    return jnp.dot(a, b, preferred_element_type=F32)


def params(limit=VMEM_BYTES):
    return pltpu.CompilerParams(vmem_limit_bytes=limit)


def on_ocean():
    return lax.axis_index("grp") == 1


def fill_water(water_ref, wide_ref, turned_ref):
    rows, longitudes = water_ref.shape
    wide_ref[:, 0:rows] = water_ref[...].astype(F32).T
    for p in range(2):
        turned_ref[:, p * rows : (p + 1) * rows] = wide_ref[pl.ds(p, longitudes // 2, stride=2), :][:, 0:rows]


def water_scratch(cols):
    return [pltpu.VMEM((2 * cols, 128), F32), pltpu.VMEM((cols, 128), F32)]


def water_of_row(turned_ref, rows, r, width, start, size):
    parts = [
        jnp.broadcast_to(turned_ref[start : start + size, p * rows + r : p * rows + r + 1], (size, width))
        for p in range(2)
    ]
    return jnp.concatenate(parts, axis=1)


def rim_shapes(rows, cols, width):
    line = jax.ShapeDtypeStruct((cols, width), BF16)
    side = jax.ShapeDtypeStruct((rows, width), F32)
    return (line, line, side, side)


def put_rim(rim, r, rows, line):
    top_ref, bottom_ref, left_ref, right_ref = rim
    cols = line.shape[0]
    exact = line.astype(F32)
    left_ref[r : r + 1] = exact[0:1]
    right_ref[r : r + 1] = exact[cols - 1 : cols]
    if r == 0:
        top_ref[...] = line
    if r == rows - 1:
        bottom_ref[...] = line


def payload_kernel(
    lists_in, state_hbm, matrices_hbm, water_ref, flux_hbm,
    first_ref, second_ref, lists_out, top_ref, bottom_ref, left_ref, right_ref,
    state_ref, matrices_ref, flux_ref, flux, surface, wide_water, turned, count, sems,
):
    rows, cols, width = state_ref.shape
    half = width // 2
    entries = matrices_ref.shape[0]
    tiles = second_ref.shape[0]
    ocean = on_ocean()
    pieces = 4
    step = rows // pieces
    flux_copy = pltpu.make_async_copy(flux_hbm, flux_ref, sems.at[pieces])
    matrices_copy = pltpu.make_async_copy(matrices_hbm, matrices_ref, sems.at[pieces + 1])
    state_copies = [
        pltpu.make_async_copy(state_hbm.at[pl.ds(k * step, step)], state_ref.at[pl.ds(k * step, step)], sems.at[k])
        for k in range(pieces)
    ]
    lists_ref = lists_in.at[0, 0, 0]
    flux_copy.start()
    for copy in state_copies:
        copy.start()
    matrices_copy.start()

    def clear(t, _):
        count[t] = 0
        return 0

    lax.fori_loop(0, tiles, clear, 0)

    def keep(e, _):
        for k in range(3):
            lists_out[k, e] = lists_ref[k, e]
        return 0

    lax.fori_loop(0, entries, keep, 0)
    second_ref[:, SLOTS * SECOND_CELLS :, :] = jnp.full((tiles, LABEL_ROWS, half), -1.0, BF16)
    i = iota((BLOCK, BLOCK), 0)
    j = iota((BLOCK, BLOCK), 1)

    def put(e, payload, cut):
        owner = lists_ref[0, e]
        rank = count[owner]
        count[owner] = rank + 1
        first_ref[e], second = cut(payload)
        at = pl.multiple_of(rank * SECOND_CELLS, BLOCK_COLS)
        second_ref[owner, pl.ds(at, SECOND_CELLS), :] = second
        label = jnp.full((LABEL_ROWS, LANES), lists_ref[2, e], jnp.int32).astype(F32).astype(BF16)
        second_ref[owner, SLOTS * SECOND_CELLS :, pl.ds(pl.multiple_of(rank * LANES, LANES), LANES)] = label

    flux_copy.wait()

    @pl.when(jnp.logical_not(ocean))
    def _():
        wide = BLOCK_COLS // 2
        c = i % wide
        p1, r1 = i // (FIRST_CELLS // 2), FIRST[0] + i % (FIRST_CELLS // 2) // wide
        k = i - FIRST_CELLS
        q = k % (SECOND_CELLS // 2) // wide
        p2, r2 = k // (SECOND_CELLS // 2), jnp.where(q == 0, 0, q + FIRST[-1])
        p, r = jnp.where(k < 0, p1, p2), jnp.where(k < 0, r1, r2)
        turn = (j == r * BLOCK_COLS + 2 * c + p).astype(BF16)
        for k in range(pieces):
            state_copies[k].wait()
            block = state_ref[k * step : (k + 1) * step].reshape(step * cols, width)
            flux[k * step : (k + 1) * step] = (
                dot(block, flux_ref[...]).astype(BF16).reshape(step, cols, half)
            )
        matrices_copy.wait()
        across = cols // BLOCK_COLS

        def entry(e, _):
            source = lists_ref[1, e]
            r0 = (source // across) * BLOCK_ROWS
            c0 = pl.multiple_of((source % across) * BLOCK_COLS, BLOCK_COLS)
            chosen = flux[pl.ds(r0, BLOCK_ROWS), pl.ds(c0, BLOCK_COLS), :].reshape(BLOCK, half)
            weight = dot(turn, matrices_ref[e]).astype(BF16)
            put(e, dot(weight, chosen).astype(BF16), lambda v: (v[:FIRST_CELLS], v[FIRST_CELLS:]))
            return 0

        lax.fori_loop(0, entries, entry, 0, unroll=8)

    @pl.when(ocean)
    def _():
        p, r, c = j // 64, (j // 8) % 8, j % 8
        turn = (i == r * BLOCK_COLS + 2 * c + p).astype(BF16)
        fill_water(water_ref, wide_water, turned)
        for k in range(pieces):
            state_copies[k].wait()
            for r0 in range(k * step, (k + 1) * step):
                surface[r0] = state_ref[r0].astype(F32) * water_of_row(turned, rows, r0, half, 0, cols)
        matrices_copy.wait()
        wide = BLOCK_COLS // 2
        across = cols // wide

        def entry(e, _):
            source = lists_ref[1, e]
            r0 = (source // across) * BLOCK_ROWS
            c0 = pl.multiple_of((source % across) * wide, wide)
            block = surface[pl.ds(r0, BLOCK_ROWS), pl.ds(c0, wide), :]
            chosen = jnp.concatenate(
                [block[:, :, q * half : (q + 1) * half].reshape(BLOCK // 2, half) for q in range(2)], axis=0
            ).astype(BF16)
            weight = dot(matrices_ref[e], turn).astype(BF16)
            low, high = BLOCK_COLS, BLOCK_COLS + FIRST_CELLS
            put(
                e,
                dot(weight, chosen).astype(BF16),
                lambda v: (v[low:high], jnp.concatenate([v[:low], v[high:]], axis=0)),
            )
            return 0

        lax.fori_loop(0, entries, entry, 0, unroll=8)

    for r in range(rows):
        put_rim((top_ref, bottom_ref, left_ref, right_ref), r, rows, state_ref[r])


def payloads(lists, state, matrices, water, flux_projection, tiles):
    rows, cols, width = state.shape
    half = width // 2
    entries = lists.shape[-1]
    return pl.pallas_call(
        payload_kernel,
        out_shape=(
            jax.ShapeDtypeStruct((entries, FIRST_CELLS, half), BF16),
            jax.ShapeDtypeStruct((tiles, SLOTS * SECOND_CELLS + LABEL_ROWS, half), BF16),
            jax.ShapeDtypeStruct((3, entries), jnp.int32),
        )
        + rim_shapes(rows, cols, width),
        in_specs=[SMEM, HBM, HBM, VMEM, HBM],
        out_specs=(VMEM, VMEM, SMEM) + (VMEM,) * 4,
        scratch_shapes=[
            pltpu.VMEM(state.shape, BF16),
            pltpu.VMEM(matrices.shape, BF16),
            pltpu.VMEM(flux_projection.shape, BF16),
            pltpu.VMEM((rows, cols, half), BF16),
            pltpu.VMEM((rows, cols, width), F32),
        ]
        + water_scratch(cols)
        + [
            pltpu.SMEM((tiles,), jnp.int32),
            pltpu.SemaphoreType.DMA((6,)),
        ],
        compiler_params=params(),
        name="payload",
    )(lists, state, matrices, water, flux_projection)


def pack_kernel(
    lists_ref, dense_ref, above_ref, below_ref, left_ref, right_ref, token_ref, slots_ref, west_ref, east_ref, count
):
    entries = lists_ref.shape[1]
    tiles = slots_ref.shape[0]

    def clear(t, _):
        count[t] = 0
        return 0

    lax.fori_loop(0, tiles, clear, 0)

    def place(e, _):
        owner = lists_ref[0, e]
        rank = count[owner]
        count[owner] = rank + 1
        at = pl.multiple_of(rank * FIRST_CELLS, BLOCK_COLS)
        slots_ref[owner, pl.ds(at, FIRST_CELLS), :] = dense_ref[e]
        return 0

    lax.fori_loop(0, entries, place, 0, unroll=4)
    del token_ref
    put_sides(above_ref, below_ref, left_ref, right_ref, west_ref, east_ref)


def pack(tiles, lists, dense, above, below, left, right, token):
    rows, width = left.shape
    side = jax.ShapeDtypeStruct((rows + 2, width), F32)
    return pl.pallas_call(
        pack_kernel,
        out_shape=(jax.ShapeDtypeStruct((tiles, SLOTS * FIRST_CELLS, dense.shape[2]), BF16), side, side),
        in_specs=[SMEM] + [VMEM] * 5 + [HBM],
        out_specs=(VMEM,) * 3,
        scratch_shapes=[pltpu.SMEM((tiles,), jnp.int32)],
        compiler_params=params(),
        name="pack",
    )(lists, dense, above, below, left, right, token)


def put_sides(above_ref, below_ref, left_ref, right_ref, west_ref, east_ref):
    rows = left_ref.shape[0]
    cols = above_ref.shape[0]
    for ref, side, at in ((west_ref, left_ref, 0), (east_ref, right_ref, cols - 1)):
        ref[0:1] = above_ref[at : at + 1].astype(F32)
        ref[1 : rows + 1] = side[...]
        ref[rows + 1 : rows + 2] = below_ref[at : at + 1].astype(F32)


def slot_labels(second):
    return second[:, SLOTS * SECOND_CELLS, ::LANES][:, :SLOTS].astype(jnp.int32).reshape(-1)


GROUP = 4


TILE = 8


def set_columns(line, before, after):
    cols = line.shape[0]
    left, right = pltpu.roll(line, 1, 0), pltpu.roll(line, cols - 1, 0)
    at = iota((TILE, line.shape[1]), 0)
    head = jnp.where(at == 0, before, left[:TILE])
    tail = jnp.where(at == TILE - 1, after, right[cols - TILE :])
    left = jnp.concatenate([head, left[TILE:]], axis=0)
    right = jnp.concatenate([right[: cols - TILE], tail], axis=0)
    return left, right


def air_line(h, before, after):
    left, right = set_columns(h, before, after)
    return jnp.concatenate([left, h, right], axis=1).astype(BF16)


def sea_line(h, before, after):
    half = h.shape[1] // 2
    left, _ = set_columns(h[:, half:], before[:, half:], after[:, half:])
    _, right = set_columns(h[:, :half], before[:, :half], after[:, :half])
    return jnp.concatenate([left, h, right], axis=1).astype(BF16)


def air_product(block, kernel):
    return dot(block, kernel.reshape(-1, kernel.shape[-1]))


def sea_product(block, kernel):
    width = kernel.shape[-1]
    flat = kernel.reshape(-1, width)
    return jnp.concatenate(
        [dot(block[:, : 3 * width], flat), dot(block[:, width : 4 * width], flat)], axis=1
    )


def each_component(run, air, sea):
    ocean = on_ocean()

    @pl.when(jnp.logical_not(ocean))
    def _():
        run(air, air_line, air_product, False)

    @pl.when(ocean)
    def _():
        run(sea, sea_line, sea_product, True)


def held_weights(air_kernels):
    return [pltpu.VMEM(air_kernels.shape[1:], BF16), pltpu.SemaphoreType.DMA((3, 3))]


def fetch_weights(layer, kernels_hbm, held, sems, wanted):
    width = kernels_hbm.shape[-1]
    copies = {
        (d, c): pltpu.make_async_copy(
            kernels_hbm.at[layer, d, c], held.at[d, c, pl.ds(0, width), pl.ds(0, width)], sems.at[d, c]
        )
        for d, c in wanted
    }
    for copy in copies.values():
        copy.start()
    return copies


def inside_conv_kernel(layer, begin, end, keep, *refs):
    x_hbm, _, air_hbm, sea_hbm, out_hbm, last_out = refs[:6]
    x_ref, lined, out, held, weight_sems, x_sems, sems = refs[6:13]
    rows, cols, width = x_hbm.shape
    low, high = max(begin - 1, 0), min(end + 1, rows)
    groups = (end - begin) // GROUP
    early = begin + GROUP + 1
    spans = [(low, early), (early, high)]
    every = [(d, c) for d in range(3) for c in range(3)]
    kept_write = None
    if keep:
        kept, kept_sems, kept_sem = refs[13:]
        kept_write = pltpu.make_async_copy(kept, last_out, kept_sem)
    else:
        last_out[...] = jnp.zeros_like(last_out)

    def read(k):
        at = pl.ds(spans[k][0], spans[k][1] - spans[k][0])
        return pltpu.make_async_copy(x_hbm.at[at], x_ref.at[at], x_sems.at[k])

    def write(g):
        at = g * GROUP
        return pltpu.make_async_copy(
            out.at[pl.ds(at, GROUP)], out_hbm.at[pl.ds(begin + at, GROUP)], sems.at[g]
        )

    def run(kernels_hbm, make_line, product, masked):
        wide = (2 if masked else 3) * width
        size = width // 2 if masked else width
        none = jnp.zeros((1, width), F32)
        read(0).start()
        weights = fetch_weights(layer, kernels_hbm, held, weight_sems, every)
        read(1).start()
        later = fetch_weights(layer + 1, kernels_hbm, kept, kept_sems, every) if keep else {}

        def put(r):
            if 0 <= r < rows:
                line = make_line(silu(x_ref[r].astype(F32)), none, none)
            else:
                line = jnp.zeros((cols, wide), BF16)
            lined[r - begin + 1, :, 0:wide] = line

        read(0).wait()
        for r in range(begin - 1, early):
            put(r)
        for copy in weights.values():
            copy.wait()
        read(1).wait()
        for g in range(groups):
            r0 = begin + g * GROUP
            total = x_ref[r0 : r0 + GROUP].astype(F32).reshape(GROUP * cols, width)
            for d in range(3):
                at = r0 - begin + d
                block = lined[at : at + GROUP, :, 0:wide].reshape(GROUP * cols, wide)
                total = total + product(block, held[d, :, 0:size, 0:size])
            if g + 1 < groups:
                for r in range(r0 + GROUP + 1, r0 + 2 * GROUP + 1):
                    put(r)
            out[r0 - begin : r0 - begin + GROUP] = total.reshape(GROUP, cols, width)
            write(g).start()
            if keep and g == 0:
                for copy in later.values():
                    copy.wait()
                kept_write.start()

    each_component(run, air_hbm, sea_hbm)
    for g in range(groups):
        write(g).wait()
    if keep:
        kept_write.wait()


def last_conv_kernel(
    x_ref, above_ref, below_ref, water_ref, held, out_hbm, sides_ref, lined, out, wide_water, turned, sems
):
    rows, cols, width = x_ref.shape
    half = width // 2
    groups = rows // GROUP

    def write(g):
        at = pl.ds(g * GROUP, GROUP)
        return pltpu.make_async_copy(out.at[at], out_hbm.at[at], sems.at[g])

    def run(_, make_line, product, masked):
        wide = (2 if masked else 3) * width
        size = half if masked else width
        none = jnp.zeros((1, width), F32)

        def put(r):
            line = above_ref[...] if r < 0 else below_ref[...] if r == rows else x_ref[r]
            lined[r + 1, :, 0:wide] = make_line(silu(line.astype(F32)), none, none)

        if masked:
            fill_water(water_ref, wide_water, turned)
        for r in range(-1, GROUP + 1):
            put(r)
        for g in range(groups):
            r0 = g * GROUP
            total = x_ref[r0 : r0 + GROUP].astype(F32).reshape(GROUP * cols, width)
            for d in range(3):
                block = lined[r0 + d : r0 + d + GROUP, :, 0:wide].reshape(GROUP * cols, wide)
                total = total + product(block, held[d, :, 0:size, 0:size])
            if g + 1 < groups:
                for r in range(r0 + GROUP + 1, r0 + 2 * GROUP + 1):
                    put(r)
            total = total.reshape(GROUP, cols, width)
            for k in range(GROUP):
                r = r0 + k
                line = total[k]
                sides_ref[0, r] = line[:BLOCK_COLS]
                sides_ref[1, r] = line[cols - BLOCK_COLS :]
                if masked:
                    line = line * water_of_row(turned, rows, r, half, 0, cols)
                out[r] = line.astype(BF16)
            write(g).start()

    each_component(run, None, None)
    for g in range(groups):
        write(g).wait()


def last_conv(state, above, below, water, held):
    rows, cols, width = state.shape
    return pl.pallas_call(
        last_conv_kernel,
        out_shape=(
            jax.ShapeDtypeStruct(state.shape, BF16),
            jax.ShapeDtypeStruct((2, rows, BLOCK_COLS, width), F32),
        ),
        in_specs=[VMEM] * 5,
        out_specs=(HBM, VMEM),
        scratch_shapes=[
            pltpu.VMEM((rows + 2, cols, 3 * width), BF16),
            pltpu.VMEM((rows, cols, width), BF16),
        ]
        + water_scratch(cols)
        + [pltpu.SemaphoreType.DMA((rows // GROUP,))],
        compiler_params=params(LATE_BYTES),
        cost_estimate=conv_cost(state, rows),
        name="last_conv",
    )(state, above, below, water, held)


def conv_cost(state, rows):
    cells = rows * state.shape[1]
    width = state.shape[2]
    return pl.CostEstimate(
        flops=2 * 9 * cells * width * width,
        bytes_accessed=cells * width * 6 + 9 * width * width * 2,
        transcendentals=cells * width,
    )


def conv_inside(layer, begin, end, state, after, air_kernels, sea_kernels, keep):
    rows, cols, width = state.shape
    count = end - begin
    kernel_shape = air_kernels.shape[1:]
    scratch = [
        pltpu.VMEM(state.shape, BF16),
        pltpu.VMEM((count + 2, cols, 3 * width), BF16),
        pltpu.VMEM((count, cols, width), F32),
    ] + held_weights(air_kernels)
    scratch += [pltpu.SemaphoreType.DMA((2,)), pltpu.SemaphoreType.DMA((count // GROUP,))]
    if keep:
        scratch += held_weights(air_kernels) + [pltpu.SemaphoreType.DMA]
    return pl.pallas_call(
        functools.partial(inside_conv_kernel, layer, begin, end, keep),
        out_shape=(
            jax.ShapeDtypeStruct(state.shape, F32),
            jax.ShapeDtypeStruct(kernel_shape, BF16) if keep else jax.ShapeDtypeStruct((8, 128), F32),
        ),
        in_specs=[HBM] * 4,
        out_specs=(HBM, HBM if keep else VMEM),
        scratch_shapes=scratch,
        input_output_aliases={1: 0} if keep else {},
        compiler_params=params(),
        cost_estimate=conv_cost(state, count),
        name="conv_inside",
    )(state, after, air_kernels, sea_kernels)


EDGE_WEIGHTS = [(0, 0), (1, 0), (2, 0), (0, 2), (1, 2), (2, 2), (0, 1), (2, 1)]


def halo_columns(rows, left_ref, right_ref, weights, held, masked):
    before = silu(left_ref[...])
    after = silu(right_ref[...])
    half = before.shape[1] // 2
    if masked:
        before, after = before[:, half:], after[:, :half]
    west = jnp.zeros((rows, before.shape[1]), F32)
    east = jnp.zeros((rows, before.shape[1]), F32)
    size = before.shape[1]
    for d in range(3):
        if weights:
            weights[d, 0].wait()
        west = west + dot(before[d : d + rows].astype(BF16), held[d, 0, 0:size, 0:size])
    for d in range(3):
        if weights:
            weights[d, 2].wait()
        east = east + dot(after[d : d + rows].astype(BF16), held[d, 2, 0:size, 0:size])
    if masked:
        blank = jnp.zeros((rows, half), F32)
        west = jnp.concatenate([west, blank], axis=1)
        east = jnp.concatenate([blank, east], axis=1)
    return west, east


def side_kernel(
    out_in_hbm, sides_ref, left_ref, right_ref, water_ref, held, out_hbm, side_out, wide_water, turned, sems,
):
    del out_in_hbm
    rows, cols, width = out_hbm.shape
    half = width // 2
    writes = [
        pltpu.make_async_copy(side_out.at[k], out_hbm.at[:, pl.ds(start, BLOCK_COLS)], sems.at[k])
        for k, start in enumerate((0, cols - BLOCK_COLS))
    ]

    def run(_, make_line, product, masked):
        if masked:
            fill_water(water_ref, wide_water, turned)
        added = halo_columns(rows, left_ref, right_ref, None, held, masked)
        at = iota((BLOCK_COLS, width), 0)
        for k, (start, here) in enumerate(((0, 0), (cols - BLOCK_COLS, BLOCK_COLS - 1))):
            for r in range(rows):
                total = sides_ref[k, r] + jnp.where(at == here, added[k][r : r + 1], 0.0)
                if masked:
                    total = total * water_of_row(turned, rows, r, half, start, BLOCK_COLS)
                side_out[k, r] = total.astype(BF16)
            writes[k].start()

    each_component(run, None, None)
    for copy in writes:
        copy.wait()


def fix_sides(out, sides, beside, water, held):
    rows, cols, width = out.shape
    return pl.pallas_call(
        side_kernel,
        out_shape=jax.ShapeDtypeStruct(out.shape, BF16),
        in_specs=[HBM] + [VMEM] * 5,
        out_specs=HBM,
        scratch_shapes=[pltpu.VMEM((2, rows, BLOCK_COLS, width), BF16)]
        + water_scratch(cols)
        + [pltpu.SemaphoreType.DMA((2,))],
        input_output_aliases={0: 0},
        compiler_params=params(LATE_BYTES),
        name="fix_sides",
    )(out, sides, *beside, water, held)


def edge_copies(rows, cols, count, lines, sides, hbm, sems, inward):
    inner = pl.ds(1, rows - 2)
    pairs = [
        (lines.at[0], hbm.at[0]),
        (lines.at[1], hbm.at[rows - 1]),
        (sides.at[0], hbm.at[inner, pl.ds(0, count)]),
        (sides.at[1], hbm.at[inner, pl.ds(cols - count, count)]),
    ]
    return [
        pltpu.make_async_copy(*(pair[::-1] if inward else pair), sems.at[k]) for k, pair in enumerate(pairs)
    ]


SIDE = 8


def sum_edge_kernel(
    layer, sum_in_hbm, top_ref, bottom_ref, left_ref, right_ref, air_hbm, sea_hbm, sum_hbm,
    lines, sides, held, weight_sems, read_sems, sems,
):
    rows, cols, width = sum_hbm.shape
    reads = edge_copies(rows, cols, SIDE, lines, sides, sum_in_hbm, read_sems, True)
    writes = edge_copies(rows, cols, SIDE, lines, sides, sum_hbm, sems, False)
    for copy in reads:
        copy.start()

    def run(kernels_hbm, make_line, product, masked):
        size = width // 2 if masked else width
        weights = fetch_weights(layer, kernels_hbm, held, weight_sems, EDGE_WEIGHTS)
        none = jnp.zeros((1, width), F32)
        west, east = halo_columns(rows, left_ref, right_ref, weights, held, masked)
        for copy in reads:
            copy.wait()
        at = iota((SIDE, width), 0)
        for r in range(1, rows - 1):
            sides[0, r - 1] += jnp.where(at == 0, west[r : r + 1], 0.0)
            sides[1, r - 1] += jnp.where(at == SIDE - 1, east[r : r + 1], 0.0)
        at = iota((cols, width), 0)
        for k, (line, d) in enumerate(((top_ref, 0), (bottom_ref, 2))):
            r = 0 if k == 0 else rows - 1
            lined = make_line(silu(line[...].astype(F32)), none, none)
            weights[d, 1].wait()
            total = lines[k] + product(lined, held[d, :, 0:size, 0:size])
            total = total + jnp.where(at == 0, west[r : r + 1], 0.0)
            lines[k] = total + jnp.where(at == cols - 1, east[r : r + 1], 0.0)

    each_component(run, air_hbm, sea_hbm)
    for copy in writes:
        copy.start()
    for copy in writes:
        copy.wait()


def add_edges(layer, summed, halo, air_kernels, sea_kernels):
    rows, cols, width = summed.shape
    return pl.pallas_call(
        functools.partial(sum_edge_kernel, layer),
        out_shape=jax.ShapeDtypeStruct(summed.shape, F32),
        in_specs=[HBM] + [VMEM] * 4 + [HBM] * 2,
        out_specs=HBM,
        scratch_shapes=[
            pltpu.VMEM((2, cols, width), F32),
            pltpu.VMEM((2, rows - 2, SIDE, width), F32),
        ]
        + held_weights(air_kernels)
        + [pltpu.SemaphoreType.DMA((4,)), pltpu.SemaphoreType.DMA((4,))],
        input_output_aliases={0: 0},
        compiler_params=params(),
        name="add_edges",
    )(summed, *halo, air_kernels, sea_kernels)


def runs_of(block_rows, rows):
    runs = []
    for r in range(rows):
        if r % BLOCK_ROWS in block_rows:
            if runs and sum(runs[-1]) == r:
                runs[-1] = (runs[-1][0], runs[-1][1] + 1)
            else:
                runs.append((r, 1))
    return runs


def update_kernel(block_rows, last, *refs):
    if last:
        (labels_ref, message_hbm, sum_hbm, water_ref, coupling_hbm, early_new, above_ref, below_ref) = refs[:8]
        (early_left, early_right, new_ref, west_ref, east_ref) = refs[8:13]
        refs = refs[13:]
        left_ref, right_ref, refs = refs[0], refs[1], refs[2:]
    else:
        (labels_ref, message_hbm, sum_hbm, water_ref, coupling_hbm) = refs[:5]
        new_ref, top_ref, bottom_ref = refs[5:8]
        refs = refs[8:]
    (total, message, sum_ref, coupling_ref, wide_water, turned) = refs[:6]
    (message_sem, coupling_sem, sum_sems) = refs[6:]
    rows, cols, width = sum_ref.shape
    half = width // 2
    slots = message_hbm.shape[0] * SLOTS
    cells = len(block_rows) * BLOCK_COLS
    runs = runs_of(block_rows, rows)
    parts = [(start, count, block_rows.index(start)) for start, count in runs_of(block_rows, BLOCK_ROWS)]
    updated = [r for start, count in runs for r in range(start, start + count)]
    ocean = on_ocean()

    def run_copy(source, target, k, sems):
        at = pl.ds(*runs[k])
        return pltpu.make_async_copy(source.at[at], target.at[at], sems.at[k])

    message_copy = pltpu.make_async_copy(message_hbm, message, message_sem)
    coupling_copy = pltpu.make_async_copy(coupling_hbm, coupling_ref, coupling_sem)
    message_copy.start()
    for k in range(len(runs)):
        run_copy(sum_hbm, sum_ref, k, sum_sems).start()
    coupling_copy.start()
    if last:
        at = 0
        for start, count in runs_of([r for r in range(BLOCK_ROWS) if r not in block_rows], rows):
            new_ref[start : start + count] = early_new[at : at + count]
            at += count
        left_ref[...] = early_left[...]
        right_ref[...] = early_right[...]

    def clear(lanes):
        for start, count in runs:
            total[start : start + count, :, 0:lanes] = jnp.zeros((count, cols, lanes), F32)

    def each_slot(act):
        def one(s, _):
            label = labels_ref[s]

            @pl.when(label >= 0)
            def _():
                at = pl.multiple_of((s % SLOTS) * cells, BLOCK_COLS)
                act(message[s // SLOTS, pl.ds(at, cells), :].astype(F32), label)

            return 0

        lax.fori_loop(0, slots, one, 0)

    def store(r, line):
        low = line.astype(BF16)
        new_ref[r if last else updated.index(r)] = low
        if last:
            left_ref[r : r + 1] = low[:TILE].astype(F32)[:1]
            right_ref[r : r + 1] = low[cols - TILE :].astype(F32)[TILE - 1 :]
        elif r == 0:
            top_ref[...] = low
        elif r == rows - 1:
            bottom_ref[...] = low

    @pl.when(jnp.logical_not(ocean))
    def _():
        clear(half)
        across = cols // BLOCK_COLS

        def add(value, label):
            r0 = (label // across) * BLOCK_ROWS
            c0 = pl.multiple_of((label % across) * BLOCK_COLS, BLOCK_COLS)
            value = value.reshape(len(block_rows), BLOCK_COLS, half)
            for start, count, at in parts:
                total[pl.ds(r0 + start, count), pl.ds(c0, BLOCK_COLS), 0:half] += value[at : at + count]

        message_copy.wait()
        each_slot(add)
        coupling_copy.wait()
        for k, (start, count) in enumerate(runs):
            block = total[start : start + count, :, 0:half].astype(BF16).reshape(count * cols, half)
            force = dot(block, coupling_ref[...]).reshape(count, cols, width)
            run_copy(sum_hbm, sum_ref, k, sum_sems).wait()
            for q in range(count):
                store(start + q, sum_ref[start + q] + force[q])

    @pl.when(ocean)
    def _():
        clear(width)
        fill_water(water_ref, wide_water, turned)
        wide = BLOCK_COLS // 2
        across = cols // wide

        def add(value, label):
            r0 = (label // across) * BLOCK_ROWS
            c0 = pl.multiple_of((label % across) * wide, wide)
            value = value.reshape(2, len(block_rows), wide, half)
            for start, count, at in parts:
                for p in range(2):
                    lanes = slice(p * half, (p + 1) * half)
                    total[pl.ds(r0 + start, count), pl.ds(c0, wide), lanes] += value[p, at : at + count]

        message_copy.wait()
        each_slot(add)
        coupling_copy.wait()
        for k, (start, count) in enumerate(runs):
            run_copy(sum_hbm, sum_ref, k, sum_sems).wait()
            for r in range(start, start + count):
                store(r, (sum_ref[r] + total[r]) * water_of_row(turned, rows, r, half, 0, cols))

    if last:
        put_sides(above_ref, below_ref, left_ref, right_ref, west_ref, east_ref)


def update(block_rows, labels, message, summed, water, coupling_matrix, early=None):
    rows, cols, width = summed.shape
    last = early is not None
    side = jax.ShapeDtypeStruct((rows + 2, width), F32)
    runs = len(runs_of(block_rows, rows))
    count = rows if last else rows // BLOCK_ROWS * len(block_rows)
    kept = [pltpu.VMEM((rows, width), F32)] * 2 if last else []
    return pl.pallas_call(
        functools.partial(update_kernel, block_rows, last),
        out_shape=(jax.ShapeDtypeStruct((count, cols, width), BF16),)
        + ((side, side) if last else rim_shapes(rows, cols, width)[:2]),
        in_specs=[SMEM, HBM, HBM, VMEM, HBM] + ([VMEM] * 5 if last else []),
        out_specs=(VMEM,) * 3,
        scratch_shapes=kept
        + [
            pltpu.VMEM((rows, cols, width), F32),
            pltpu.VMEM(message.shape, BF16),
            pltpu.VMEM((rows, cols, width), F32),
            pltpu.VMEM(coupling_matrix.shape, BF16),
        ]
        + water_scratch(cols)
        + [
            pltpu.SemaphoreType.DMA,
            pltpu.SemaphoreType.DMA,
            pltpu.SemaphoreType.DMA((runs,)),
        ],
        compiler_params=params(UPDATE_BYTES if last else VMEM_BYTES),
        name="update",
    )(labels, message, summed, water, coupling_matrix, *(early or ()))


def early_sides_kernel(new_ref, left_ref, right_ref):
    rows = left_ref.shape[0]
    cols = new_ref.shape[1]
    left_ref[...] = jnp.zeros_like(left_ref)
    right_ref[...] = jnp.zeros_like(right_ref)
    updated = [r for start, count in runs_of(SECOND, rows) for r in range(start, start + count)]
    for k, r in enumerate(updated):
        left_ref[r : r + 1] = new_ref[k, :TILE].astype(F32)[:1]
        right_ref[r : r + 1] = new_ref[k, cols - TILE :].astype(F32)[TILE - 1 :]


def early_sides(rows, new):
    side = jax.ShapeDtypeStruct((rows, new.shape[2]), F32)
    return pl.pallas_call(
        early_sides_kernel,
        out_shape=(side, side),
        in_specs=[VMEM],
        out_specs=(VMEM, VMEM),
        compiler_params=params(LATE_BYTES),
        name="early_sides",
    )(new)


def exchange(value, axis, bit):
    return lax.ppermute(value, axis, [(i, i ^ bit) for i in range(lax.axis_size(axis))])


def across_groups(value):
    return exchange(value, "grp", 1)


def to_owners(value):
    return lax.all_to_all(value, ("lat", "lon"), split_axis=0, concat_axis=0, tiled=True)


def rows_beside(top, bottom):
    lats = lax.axis_size("lat")
    above = lax.ppermute(bottom, "lat", [(i, i + 1) for i in range(lats - 1)])
    below = lax.ppermute(top, "lat", [(i + 1, i) for i in range(lats - 1)])
    return above, below


def columns_beside(west, east):
    lons = lax.axis_size("lon")
    before = lax.ppermute(east, "lon", [(i, (i + 1) % lons) for i in range(lons)])
    after = lax.ppermute(west, "lon", [((i + 1) % lons, i) for i in range(lons)])
    return before, after


def body(
    state,
    intersection_lists,
    intersection_matrices,
    water,
    air_kernels,
    sea_kernels,
    flux_projection,
    coupling_matrix,
):
    current = state[0]
    rows = current.shape[0]
    tiles = lax.axis_size("lat") * lax.axis_size("lon")
    entries = intersection_lists.shape[-1]
    matrices = intersection_matrices.reshape(entries, BLOCK, BLOCK)

    first, second, lists, top, bottom, left, right = payloads(
        intersection_lists, current, matrices, water, flux_projection, tiles
    )
    first = across_groups(first)
    second = to_owners(second)
    halo_rows = rows_beside(top, bottom)
    middle = rows // 2
    summed, token = conv_inside(0, 0, middle, current, left, air_kernels, sea_kernels, False)
    first, west, east = pack(tiles, across_groups(lists), first, *halo_rows, left, right, token)
    first = to_owners(first)
    second = across_groups(second)
    halo = halo_rows + columns_beside(west, east)
    summed, held = conv_inside(0, middle, rows, current, summed, air_kernels, sea_kernels, True)
    summed = add_edges(0, summed, halo, air_kernels, sea_kernels)

    labels = slot_labels(second)
    early, top, bottom = update(SECOND, labels, second, summed, water, coupling_matrix)
    halo_rows = rows_beside(top, bottom)
    current, west, east = update(
        FIRST, labels, first, summed, water, coupling_matrix, (early, *halo_rows, *early_sides(rows, early))
    )
    beside = columns_beside(west, east)
    out, sides = last_conv(current, *halo_rows, water, held)
    out = fix_sides(out, sides, beside, water, held)
    return out[None]


def solution(mesh):
    placed = (
        P("grp", "lat", "lon", None),
        P("grp", "lat", "lon", None, None),
        P("grp", "lat", "lon", None, None, None),
        P("lat", "lon"),
        P(),
        P(),
        P(),
        P(),
    )
    return jax.shard_map(
        body, mesh=mesh, in_specs=placed, out_specs=P("grp", "lat", "lon", None), check_vma=False
    )
```

time: 122 us -> 105 us (0.86)
  the two profiles are of different devices: /device:TPU:24 before, /device:TPU:9 now
where the time goes in v2:
time: 105 us; the launch traced here: 104 us
  Pallas kernels  53.8 us (51%)
  starting transfers between devices  29.7 us (28%)
  waiting for transfers between devices  10.4 us (10%)
  local copies, waits for them, and re-layouts  9.48 us (9%)
    pallas_call x2, Pallas kernels, conv_inside(): pl.pallas_call(functools.partial(inside_conv_kernel, layer, begin, end, k...  20 us
    all_to_all x2, starting transfers between devices, to_owners(): lax.all_to_all(value, ('lat', 'lon'), split_axis=0, concat_axis=0, tiled=...  13.4 us
    pallas_call x1, Pallas kernels, last_conv(): pl.pallas_call(last_conv_kernel, out_shape=(jax.ShapeDtypeStruct(state.sh...  10.8 us
    unnamed x33, local copies, waits for them, and re-layouts  7.97 us
    pallas_call x2, Pallas kernels, update(): pl.pallas_call(functools.partial(update_kernel, block_rows, last), out_sh...  7.25 us
    pallas_call x1, Pallas kernels, payloads(): pl.pallas_call(payload_kernel, out_shape=(jax.ShapeDtypeStruct((entries,...  6.38 us
    ppermute x2, starting transfers between devices, rows_beside(): above = lax.ppermute(bottom, 'lat', [(i, i + 1) for i in range(lats - 1)])  6.06 us
    ppermute x2, waiting for transfers between devices, rows_beside(): above = lax.ppermute(bottom, 'lat', [(i, i + 1) for i in range(lats - 1)])  5.94 us
  transfers between devices with their start and end apart: 13, of which 3 were waited for; matrix products, arithmetic and copies ran while one was open for 1% of the time, Pallas kernels for 42%

profile of v2, /device:TPU:9, one launch (start us, length us, event | category | flops | bytes accessed | tf_op | source)
XLA Modules:
  0.0 103.9 jit_solution(12618447282165976041)
XLA Ops:
  0.0 1.3 %copy.13.lists_in = s32[1,1,1,3,16]{4,3,2,1,0:T(4,128)} copy(s32[1,1,1,3,16]{4,2,3,1,0:T(1,128)} %param.9) | data formatting | bytes 384 | tf_op args[1]
  1.3 6.4 %payload.1 = (bf16[16,96,256]{2,1,0:T(8,128)(2,1)}, bf16[16,80,256]{2,1,0:T(8,128)(2,1)}, s32[3,16]{1,0:T(4,128)}, bf16[128,512]{1,0:T(8,128)(2,1)}, bf16[128,51...) custom-call(s32[1,1,1,3,16]{4,3,2,1,0:T(4,128)} %copy.13.lists_in, bf16[16,128,512]{2,1,0:T(8,128)(2,1)} %bitcast.3, ...), custom_call_target="tpu_custom_call" | custom-call | tf_op jit(solution)/shard_map/payload/pallas_call | solution.py:212
  7.7 6.6 %all-to-all-start = ((bf16[16,80,256]{2,1,0:T(8,128)(2,1)}), bf16[16,80,256]{2,1,0:T(8,128)(2,1)S(1)}, u32[]{:S(2)}, u32[]{:S(2)}) async-start(bf16[16,80,256]{2,1,0:T(8,128)(2,1)} %get-tuple-element.29), calls=%async_computation | async-start | bytes 1310720 | tf_op jit(solution)/shard_map/all_to_all | solution.py:877
  14.3 0.4 collective-permute-start.2
  14.7 3.1 %collective-permute-start.3 = (bf16[128,512]{1,0:T(8,128)(2,1)}, bf16[128,512]{1,0:T(8,128)(2,1)S(1)}, u32[]{:S(2)}, u32[]{:S(2)}) collective-permute-start(bf16[128,512]{1,0:T(8,128)(2,1)} %get-tuple-element.32), channel_id=1, source_target_pairs={{0,4},{4,8},{8,12},{1,5},{5,9},{9,13},{2,6},{6,10},{10,14},{3,7},{... | collective-permute-start | bytes 393224 | tf_op jit(solution)/shard_map/ppermute | solution.py:882
  17.8 2.2 %collective-permute-start.4 = (bf16[128,512]{1,0:T(8,128)(2,1)}, bf16[128,512]{1,0:T(8,128)(2,1)S(1)}, u32[]{:S(2)}, u32[]{:S(2)}) collective-permute-start(bf16[128,512]{1,0:T(8,128)(2,1)} %get-tuple-element.33), channel_id=1, source_target_pairs={{4,0},{8,4},{12,8},{5,1},{9,5},{13,9},{6,2},{10,6},{14,10},{7,3},{... | collective-permute-start | bytes 393224 | tf_op jit(solution)/shard_map/ppermute | solution.py:883
  20.0 1.1 %collective-permute-start.1 = (s32[3,16]{1,0:T(4,128)}, s32[3,16]{1,0:T(4,128)S(1)}, u32[]{:S(2)}, u32[]{:S(2)}) collective-permute-start(s32[3,16]{1,0:T(4,128)} %get-tuple-element.30), channel_id=1, source_target_pairs={{0,16},{16,0},{1,17},{17,1},{2,18},{18,2},{3,19},{19,3},{4,20},{20... | collective-permute-start | bytes 584 | tf_op jit(solution)/shard_map/ppermute | solution.py:869
  21.1 9.5 %conv_inside.2 = (f32[16,128,512]{2,1,0:T(8,128)}, f32[8,128]{1,0:T(8,128)}) custom-call(bf16[16,128,512]{2,1,0:T(8,128)(2,1)} %bitcast.4, f32[16,512]{1,0:T(8,128)} %get-tuple-element.34.refs_1_.left_ref, bf16[2,3,3,512,512]{4,3,2,1,0:T(8,128)(2,1)} %air_hbm.1, bf16[2,3,3,256,256]{4,3,2,1,0:T(8,128)(2,1)} %sea_hbm.1), custom_call_target="tpu_custom_call" | custom-call | flops 4831838208 | bytes 7864320 | tf_op jit(solution)/shard_map/conv_inside/pallas_call | solution.py:526
  30.5 2.7 %collective-permute-done.1.lists_ref = s32[3,16]{1,0:T(4,128)S(1)} collective-permute-done((s32[3,16]{1,0:T(4,128)}, s32[3,16]{1,0:T(4,128)S(1)}, u32[]{:S(2)}, u32[]{:S(2)}) %collective-permute-start.1) | collective-permute-done | bytes 224 | tf_op jit(solution)/shard_map/ppermute | solution.py:869
  33.3 0.0 collective-permute-done.3.above_ref.top_ref
  33.3 0.0 collective-permute-done.4.below_ref.bottom_ref
  33.3 0.0 collective-permute-done.2.dense_ref
  33.3 0.5 copy-done.13
  33.9 0.1 copy-done.9
  33.9 0.0 copy-done.10
  34.0 0.3 copy-done.7
  34.3 2.6 %pack.1 = (bf16[16,192,256]{2,1,0:T(8,128)(2,1)}, f32[18,512]{1,0:T(8,128)}, f32[18,512]{1,0:T(8,128)}) custom-call(s32[3,16]{1,0:T(4,128)} %copy-done.13, bf16[16,96,256]{2,1,0:T(8,128)(2,1)} %copy-done.7, bf16[128,512]{1,0:T(8,128)(2,1)} %copy-done.9, bf16[128,512]{1,0:T(8,128)(2,1)} %copy-done.10, f32[16,512]{1,0:T(8,128)} %get-tuple-element.34.refs_1_.left_ref, ...), custom_call_target="tpu_custom_call" | custom-call | tf_op jit(solution)/shard_map/pack/pallas_call | solution.py:267
  36.9 0.0 all-to-all-done
  36.9 0.9 copy-done.8
  37.7 6.8 %all-to-all-start.1 = ((bf16[16,192,256]{2,1,0:T(8,128)(2,1)}), bf16[16,192,256]{2,1,0:T(8,128)(2,1)S(1)}, u32[]{:S(2)}, u32[]{:S(2)}) async-start(bf16[16,192,256]{2,1,0:T(8,128)(2,1)} %get-tuple-element.37), calls=%async_computation.1 | async-start | bytes 3145728 | tf_op jit(solution)/shard_map/all_to_all | solution.py:877
  44.6 0.4 collective-permute-start
  45.0 1.7 %collective-permute-start.5 = (f32[18,512]{1,0:T(8,128)S(1)}, f32[18,512]{1,0:T(8,128)S(1)}, u32[]{:S(2)}, u32[]{:S(2)}) collective-permute-start(f32[18,512]{1,0:T(8,128)S(1)} %copy-done.15), channel_id=1, source_target_pairs={{0,1},{1,2},{2,3},{3,0},{4,5},{5,6},{6,7},{7,4},{8,9},{9,10},{10,1... | collective-permute-start | bytes 110600 | tf_op jit(solution)/shard_map/ppermute | solution.py:889
  46.7 0.0 collective-permute-start.6
  46.7 10.6 %conv_inside.3 = (f32[16,128,512]{2,1,0:T(8,128)}, bf16[3,3,512,512]{3,2,1,0:T(8,128)(2,1)}) custom-call(bf16[16,128,512]{2,1,0:T(8,128)(2,1)} %bitcast.5, f32[16,128,512]{2,1,0:T(8,128)} %get-tuple-element.38.refs_1_, bf16[2,3,3,512,512]{4,3,2,1,0:T(8,128)(2,1)} %air_hbm.1, bf16[2,3,3,256,256]{4,3,2,1,0:T(8,128)(2,1)} %sea_hbm.1), custom_call_target="tpu_custom_call", output_to_operand_aliasing={{0}: (1, {})} | custom-call | flops 4831838208 | bytes 7864320 | tf_op jit(solution)/shard_map/conv_inside/pallas_call | solution.py:526
  57.3 0.0 collective-permute-done.5.left_ref
  57.3 0.0 collective-permute-done.6.right_ref
  57.4 0.6 copy-done.11
  57.9 0.0 copy-done.12
  58.0 5.4 %add_edges.1.refs_2_ = f32[16,128,512]{2,1,0:T(8,128)} custom-call(f32[16,128,512]{2,1,0:T(8,128)} %get-tuple-element.39.sum_in_hbm, bf16[128,512]{1,0:T(8,128)(2,1)} %copy-done.9, bf16[128,512]{1,0:T(8,128)(2,1)} %copy-done.10, f32[18,512]{1,0:T(8,128)} %copy-done.11, f32[18,512]{1,0:T(8,128)} %copy-done.12, ...), custom_call_target="tpu_custom_call", output_to_operand_aliasing={{}: (0, {})} | custom-call | tf_op jit(solution)/shard_map/add_edges/pallas_call | solution.py:669
  63.4 0.0 collective-permute-done.refs_1_
  63.4 0.9 slice.3
  64.4 0.6 reshape.8.refs_0_
  64.9 4.4 %update.2 = (bf16[4,128,512]{2,1,0:T(8,128)(2,1)}, bf16[128,512]{1,0:T(8,128)(2,1)}, bf16[128,512]{1,0:T(8,128)(2,1)}) custom-call(s32[32]{0:T(128)} %reshape.8.refs_0_, bf16[16,80,256]{2,1,0:T(8,128)(2,1)} %collective-permute-done.refs_1_, f32[16,128,512]{2,1,0:T(8,128)} %add_edges.1.refs_2_, s32[16,256]{1,0:T(8,128)} %water_ref.5, bf16[256,512]{1,0:T(8,128)(2,1)} %refs_4_.3), custom_call_target="tpu_custom_call" | custom-call | tf_op jit(solution)/shard_map/update/pallas_call | solution.py:821
  69.3 3.0 %collective-permute-start.7 = (bf16[128,512]{1,0:T(8,128)(2,1)}, bf16[128,512]{1,0:T(8,128)(2,1)S(1)}, u32[]{:S(2)}, u32[]{:S(2)}) collective-permute-start(bf16[128,512]{1,0:T(8,128)(2,1)} %get-tuple-element.43), channel_id=1, source_target_pairs={{0,4},{4,8},{8,12},{1,5},{5,9},{9,13},{2,6},{6,10},{10,14},{3,7},{... | collective-permute-start | bytes 393224 | tf_op jit(solution)/shard_map/ppermute | solution.py:882
  72.3 2.3 %collective-permute-start.8 = (bf16[128,512]{1,0:T(8,128)(2,1)}, bf16[128,512]{1,0:T(8,128)(2,1)S(1)}, u32[]{:S(2)}, u32[]{:S(2)}) collective-permute-start(bf16[128,512]{1,0:T(8,128)(2,1)} %get-tuple-element.44), channel_id=1, source_target_pairs={{4,0},{8,4},{12,8},{5,1},{9,5},{13,9},{6,2},{10,6},{14,10},{7,3},{... | collective-permute-start | bytes 393224 | tf_op jit(solution)/shard_map/ppermute | solution.py:883
  74.6 1.0 copy-done.2
  75.7 5.9 %collective-permute-done.7.refs_6_.above_ref = bf16[128,512]{1,0:T(8,128)(2,1)S(1)} collective-permute-done((bf16[128,512]{1,0:T(8,128)(2,1)}, bf16[128,512]{1,0:T(8,128)(2,1)S(1)}, u32[]{:S(2)}, u32[]{:S(2)}) %collective-permute-start.7) | collective-permute-done | bytes 131104 | tf_op jit(solution)/shard_map/ppermute | solution.py:882
  81.6 1.7 %collective-permute-done.8.refs_7_.below_ref = bf16[128,512]{1,0:T(8,128)(2,1)S(1)} collective-permute-done((bf16[128,512]{1,0:T(8,128)(2,1)}, bf16[128,512]{1,0:T(8,128)(2,1)S(1)}, u32[]{:S(2)}, u32[]{:S(2)}) %collective-permute-start.8) | collective-permute-done | bytes 131104 | tf_op jit(solution)/shard_map/ppermute | solution.py:883
  83.3 0.0 all-to-all-done.1.refs_1_
  83.4 2.2 %copy-done = f32[16,128,512]{2,1,0:T(8,128)S(1)} copy-done((f32[16,128,512]{2,1,0:T(8,128)S(1)}, f32[16,128,512]{2,1,0:T(8,128)}, u32[]{:S(2)}) %copy-start) | copy-done | bytes 4194328
  85.6 1.0 %copy-done.3 = bf16[4,128,512]{2,1,0:T(8,128)(2,1)S(1)} copy-done((bf16[4,128,512]{2,1,0:T(8,128)(2,1)S(1)}, bf16[4,128,512]{2,1,0:T(8,128)(2,1)}, u32[]{:S(2)}) %copy-start.3) | copy-done | bytes 524312
  86.6 2.9 %update.3 = (bf16[16,128,512]{2,1,0:T(8,128)(2,1)S(1)}, f32[18,512]{1,0:T(8,128)S(1)}, f32[18,512]{1,0:T(8,128)S(1)}) custom-call(s32[32]{0:T(128)S(1)} %copy-done.6, bf16[16,192,256]{2,1,0:T(8,128)(2,1)S(1)} %all-to-all-done.1.refs_1_, f32[16,128,512]{2,1,0:T(8,128)S(1)} %copy-done, s32[16,256]{1,0:T(8,128)S(1)} %copy-done.5, ...), custom_call_target="tpu_custom_call" | custom-call | tf_op jit(solution)/shard_map/update/pallas_call | solution.py:821
  89.5 0.8 collective-permute-start.10
  90.3 1.3 %collective-permute-start.9 = (f32[18,512]{1,0:T(8,128)S(1)}, f32[18,512]{1,0:T(8,128)S(1)}, u32[]{:S(2)}, u32[]{:S(2)}) collective-permute-start(f32[18,512]{1,0:T(8,128)S(1)} %get-tuple-element.51), channel_id=1, source_target_pairs={{0,1},{1,2},{2,3},{3,0},{4,5},{5,6},{6,7},{7,4},{8,9},{9,10},{10,1... | collective-permute-start | bytes 110600 | tf_op jit(solution)/shard_map/ppermute | solution.py:889
  91.6 10.8 %last_conv.1 = (bf16[16,128,512]{2,1,0:T(8,128)(2,1)}, f32[2,16,16,512]{3,2,1,0:T(8,128)S(1)}) custom-call(bf16[16,128,512]{2,1,0:T(8,128)(2,1)S(1)} %get-tuple-element.47.x_ref, bf16[128,512]{1,0:T(8,128)(2,1)S(1)} %collective-permute-done.7.refs_6_.above_ref, bf16[128,512]{1,0:T(8,128)(2,1)S(1)} %collective-permute-done.8.refs_7_.below_ref, ...), custom_call_target="tpu_custom_call" | custom-call | flops 9663676416 | bytes 11010048 | tf_op jit(solution)/shard_map/last_conv/pallas_call | solution.py:484
  102.4 0.0 collective-permute-done.10.right_ref
  102.4 0.0 collective-permute-done.9.left_ref
  102.4 1.3 %fix_sides.1 = bf16[16,128,512]{2,1,0:T(8,128)(2,1)} custom-call(bf16[16,128,512]{2,1,0:T(8,128)(2,1)} %get-tuple-element.49.out_in_hbm, f32[2,16,16,512]{3,2,1,0:T(8,128)S(1)} %get-tuple-element.50.sides_ref, f32[18,512]{1,0:T(8,128)S(1)} %collective-permute-done.9.left_ref, ...), custom_call_target="tpu_custom_call", output_to_operand_aliasing={{}: (0, {})} | custom-call | tf_op jit(solution)/shard_map/fix_sides/pallas_call | solution.py:600
  (24 shorter events, 0.1 us)
Async XLA Ops:
  7.7 29.2 %all-to-all-start = ((bf16[16,80,256]{2,1,0:T(8,128)(2,1)}), bf16[16,80,256]{2,1,0:T(8,128)(2,1)S(1)}, u32[]{:S(2)}, u32[]{:S(2)}) async-start(bf16[16,80,256]{2,1,0:T(8,128)(2,1)} %get-tuple-element.29), calls=%async_computation | async-start | bytes 1310720 | tf_op jit(solution)/shard_map/all_to_all | solution.py:877
  14.3 19.1 %collective-permute-start.2 = (bf16[16,96,256]{2,1,0:T(8,128)(2,1)}, bf16[16,96,256]{2,1,0:T(8,128)(2,1)S(1)}, u32[]{:S(2)}, u32[]{:S(2)}) collective-permute-start(bf16[16,96,256]{2,1,0:T(8,128)(2,1)} %get-tuple-element.31), channel_id=1, source_target_pairs={{0,16},{16,0},{1,17},{17,1},{2,18},{18,2},{3,19},{19,3},{4,20},{20... | collective-permute-start | bytes 2359304 | tf_op jit(solution)/shard_map/ppermute | solution.py:869
  14.7 18.6 %collective-permute-start.3 = (bf16[128,512]{1,0:T(8,128)(2,1)}, bf16[128,512]{1,0:T(8,128)(2,1)S(1)}, u32[]{:S(2)}, u32[]{:S(2)}) collective-permute-start(bf16[128,512]{1,0:T(8,128)(2,1)} %get-tuple-element.32), channel_id=1, source_target_pairs={{0,4},{4,8},{8,12},{1,5},{5,9},{9,13},{2,6},{6,10},{10,14},{3,7},{... | collective-permute-start | bytes 393224 | tf_op jit(solution)/shard_map/ppermute | solution.py:882
  17.8 15.5 %collective-permute-start.4 = (bf16[128,512]{1,0:T(8,128)(2,1)}, bf16[128,512]{1,0:T(8,128)(2,1)S(1)}, u32[]{:S(2)}, u32[]{:S(2)}) collective-permute-start(bf16[128,512]{1,0:T(8,128)(2,1)} %get-tuple-element.33), channel_id=1, source_target_pairs={{4,0},{8,4},{12,8},{5,1},{9,5},{13,9},{6,2},{10,6},{14,10},{7,3},{... | collective-permute-start | bytes 393224 | tf_op jit(solution)/shard_map/ppermute | solution.py:883
  20.0 13.3 %collective-permute-start.1 = (s32[3,16]{1,0:T(4,128)}, s32[3,16]{1,0:T(4,128)S(1)}, u32[]{:S(2)}, u32[]{:S(2)}) collective-permute-start(s32[3,16]{1,0:T(4,128)} %get-tuple-element.30), channel_id=1, source_target_pairs={{0,16},{16,0},{1,17},{17,1},{2,18},{18,2},{3,19},{19,3},{4,20},{20... | collective-permute-start | bytes 584 | tf_op jit(solution)/shard_map/ppermute | solution.py:869
  33.3 0.6 copy-start.13
  33.3 0.7 copy-start.9
  33.3 0.7 copy-start.10
  33.3 1.0 copy-start.7
  36.9 8.2 %copy-start.15 = (f32[18,512]{1,0:T(8,128)S(1)}, f32[18,512]{1,0:T(8,128)}, u32[]{:S(2)}) copy-start(f32[18,512]{1,0:T(8,128)} %get-tuple-element.40) | copy-start | bytes 110596
  36.9 9.9 %copy-start.14 = (f32[18,512]{1,0:T(8,128)S(1)}, f32[18,512]{1,0:T(8,128)}, u32[]{:S(2)}) copy-start(f32[18,512]{1,0:T(8,128)} %get-tuple-element.41) | copy-start | bytes 110596
  36.9 0.9 copy-start.8
  37.7 45.6 %all-to-all-start.1 = ((bf16[16,192,256]{2,1,0:T(8,128)(2,1)}), bf16[16,192,256]{2,1,0:T(8,128)(2,1)S(1)}, u32[]{:S(2)}, u32[]{:S(2)}) async-start(bf16[16,192,256]{2,1,0:T(8,128)(2,1)} %get-tuple-element.37), calls=%async_computation.1 | async-start | bytes 3145728 | tf_op jit(solution)/shard_map/all_to_all | solution.py:877
  44.6 18.8 %collective-permute-start = (bf16[16,80,256]{2,1,0:T(8,128)(2,1)}, bf16[16,80,256]{2,1,0:T(8,128)(2,1)}, u32[]{:S(2)}, u32[]{:S(2)}) collective-permute-start(bf16[16,80,256]{2,1,0:T(8,128)(2,1)} %copy-done.8), channel_id=1, source_target_pairs={{0,16},{16,0},{1,17},{17,1},{2,18},{18,2},{3,19},{19,3},{4,20},{20... | collective-permute-start | bytes 1966088 | tf_op jit(solution)/shard_map/ppermute | solution.py:869
  45.0 12.3 %collective-permute-start.5 = (f32[18,512]{1,0:T(8,128)S(1)}, f32[18,512]{1,0:T(8,128)S(1)}, u32[]{:S(2)}, u32[]{:S(2)}) collective-permute-start(f32[18,512]{1,0:T(8,128)S(1)} %copy-done.15), channel_id=1, source_target_pairs={{0,1},{1,2},{2,3},{3,0},{4,5},{5,6},{6,7},{7,4},{8,9},{9,10},{10,1... | collective-permute-start | bytes 110600 | tf_op jit(solution)/shard_map/ppermute | solution.py:889
  46.7 10.6 %collective-permute-start.6 = (f32[18,512]{1,0:T(8,128)S(1)}, f32[18,512]{1,0:T(8,128)S(1)}, u32[]{:S(2)}, u32[]{:S(2)}) collective-permute-start(f32[18,512]{1,0:T(8,128)S(1)} %copy-done.14), channel_id=1, source_target_pairs={{1,0},{2,1},{3,2},{0,3},{5,4},{6,5},{7,6},{4,7},{9,8},{10,9},{11,1... | collective-permute-start | bytes 110600 | tf_op jit(solution)/shard_map/ppermute | solution.py:890
  57.3 0.6 copy-start.11
  57.3 0.6 copy-start.12
  64.9 18.4 %copy-start.4 = (bf16[256,512]{1,0:T(8,128)(2,1)S(1)}, bf16[256,512]{1,0:T(8,128)(2,1)}, u32[]{:S(2)}) copy-start(bf16[256,512]{1,0:T(8,128)(2,1)} %refs_4_.3) | copy-start | bytes 786436
  64.9 18.4 %copy-start.5 = (s32[16,256]{1,0:T(8,128)S(1)}, s32[16,256]{1,0:T(8,128)}, u32[]{:S(2)}) copy-start(s32[16,256]{1,0:T(8,128)} %water_ref.5) | copy-start | bytes 49156
  64.9 18.4 %copy-start.6 = (s32[32]{0:T(128)S(1)}, s32[32]{0:T(128)}, u32[]{:S(2)}) copy-start(s32[32]{0:T(128)} %reshape.8.refs_0_) | copy-start | bytes 388
  69.3 12.3 %collective-permute-start.7 = (bf16[128,512]{1,0:T(8,128)(2,1)}, bf16[128,512]{1,0:T(8,128)(2,1)S(1)}, u32[]{:S(2)}, u32[]{:S(2)}) collective-permute-start(bf16[128,512]{1,0:T(8,128)(2,1)} %get-tuple-element.43), channel_id=1, source_target_pairs={{0,4},{4,8},{8,12},{1,5},{5,9},{9,13},{2,6},{6,10},{10,14},{3,7},{... | collective-permute-start | bytes 393224 | tf_op jit(solution)/shard_map/ppermute | solution.py:882
  72.3 11.0 %collective-permute-start.8 = (bf16[128,512]{1,0:T(8,128)(2,1)}, bf16[128,512]{1,0:T(8,128)(2,1)S(1)}, u32[]{:S(2)}, u32[]{:S(2)}) collective-permute-start(bf16[128,512]{1,0:T(8,128)(2,1)} %get-tuple-element.44), channel_id=1, source_target_pairs={{4,0},{8,4},{12,8},{5,1},{9,5},{13,9},{6,2},{10,6},{14,10},{7,3},{... | collective-permute-start | bytes 393224 | tf_op jit(solution)/shard_map/ppermute | solution.py:883
  74.6 1.0 %copy-start.2 = (bf16[4,128,512]{2,1,0:T(8,128)(2,1)S(1)}, bf16[4,128,512]{2,1,0:T(8,128)(2,1)}, u32[]{:S(2)}) copy-start(bf16[4,128,512]{2,1,0:T(8,128)(2,1)} %get-tuple-element.42.new_ref.refs_5_) | copy-start | bytes 1572868
  83.4 2.2 %copy-start = (f32[16,128,512]{2,1,0:T(8,128)S(1)}, f32[16,128,512]{2,1,0:T(8,128)}, u32[]{:S(2)}) copy-start(f32[16,128,512]{2,1,0:T(8,128)} %add_edges.1.refs_2_) | copy-start | bytes 12582916
  85.6 1.0 %copy-start.3 = (bf16[4,128,512]{2,1,0:T(8,128)(2,1)S(1)}, bf16[4,128,512]{2,1,0:T(8,128)(2,1)}, u32[]{:S(2)}) copy-start(bf16[4,128,512]{2,1,0:T(8,128)(2,1)} %get-tuple-element.42.new_ref.refs_5_) | copy-start | bytes 1572868
  86.6 5.0 %copy-start.1 = (bf16[3,3,512,512]{3,2,1,0:T(8,128)(2,1)S(1)}, bf16[3,3,512,512]{3,2,1,0:T(8,128)(2,1)}, u32[]{:S(2)}) copy-start(bf16[3,3,512,512]{3,2,1,0:T(8,128)(2,1)} %get-tuple-element.48.held) | copy-start | bytes 14155780
  89.5 12.9 %collective-permute-start.10 = (f32[18,512]{1,0:T(8,128)S(1)}, f32[18,512]{1,0:T(8,128)S(1)}, u32[]{:S(2)}, u32[]{:S(2)}) collective-permute-start(f32[18,512]{1,0:T(8,128)S(1)} %get-tuple-element.52), channel_id=1, source_target_pairs={{1,0},{2,1},{3,2},{0,3},{5,4},{6,5},{7,6},{4,7},{9,8},{10,9},{11,1... | collective-permute-start | bytes 110600 | tf_op jit(solution)/shard_map/ppermute | solution.py:890
  90.3 12.1 %collective-permute-start.9 = (f32[18,512]{1,0:T(8,128)S(1)}, f32[18,512]{1,0:T(8,128)S(1)}, u32[]{:S(2)}, u32[]{:S(2)}) collective-permute-start(f32[18,512]{1,0:T(8,128)S(1)} %get-tuple-element.51), channel_id=1, source_target_pairs={{0,1},{1,2},{2,3},{3,0},{4,5},{5,6},{6,7},{7,4},{8,9},{9,10},{10,1... | collective-permute-start | bytes 110600 | tf_op jit(solution)/shard_map/ppermute | solution.py:889

commit v3 on v2

--- a/solution.py
+++ b/solution.py
@@ -27,6 +27,7 @@
 VMEM = pl.BlockSpec(memory_space=pltpu.VMEM)
 SMEM = pl.BlockSpec(memory_space=pltpu.SMEM)
 HBM = pl.BlockSpec(memory_space=pltpu.HBM)
+ANY = pl.BlockSpec(memory_space=pl.ANY)
 
 
 def silu(v):
@@ -90,7 +91,7 @@
 def payload_kernel(
     lists_in, state_hbm, matrices_hbm, water_ref, flux_hbm,
     first_ref, second_ref, lists_out, top_ref, bottom_ref, left_ref, right_ref,
-    state_ref, matrices_ref, flux_ref, flux, surface, wide_water, turned, count, sems,
+    state_ref, matrices_ref, weights, flux_ref, flux, surface, wide_water, turned, count, sems,
 ):
     rows, cols, width = state_ref.shape
     half = width // 2
@@ -106,10 +107,10 @@
         for k in range(pieces)
     ]
     lists_ref = lists_in.at[0, 0, 0]
+    matrices_copy.start()
     flux_copy.start()
     for copy in state_copies:
         copy.start()
-    matrices_copy.start()
 
     def clear(t, _):
         count[t] = 0
@@ -137,6 +138,7 @@
         label = jnp.full((LABEL_ROWS, LANES), lists_ref[2, e], jnp.int32).astype(F32).astype(BF16)
         second_ref[owner, SLOTS * SECOND_CELLS :, pl.ds(pl.multiple_of(rank * LANES, LANES), LANES)] = label
 
+    matrices_copy.wait()
     flux_copy.wait()
 
     @pl.when(jnp.logical_not(ocean))
@@ -149,13 +151,14 @@
         p2, r2 = k // (SECOND_CELLS // 2), jnp.where(q == 0, 0, q + FIRST[-1])
         p, r = jnp.where(k < 0, p1, p2), jnp.where(k < 0, r1, r2)
         turn = (j == r * BLOCK_COLS + 2 * c + p).astype(BF16)
+        for e in range(entries):
+            weights[e] = dot(turn, matrices_ref[e]).astype(BF16)
         for k in range(pieces):
             state_copies[k].wait()
             block = state_ref[k * step : (k + 1) * step].reshape(step * cols, width)
             flux[k * step : (k + 1) * step] = (
                 dot(block, flux_ref[...]).astype(BF16).reshape(step, cols, half)
             )
-        matrices_copy.wait()
         across = cols // BLOCK_COLS
 
         def entry(e, _):
@@ -163,8 +166,7 @@
             r0 = (source // across) * BLOCK_ROWS
             c0 = pl.multiple_of((source % across) * BLOCK_COLS, BLOCK_COLS)
             chosen = flux[pl.ds(r0, BLOCK_ROWS), pl.ds(c0, BLOCK_COLS), :].reshape(BLOCK, half)
-            weight = dot(turn, matrices_ref[e]).astype(BF16)
-            put(e, dot(weight, chosen).astype(BF16), lambda v: (v[:FIRST_CELLS], v[FIRST_CELLS:]))
+            put(e, dot(weights[e], chosen).astype(BF16), lambda v: (v[:FIRST_CELLS], v[FIRST_CELLS:]))
             return 0
 
         lax.fori_loop(0, entries, entry, 0, unroll=8)
@@ -173,12 +175,13 @@
     def _():
         p, r, c = j // 64, (j // 8) % 8, j % 8
         turn = (i == r * BLOCK_COLS + 2 * c + p).astype(BF16)
+        for e in range(entries):
+            weights[e] = dot(matrices_ref[e], turn).astype(BF16)
         fill_water(water_ref, wide_water, turned)
         for k in range(pieces):
             state_copies[k].wait()
             for r0 in range(k * step, (k + 1) * step):
                 surface[r0] = state_ref[r0].astype(F32) * water_of_row(turned, rows, r0, half, 0, cols)
-        matrices_copy.wait()
         wide = BLOCK_COLS // 2
         across = cols // wide
 
@@ -190,11 +193,10 @@
             chosen = jnp.concatenate(
                 [block[:, :, q * half : (q + 1) * half].reshape(BLOCK // 2, half) for q in range(2)], axis=0
             ).astype(BF16)
-            weight = dot(matrices_ref[e], turn).astype(BF16)
             low, high = BLOCK_COLS, BLOCK_COLS + FIRST_CELLS
             put(
                 e,
-                dot(weight, chosen).astype(BF16),
+                dot(weights[e], chosen).astype(BF16),
                 lambda v: (v[low:high], jnp.concatenate([v[:low], v[high:]], axis=0)),
             )
             return 0
@@ -221,6 +223,7 @@
         out_specs=(VMEM, VMEM, SMEM) + (VMEM,) * 4,
         scratch_shapes=[
             pltpu.VMEM(state.shape, BF16),
+            pltpu.VMEM(matrices.shape, BF16),
             pltpu.VMEM(matrices.shape, BF16),
             pltpu.VMEM(flux_projection.shape, BF16),
             pltpu.VMEM((rows, cols, half), BF16),
@@ -842,7 +845,7 @@
     )(labels, message, summed, water, coupling_matrix, *(early or ()))
 
 
-def early_sides_kernel(new_ref, left_ref, right_ref):
+def early_sides_kernel(new_ref, _, __, left_ref, right_ref, ___):
     rows = left_ref.shape[0]
     cols = new_ref.shape[1]
     left_ref[...] = jnp.zeros_like(left_ref)
@@ -853,16 +856,17 @@
         right_ref[r : r + 1] = new_ref[k, cols - TILE :].astype(F32)[TILE - 1 :]
 
 
-def early_sides(rows, new):
+def early_sides(rows, new, summed, coupling_matrix):
     side = jax.ShapeDtypeStruct((rows, new.shape[2]), F32)
     return pl.pallas_call(
         early_sides_kernel,
-        out_shape=(side, side),
-        in_specs=[VMEM],
-        out_specs=(VMEM, VMEM),
+        out_shape=(side, side, jax.ShapeDtypeStruct(summed.shape, F32)),
+        in_specs=[VMEM, ANY, ANY],
+        out_specs=(VMEM, VMEM, ANY),
+        input_output_aliases={1: 2},
         compiler_params=params(LATE_BYTES),
         name="early_sides",
-    )(new)
+    )(new, summed, coupling_matrix)
 
 
 def exchange(value, axis, bit):
@@ -925,8 +929,9 @@
     labels = slot_labels(second)
     early, top, bottom = update(SECOND, labels, second, summed, water, coupling_matrix)
     halo_rows = rows_beside(top, bottom)
+    left, right, summed = early_sides(rows, early, summed, coupling_matrix)
     current, west, east = update(
-        FIRST, labels, first, summed, water, coupling_matrix, (early, *halo_rows, *early_sides(rows, early))
+        FIRST, labels, first, summed, water, coupling_matrix, (early, *halo_rows, left, right)
     )
     beside = columns_beside(west, east)
     out, sides = last_conv(current, *halo_rows, water, held)

time: 105 us -> 103 us (0.981)
  waiting for transfers between devices: 10.4 us -> 6.26 us
  local copies, waits for them, and re-layouts: 9.48 us -> 12.7 us
    ppermute x2, waiting for transfers between devices: 5.94 us -> 1.76 us  [rows_beside(): above = lax.ppermute(bottom, 'lat', [(i, i + 1) for i in range(lats - 1)])]
    unnamed x33 -> x37, local copies, waits for them, and re-layouts: 7.97 us -> 11.1 us
  transfers between devices with their start and end apart: 13 -> 13, of which waited for: 3 -> 3; matrix products, arithmetic and copies ran while one was open for 1% -> 2% of each run, Pallas kernels for 42% -> 42%
where the time goes in v3:
time: 103 us; the launch traced here: 102 us
  Pallas kernels  53.1 us (52%)
  starting transfers between devices  29.8 us (29%)
  local copies, waits for them, and re-layouts  12.7 us (12%)
  waiting for transfers between devices  6.26 us (6%)
    pallas_call x2, Pallas kernels, conv_inside(): pl.pallas_call(functools.partial(inside_conv_kernel, layer, begin, end, k...  20 us
    all_to_all x2, starting transfers between devices, to_owners(): lax.all_to_all(value, ('lat', 'lon'), split_axis=0, concat_axis=0, tiled=...  13.4 us
    unnamed x37, local copies, waits for them, and re-layouts  11.1 us
    pallas_call x1, Pallas kernels, last_conv(): pl.pallas_call(last_conv_kernel, out_shape=(jax.ShapeDtypeStruct(state.sh...  10.8 us
    pallas_call x2, Pallas kernels, update(): pl.pallas_call(functools.partial(update_kernel, block_rows, last), out_sh...  7.14 us
    ppermute x2, starting transfers between devices, rows_beside(): above = lax.ppermute(bottom, 'lat', [(i, i + 1) for i in range(lats - 1)])  6.15 us
    pallas_call x1, Pallas kernels, payloads(): pl.pallas_call(payload_kernel, out_shape=(jax.ShapeDtypeStruct((entries,...  5.71 us
    pallas_call x1, Pallas kernels, add_edges(): pl.pallas_call(functools.partial(sum_edge_kernel, layer), out_shape=jax.S...  5.42 us
  transfers between devices with their start and end apart: 13, of which 3 were waited for; matrix products, arithmetic and copies ran while one was open for 2% of the time, Pallas kernels for 42%

profile of v3, /device:TPU:9, one launch (start us, length us, event | category | flops | bytes accessed | tf_op | source)
XLA Modules:
  0.0 102.3 jit_solution(17279079910047361042)
XLA Ops:
  0.0 1.3 %copy.14.lists_in = s32[1,1,1,3,16]{4,3,2,1,0:T(4,128)} copy(s32[1,1,1,3,16]{4,2,3,1,0:T(1,128)} %param.9) | data formatting | bytes 384 | tf_op args[1]
  1.3 5.7 %payload.1 = (bf16[16,96,256]{2,1,0:T(8,128)(2,1)}, bf16[16,80,256]{2,1,0:T(8,128)(2,1)}, s32[3,16]{1,0:T(4,128)}, bf16[128,512]{1,0:T(8,128)(2,1)}, bf16[128,51...) custom-call(s32[1,1,1,3,16]{4,3,2,1,0:T(4,128)} %copy.14.lists_in, bf16[16,128,512]{2,1,0:T(8,128)(2,1)} %bitcast.3, ...), custom_call_target="tpu_custom_call" | custom-call | tf_op jit(solution)/shard_map/payload/pallas_call | solution.py:214
  7.0 6.6 %all-to-all-start = ((bf16[16,80,256]{2,1,0:T(8,128)(2,1)}), bf16[16,80,256]{2,1,0:T(8,128)(2,1)S(1)}, u32[]{:S(2)}, u32[]{:S(2)}) async-start(bf16[16,80,256]{2,1,0:T(8,128)(2,1)} %get-tuple-element.30), calls=%async_computation | async-start | bytes 1310720 | tf_op jit(solution)/shard_map/all_to_all | solution.py:881
  13.6 0.4 collective-permute-start.2
  14.0 3.1 %collective-permute-start.3 = (bf16[128,512]{1,0:T(8,128)(2,1)}, bf16[128,512]{1,0:T(8,128)(2,1)S(1)}, u32[]{:S(2)}, u32[]{:S(2)}) collective-permute-start(bf16[128,512]{1,0:T(8,128)(2,1)} %get-tuple-element.33), channel_id=1, source_target_pairs={{0,4},{4,8},{8,12},{1,5},{5,9},{9,13},{2,6},{6,10},{10,14},{3,7},{... | collective-permute-start | bytes 393224 | tf_op jit(solution)/shard_map/ppermute | solution.py:886
  17.0 2.2 %collective-permute-start.4 = (bf16[128,512]{1,0:T(8,128)(2,1)}, bf16[128,512]{1,0:T(8,128)(2,1)S(1)}, u32[]{:S(2)}, u32[]{:S(2)}) collective-permute-start(bf16[128,512]{1,0:T(8,128)(2,1)} %get-tuple-element.34), channel_id=1, source_target_pairs={{4,0},{8,4},{12,8},{5,1},{9,5},{13,9},{6,2},{10,6},{14,10},{7,3},{... | collective-permute-start | bytes 393224 | tf_op jit(solution)/shard_map/ppermute | solution.py:887
  19.2 1.2 %collective-permute-start.1 = (s32[3,16]{1,0:T(4,128)}, s32[3,16]{1,0:T(4,128)S(1)}, u32[]{:S(2)}, u32[]{:S(2)}) collective-permute-start(s32[3,16]{1,0:T(4,128)} %get-tuple-element.31), channel_id=1, source_target_pairs={{0,16},{16,0},{1,17},{17,1},{2,18},{18,2},{3,19},{19,3},{4,20},{20... | collective-permute-start | bytes 584 | tf_op jit(solution)/shard_map/ppermute | solution.py:873
  20.4 9.5 %conv_inside.2 = (f32[16,128,512]{2,1,0:T(8,128)}, f32[8,128]{1,0:T(8,128)}) custom-call(bf16[16,128,512]{2,1,0:T(8,128)(2,1)} %bitcast.4, f32[16,512]{1,0:T(8,128)} %get-tuple-element.35.refs_1_.left_ref, bf16[2,3,3,512,512]{4,3,2,1,0:T(8,128)(2,1)} %air_hbm.1, bf16[2,3,3,256,256]{4,3,2,1,0:T(8,128)(2,1)} %sea_hbm.1), custom_call_target="tpu_custom_call" | custom-call | flops 4831838208 | bytes 7864320 | tf_op jit(solution)/shard_map/conv_inside/pallas_call | solution.py:529
  29.9 2.7 %collective-permute-done.1.lists_ref = s32[3,16]{1,0:T(4,128)S(1)} collective-permute-done((s32[3,16]{1,0:T(4,128)}, s32[3,16]{1,0:T(4,128)S(1)}, u32[]{:S(2)}, u32[]{:S(2)}) %collective-permute-start.1) | collective-permute-done | bytes 224 | tf_op jit(solution)/shard_map/ppermute | solution.py:873
  32.6 0.0 collective-permute-done.3.above_ref.top_ref
  32.6 0.0 collective-permute-done.4.below_ref.bottom_ref
  32.6 0.0 collective-permute-done.2.dense_ref
  32.7 0.5 copy-done.15
  33.2 0.1 copy-done.11
  33.3 0.1 copy-done.12
  33.3 0.3 copy-done.9
  33.6 2.6 %pack.1 = (bf16[16,192,256]{2,1,0:T(8,128)(2,1)}, f32[18,512]{1,0:T(8,128)}, f32[18,512]{1,0:T(8,128)}) custom-call(s32[3,16]{1,0:T(4,128)} %copy-done.15, bf16[16,96,256]{2,1,0:T(8,128)(2,1)} %copy-done.9, bf16[128,512]{1,0:T(8,128)(2,1)} %copy-done.11, bf16[128,512]{1,0:T(8,128)(2,1)} %copy-done.12, f32[16,512]{1,0:T(8,128)} %get-tuple-element.35.refs_1_.left_ref, ...), custom_call_target="tpu_custom_call" | custom-call | tf_op jit(solution)/shard_map/pack/pallas_call | solution.py:270
  36.2 0.0 all-to-all-done
  36.2 0.9 copy-done.10
  37.1 6.8 %all-to-all-start.1 = ((bf16[16,192,256]{2,1,0:T(8,128)(2,1)}), bf16[16,192,256]{2,1,0:T(8,128)(2,1)S(1)}, u32[]{:S(2)}, u32[]{:S(2)}) async-start(bf16[16,192,256]{2,1,0:T(8,128)(2,1)} %get-tuple-element.38), calls=%async_computation.1 | async-start | bytes 3145728 | tf_op jit(solution)/shard_map/all_to_all | solution.py:881
  43.9 0.4 collective-permute-start
  44.3 1.7 %collective-permute-start.5 = (f32[18,512]{1,0:T(8,128)S(1)}, f32[18,512]{1,0:T(8,128)S(1)}, u32[]{:S(2)}, u32[]{:S(2)}) collective-permute-start(f32[18,512]{1,0:T(8,128)S(1)} %copy-done.17), channel_id=1, source_target_pairs={{0,1},{1,2},{2,3},{3,0},{4,5},{5,6},{6,7},{7,4},{8,9},{9,10},{10,1... | collective-permute-start | bytes 110600 | tf_op jit(solution)/shard_map/ppermute | solution.py:893
  46.0 0.0 collective-permute-start.6
  46.0 10.6 %conv_inside.3 = (f32[16,128,512]{2,1,0:T(8,128)}, bf16[3,3,512,512]{3,2,1,0:T(8,128)(2,1)}) custom-call(bf16[16,128,512]{2,1,0:T(8,128)(2,1)} %bitcast.5, f32[16,128,512]{2,1,0:T(8,128)} %get-tuple-element.39.refs_1_, bf16[2,3,3,512,512]{4,3,2,1,0:T(8,128)(2,1)} %air_hbm.1, bf16[2,3,3,256,256]{4,3,2,1,0:T(8,128)(2,1)} %sea_hbm.1), custom_call_target="tpu_custom_call", output_to_operand_aliasing={{0}: (1, {})} | custom-call | flops 4831838208 | bytes 7864320 | tf_op jit(solution)/shard_map/conv_inside/pallas_call | solution.py:529
  56.6 0.0 collective-permute-done.5.left_ref
  56.6 0.0 collective-permute-done.6.right_ref
  56.7 0.6 copy-done.13
  57.3 0.0 copy-done.14
  57.3 5.4 %add_edges.1.refs_2_._ = f32[16,128,512]{2,1,0:T(8,128)} custom-call(f32[16,128,512]{2,1,0:T(8,128)} %get-tuple-element.40.sum_in_hbm, bf16[128,512]{1,0:T(8,128)(2,1)} %copy-done.11, bf16[128,512]{1,0:T(8,128)(2,1)} %copy-done.12, f32[18,512]{1,0:T(8,128)} %copy-done.13, f32[18,512]{1,0:T(8,128)} %copy-done.14, ...), custom_call_target="tpu_custom_call", output_to_operand_aliasing={{}: (0, {})} | custom-call | tf_op jit(solution)/shard_map/add_edges/pallas_call | solution.py:672
  62.7 0.0 collective-permute-done.refs_1_
  62.7 0.9 slice.3
  63.7 0.6 reshape.8.refs_0_
  64.3 4.3 %update.2 = (bf16[4,128,512]{2,1,0:T(8,128)(2,1)}, bf16[128,512]{1,0:T(8,128)(2,1)}, bf16[128,512]{1,0:T(8,128)(2,1)}) custom-call(s32[32]{0:T(128)} %reshape.8.refs_0_, bf16[16,80,256]{2,1,0:T(8,128)(2,1)} %collective-permute-done.refs_1_, f32[16,128,512]{2,1,0:T(8,128)} %add_edges.1.refs_2_._, s32[16,256]{1,0:T(8,128)} %water_ref.5, bf16[256,512]{1,0:T(8,128)(2,1)} %refs_4_.3), custom_call_target="tpu_custom_call" | custom-call | tf_op jit(solution)/shard_map/update/pallas_call | solution.py:824
  68.6 3.1 %collective-permute-start.7 = (bf16[128,512]{1,0:T(8,128)(2,1)}, bf16[128,512]{1,0:T(8,128)(2,1)S(1)}, u32[]{:S(2)}, u32[]{:S(2)}) collective-permute-start(bf16[128,512]{1,0:T(8,128)(2,1)} %get-tuple-element.45), channel_id=1, source_target_pairs={{0,4},{4,8},{8,12},{1,5},{5,9},{9,13},{2,6},{6,10},{10,14},{3,7},{... | collective-permute-start | bytes 393224 | tf_op jit(solution)/shard_map/ppermute | solution.py:886
  71.7 2.2 %collective-permute-start.8 = (bf16[128,512]{1,0:T(8,128)(2,1)}, bf16[128,512]{1,0:T(8,128)(2,1)S(1)}, u32[]{:S(2)}, u32[]{:S(2)}) collective-permute-start(bf16[128,512]{1,0:T(8,128)(2,1)} %get-tuple-element.46), channel_id=1, source_target_pairs={{4,0},{8,4},{12,8},{5,1},{9,5},{13,9},{6,2},{10,6},{14,10},{7,3},{... | collective-permute-start | bytes 393224 | tf_op jit(solution)/shard_map/ppermute | solution.py:887
  73.9 2.2 %copy-done = f32[16,128,512]{2,1,0:T(8,128)S(1)} copy-done((f32[16,128,512]{2,1,0:T(8,128)S(1)}, f32[16,128,512]{2,1,0:T(8,128)}, u32[]{:S(2)}) %copy-start) | copy-done | bytes 4194328
  76.1 1.0 %copy-done.5 = bf16[4,128,512]{2,1,0:T(8,128)(2,1)S(1)} copy-done((bf16[4,128,512]{2,1,0:T(8,128)(2,1)S(1)}, bf16[4,128,512]{2,1,0:T(8,128)(2,1)}, u32[]{:S(2)}) %copy-start.5) | copy-done | bytes 524312
  77.2 2.0 %copy-done.1 = f32[16,128,512]{2,1,0:T(8,128)} copy-done((f32[16,128,512]{2,1,0:T(8,128)}, f32[16,128,512]{2,1,0:T(8,128)S(1)}, u32[]{:S(2)}) %copy-start.1) | copy-done | bytes 4194328
  79.2 1.8 %collective-permute-done.7.refs_6_.above_ref = bf16[128,512]{1,0:T(8,128)(2,1)S(1)} collective-permute-done((bf16[128,512]{1,0:T(8,128)(2,1)}, bf16[128,512]{1,0:T(8,128)(2,1)S(1)}, u32[]{:S(2)}, u32[]{:S(2)}) %collective-permute-start.7) | collective-permute-done | bytes 131104 | tf_op jit(solution)/shard_map/ppermute | solution.py:886
  81.0 1.7 %collective-permute-done.8.refs_7_.below_ref = bf16[128,512]{1,0:T(8,128)(2,1)S(1)} collective-permute-done((bf16[128,512]{1,0:T(8,128)(2,1)}, bf16[128,512]{1,0:T(8,128)(2,1)S(1)}, u32[]{:S(2)}, u32[]{:S(2)}) %collective-permute-start.8) | collective-permute-done | bytes 131104 | tf_op jit(solution)/shard_map/ppermute | solution.py:887
  82.7 0.0 all-to-all-done.1.refs_1_
  82.7 2.2 %copy-done.2 = f32[16,128,512]{2,1,0:T(8,128)S(1)} copy-done((f32[16,128,512]{2,1,0:T(8,128)S(1)}, f32[16,128,512]{2,1,0:T(8,128)}, u32[]{:S(2)}) %copy-start.2) | copy-done | bytes 4194328
  84.9 2.8 %update.3 = (bf16[16,128,512]{2,1,0:T(8,128)(2,1)S(1)}, f32[18,512]{1,0:T(8,128)S(1)}, f32[18,512]{1,0:T(8,128)S(1)}) custom-call(s32[32]{0:T(128)S(1)} %copy-done.8, bf16[16,192,256]{2,1,0:T(8,128)(2,1)S(1)} %all-to-all-done.1.refs_1_, f32[16,128,512]{2,1,0:T(8,128)S(1)} %copy-done.2, s32[16,256]{1,0:T(8,128)S(1)} %copy-done.7, ...), custom_call_target="tpu_custom_call" | custom-call | tf_op jit(solution)/shard_map/update/pallas_call | solution.py:824
  87.7 1.0 collective-permute-start.10
  88.7 1.2 %collective-permute-start.9 = (f32[18,512]{1,0:T(8,128)S(1)}, f32[18,512]{1,0:T(8,128)S(1)}, u32[]{:S(2)}, u32[]{:S(2)}) collective-permute-start(f32[18,512]{1,0:T(8,128)S(1)} %get-tuple-element.53), channel_id=1, source_target_pairs={{0,1},{1,2},{2,3},{3,0},{4,5},{5,6},{6,7},{7,4},{8,9},{9,10},{10,1... | collective-permute-start | bytes 110600 | tf_op jit(solution)/shard_map/ppermute | solution.py:893
  90.0 10.8 %last_conv.1 = (bf16[16,128,512]{2,1,0:T(8,128)(2,1)}, f32[2,16,16,512]{3,2,1,0:T(8,128)S(1)}) custom-call(bf16[16,128,512]{2,1,0:T(8,128)(2,1)S(1)} %get-tuple-element.49.x_ref, bf16[128,512]{1,0:T(8,128)(2,1)S(1)} %collective-permute-done.7.refs_6_.above_ref, bf16[128,512]{1,0:T(8,128)(2,1)S(1)} %collective-permute-done.8.refs_7_.below_ref, ...), custom_call_target="tpu_custom_call" | custom-call | flops 9663676416 | bytes 11010048 | tf_op jit(solution)/shard_map/last_conv/pallas_call | solution.py:487
  100.8 0.0 collective-permute-done.9.left_ref
  100.8 1.3 %fix_sides.1 = bf16[16,128,512]{2,1,0:T(8,128)(2,1)} custom-call(bf16[16,128,512]{2,1,0:T(8,128)(2,1)} %get-tuple-element.51.out_in_hbm, f32[2,16,16,512]{3,2,1,0:T(8,128)S(1)} %get-tuple-element.52.sides_ref, f32[18,512]{1,0:T(8,128)S(1)} %collective-permute-done.9.left_ref, ...), custom_call_target="tpu_custom_call", output_to_operand_aliasing={{}: (0, {})} | custom-call | tf_op jit(solution)/shard_map/fix_sides/pallas_call | solution.py:603
  (28 shorter events, 0.1 us)
Async XLA Ops:
  7.0 29.2 %all-to-all-start = ((bf16[16,80,256]{2,1,0:T(8,128)(2,1)}), bf16[16,80,256]{2,1,0:T(8,128)(2,1)S(1)}, u32[]{:S(2)}, u32[]{:S(2)}) async-start(bf16[16,80,256]{2,1,0:T(8,128)(2,1)} %get-tuple-element.30), calls=%async_computation | async-start | bytes 1310720 | tf_op jit(solution)/shard_map/all_to_all | solution.py:881
  13.6 19.1 %collective-permute-start.2 = (bf16[16,96,256]{2,1,0:T(8,128)(2,1)}, bf16[16,96,256]{2,1,0:T(8,128)(2,1)S(1)}, u32[]{:S(2)}, u32[]{:S(2)}) collective-permute-start(bf16[16,96,256]{2,1,0:T(8,128)(2,1)} %get-tuple-element.32), channel_id=1, source_target_pairs={{0,16},{16,0},{1,17},{17,1},{2,18},{18,2},{3,19},{19,3},{4,20},{20... | collective-permute-start | bytes 2359304 | tf_op jit(solution)/shard_map/ppermute | solution.py:873
  14.0 18.7 %collective-permute-start.3 = (bf16[128,512]{1,0:T(8,128)(2,1)}, bf16[128,512]{1,0:T(8,128)(2,1)S(1)}, u32[]{:S(2)}, u32[]{:S(2)}) collective-permute-start(bf16[128,512]{1,0:T(8,128)(2,1)} %get-tuple-element.33), channel_id=1, source_target_pairs={{0,4},{4,8},{8,12},{1,5},{5,9},{9,13},{2,6},{6,10},{10,14},{3,7},{... | collective-permute-start | bytes 393224 | tf_op jit(solution)/shard_map/ppermute | solution.py:886
  17.0 15.6 %collective-permute-start.4 = (bf16[128,512]{1,0:T(8,128)(2,1)}, bf16[128,512]{1,0:T(8,128)(2,1)S(1)}, u32[]{:S(2)}, u32[]{:S(2)}) collective-permute-start(bf16[128,512]{1,0:T(8,128)(2,1)} %get-tuple-element.34), channel_id=1, source_target_pairs={{4,0},{8,4},{12,8},{5,1},{9,5},{13,9},{6,2},{10,6},{14,10},{7,3},{... | collective-permute-start | bytes 393224 | tf_op jit(solution)/shard_map/ppermute | solution.py:887
  19.2 13.4 %collective-permute-start.1 = (s32[3,16]{1,0:T(4,128)}, s32[3,16]{1,0:T(4,128)S(1)}, u32[]{:S(2)}, u32[]{:S(2)}) collective-permute-start(s32[3,16]{1,0:T(4,128)} %get-tuple-element.31), channel_id=1, source_target_pairs={{0,16},{16,0},{1,17},{17,1},{2,18},{18,2},{3,19},{19,3},{4,20},{20... | collective-permute-start | bytes 584 | tf_op jit(solution)/shard_map/ppermute | solution.py:873
  32.6 0.6 copy-start.15
  32.6 0.7 copy-start.11
  32.6 0.7 copy-start.12
  32.6 1.0 copy-start.9
  36.2 8.1 %copy-start.17 = (f32[18,512]{1,0:T(8,128)S(1)}, f32[18,512]{1,0:T(8,128)}, u32[]{:S(2)}) copy-start(f32[18,512]{1,0:T(8,128)} %get-tuple-element.41) | copy-start | bytes 110596
  36.2 9.8 %copy-start.16 = (f32[18,512]{1,0:T(8,128)S(1)}, f32[18,512]{1,0:T(8,128)}, u32[]{:S(2)}) copy-start(f32[18,512]{1,0:T(8,128)} %get-tuple-element.42) | copy-start | bytes 110596
  36.2 0.9 copy-start.10
  37.1 45.6 %all-to-all-start.1 = ((bf16[16,192,256]{2,1,0:T(8,128)(2,1)}), bf16[16,192,256]{2,1,0:T(8,128)(2,1)S(1)}, u32[]{:S(2)}, u32[]{:S(2)}) async-start(bf16[16,192,256]{2,1,0:T(8,128)(2,1)} %get-tuple-element.38), calls=%async_computation.1 | async-start | bytes 3145728 | tf_op jit(solution)/shard_map/all_to_all | solution.py:881
  43.9 18.8 %collective-permute-start = (bf16[16,80,256]{2,1,0:T(8,128)(2,1)}, bf16[16,80,256]{2,1,0:T(8,128)(2,1)}, u32[]{:S(2)}, u32[]{:S(2)}) collective-permute-start(bf16[16,80,256]{2,1,0:T(8,128)(2,1)} %copy-done.10), channel_id=1, source_target_pairs={{0,16},{16,0},{1,17},{17,1},{2,18},{18,2},{3,19},{19,3},{4,20},{20... | collective-permute-start | bytes 1966088 | tf_op jit(solution)/shard_map/ppermute | solution.py:873
  44.3 12.3 %collective-permute-start.5 = (f32[18,512]{1,0:T(8,128)S(1)}, f32[18,512]{1,0:T(8,128)S(1)}, u32[]{:S(2)}, u32[]{:S(2)}) collective-permute-start(f32[18,512]{1,0:T(8,128)S(1)} %copy-done.17), channel_id=1, source_target_pairs={{0,1},{1,2},{2,3},{3,0},{4,5},{5,6},{6,7},{7,4},{8,9},{9,10},{10,1... | collective-permute-start | bytes 110600 | tf_op jit(solution)/shard_map/ppermute | solution.py:893
  46.0 10.6 %collective-permute-start.6 = (f32[18,512]{1,0:T(8,128)S(1)}, f32[18,512]{1,0:T(8,128)S(1)}, u32[]{:S(2)}, u32[]{:S(2)}) collective-permute-start(f32[18,512]{1,0:T(8,128)S(1)} %copy-done.16), channel_id=1, source_target_pairs={{1,0},{2,1},{3,2},{0,3},{5,4},{6,5},{7,6},{4,7},{9,8},{10,9},{11,1... | collective-permute-start | bytes 110600 | tf_op jit(solution)/shard_map/ppermute | solution.py:894
  56.6 0.6 copy-start.13
  56.6 0.6 copy-start.14
  64.3 9.6 %copy-start.4 = (bf16[256,512]{1,0:T(8,128)(2,1)S(1)}, bf16[256,512]{1,0:T(8,128)(2,1)}, u32[]{:S(2)}) copy-start(bf16[256,512]{1,0:T(8,128)(2,1)} %refs_4_.3) | copy-start | bytes 786436
  68.6 12.3 %collective-permute-start.7 = (bf16[128,512]{1,0:T(8,128)(2,1)}, bf16[128,512]{1,0:T(8,128)(2,1)S(1)}, u32[]{:S(2)}, u32[]{:S(2)}) collective-permute-start(bf16[128,512]{1,0:T(8,128)(2,1)} %get-tuple-element.45), channel_id=1, source_target_pairs={{0,4},{4,8},{8,12},{1,5},{5,9},{9,13},{2,6},{6,10},{10,14},{3,7},{... | collective-permute-start | bytes 393224 | tf_op jit(solution)/shard_map/ppermute | solution.py:886
  71.7 11.0 %collective-permute-start.8 = (bf16[128,512]{1,0:T(8,128)(2,1)}, bf16[128,512]{1,0:T(8,128)(2,1)S(1)}, u32[]{:S(2)}, u32[]{:S(2)}) collective-permute-start(bf16[128,512]{1,0:T(8,128)(2,1)} %get-tuple-element.46), channel_id=1, source_target_pairs={{4,0},{8,4},{12,8},{5,1},{9,5},{13,9},{6,2},{10,6},{14,10},{7,3},{... | collective-permute-start | bytes 393224 | tf_op jit(solution)/shard_map/ppermute | solution.py:887
  73.9 2.2 %copy-start = (f32[16,128,512]{2,1,0:T(8,128)S(1)}, f32[16,128,512]{2,1,0:T(8,128)}, u32[]{:S(2)}) copy-start(f32[16,128,512]{2,1,0:T(8,128)} %add_edges.1.refs_2_._) | copy-start | bytes 12582916
  76.1 1.0 %copy-start.5 = (bf16[4,128,512]{2,1,0:T(8,128)(2,1)S(1)}, bf16[4,128,512]{2,1,0:T(8,128)(2,1)}, u32[]{:S(2)}) copy-start(bf16[4,128,512]{2,1,0:T(8,128)(2,1)} %get-tuple-element.43.new_ref.refs_5_) | copy-start | bytes 1572868
  77.2 5.5 %copy-start.6 = (bf16[4,128,512]{2,1,0:T(8,128)(2,1)S(1)}, bf16[4,128,512]{2,1,0:T(8,128)(2,1)}, u32[]{:S(2)}) copy-start(bf16[4,128,512]{2,1,0:T(8,128)(2,1)} %get-tuple-element.43.new_ref.refs_5_) | copy-start | bytes 1572868
  77.2 5.5 %copy-start.7 = (s32[16,256]{1,0:T(8,128)S(1)}, s32[16,256]{1,0:T(8,128)}, u32[]{:S(2)}) copy-start(s32[16,256]{1,0:T(8,128)} %water_ref.5) | copy-start | bytes 49156
  77.2 5.5 %copy-start.8 = (s32[32]{0:T(128)S(1)}, s32[32]{0:T(128)}, u32[]{:S(2)}) copy-start(s32[32]{0:T(128)} %reshape.8.refs_0_) | copy-start | bytes 388
  77.2 2.0 %copy-start.1 = (f32[16,128,512]{2,1,0:T(8,128)}, f32[16,128,512]{2,1,0:T(8,128)S(1)}, u32[]{:S(2)}) copy-start(f32[16,128,512]{2,1,0:T(8,128)S(1)} %get-tuple-element.44.refs_2_) | copy-start | bytes 12582916
  82.7 2.2 %copy-start.2 = (f32[16,128,512]{2,1,0:T(8,128)S(1)}, f32[16,128,512]{2,1,0:T(8,128)}, u32[]{:S(2)}) copy-start(f32[16,128,512]{2,1,0:T(8,128)} %copy-done.1) | copy-start | bytes 12582916
  84.9 5.0 %copy-start.3 = (bf16[3,3,512,512]{3,2,1,0:T(8,128)(2,1)S(1)}, bf16[3,3,512,512]{3,2,1,0:T(8,128)(2,1)}, u32[]{:S(2)}) copy-start(bf16[3,3,512,512]{3,2,1,0:T(8,128)(2,1)} %get-tuple-element.50.held) | copy-start | bytes 14155780
  87.7 13.1 %collective-permute-start.10 = (f32[18,512]{1,0:T(8,128)S(1)}, f32[18,512]{1,0:T(8,128)S(1)}, u32[]{:S(2)}, u32[]{:S(2)}) collective-permute-start(f32[18,512]{1,0:T(8,128)S(1)} %get-tuple-element.54), channel_id=1, source_target_pairs={{1,0},{2,1},{3,2},{0,3},{5,4},{6,5},{7,6},{4,7},{9,8},{10,9},{11,1... | collective-permute-start | bytes 110600 | tf_op jit(solution)/shard_map/ppermute | solution.py:894
  88.7 12.1 %collective-permute-start.9 = (f32[18,512]{1,0:T(8,128)S(1)}, f32[18,512]{1,0:T(8,128)S(1)}, u32[]{:S(2)}, u32[]{:S(2)}) collective-permute-start(f32[18,512]{1,0:T(8,128)S(1)} %get-tuple-element.53), channel_id=1, source_target_pairs={{0,1},{1,2},{2,3},{3,0},{4,5},{5,6},{6,7},{7,4},{8,9},{9,10},{10,1... | collective-permute-start | bytes 110600 | tf_op jit(solution)/shard_map/ppermute | solution.py:893

commit v4 on v3

--- a/solution.py
+++ b/solution.py
@@ -17,7 +17,7 @@
 SECOND_CELLS = len(SECOND) * BLOCK_COLS
 LABEL_ROWS = 16
 LANES = 128
-VMEM_BYTES = 62 * 2**20
+VMEM_BYTES = 61 * 2**20
 LATE_BYTES = 36 * 2**20
 UPDATE_BYTES = 36 * 2**20
 

time: 103 us -> 102 us (level)
  local copies, waits for them, and re-layouts: 12.7 us -> 11.1 us
  transfers between devices with their start and end apart: 13 -> 13, of which waited for: 3 -> 3; matrix products, arithmetic and copies ran while one was open for 2% -> 1% of each run, Pallas kernels for 42% -> 43%
where the time goes in v4:
time: 102 us
  Pallas kernels  53.1 us (52%)
  starting transfers between devices  30 us (29%)
  local copies, waits for them, and re-layouts  11.1 us (11%)
  waiting for transfers between devices  6.99 us (7%)
    pallas_call x2, Pallas kernels, conv_inside(): pl.pallas_call(functools.partial(inside_conv_kernel, layer, begin, end, k...  20 us
    all_to_all x2, starting transfers between devices, to_owners(): lax.all_to_all(value, ('lat', 'lon'), split_axis=0, concat_axis=0, tiled=...  13.6 us
    pallas_call x1, Pallas kernels, last_conv(): pl.pallas_call(last_conv_kernel, out_shape=(jax.ShapeDtypeStruct(state.sh...  10.8 us
    unnamed x37, local copies, waits for them, and re-layouts  10.4 us
    pallas_call x2, Pallas kernels, update(): pl.pallas_call(functools.partial(update_kernel, block_rows, last), out_sh...  7.14 us
    ppermute x2, starting transfers between devices, rows_beside(): above = lax.ppermute(bottom, 'lat', [(i, i + 1) for i in range(lats - 1)])  6.16 us
    pallas_call x1, Pallas kernels, payloads(): pl.pallas_call(payload_kernel, out_shape=(jax.ShapeDtypeStruct((entries,...  5.72 us
    pallas_call x1, Pallas kernels, add_edges(): pl.pallas_call(functools.partial(sum_edge_kernel, layer), out_shape=jax.S...  5.42 us
  transfers between devices with their start and end apart: 13, of which 3 were waited for; matrix products, arithmetic and copies ran while one was open for 1% of the time, Pallas kernels for 43%

profile of v4, /device:TPU:9, one launch (start us, length us, event | category | flops | bytes accessed | tf_op | source)
XLA Modules:
  0.0 101.5 jit_solution(4836015626150795890)
XLA Ops:
  0.0 1.3 %copy.14.lists_in = s32[1,1,1,3,16]{4,3,2,1,0:T(4,128)} copy(s32[1,1,1,3,16]{4,2,3,1,0:T(1,128)} %param.9) | data formatting | bytes 384 | tf_op args[1]
  1.3 5.7 %payload.1 = (bf16[16,96,256]{2,1,0:T(8,128)(2,1)}, bf16[16,80,256]{2,1,0:T(8,128)(2,1)}, s32[3,16]{1,0:T(4,128)}, bf16[128,512]{1,0:T(8,128)(2,1)}, bf16[128,51...) custom-call(s32[1,1,1,3,16]{4,3,2,1,0:T(4,128)} %copy.14.lists_in, bf16[16,128,512]{2,1,0:T(8,128)(2,1)} %bitcast.3, ...), custom_call_target="tpu_custom_call" | custom-call | tf_op jit(solution)/shard_map/payload/pallas_call | solution.py:214
  7.0 6.6 %all-to-all-start = ((bf16[16,80,256]{2,1,0:T(8,128)(2,1)}), bf16[16,80,256]{2,1,0:T(8,128)(2,1)S(1)}, u32[]{:S(2)}, u32[]{:S(2)}) async-start(bf16[16,80,256]{2,1,0:T(8,128)(2,1)} %get-tuple-element.30), calls=%async_computation | async-start | bytes 1310720 | tf_op jit(solution)/shard_map/all_to_all | solution.py:881
  13.6 0.4 collective-permute-start.2
  14.0 3.1 %collective-permute-start.3 = (bf16[128,512]{1,0:T(8,128)(2,1)}, bf16[128,512]{1,0:T(8,128)(2,1)S(1)}, u32[]{:S(2)}, u32[]{:S(2)}) collective-permute-start(bf16[128,512]{1,0:T(8,128)(2,1)} %get-tuple-element.33), channel_id=1, source_target_pairs={{0,4},{4,8},{8,12},{1,5},{5,9},{9,13},{2,6},{6,10},{10,14},{3,7},{... | collective-permute-start | bytes 393224 | tf_op jit(solution)/shard_map/ppermute | solution.py:886
  17.1 2.2 %collective-permute-start.4 = (bf16[128,512]{1,0:T(8,128)(2,1)}, bf16[128,512]{1,0:T(8,128)(2,1)S(1)}, u32[]{:S(2)}, u32[]{:S(2)}) collective-permute-start(bf16[128,512]{1,0:T(8,128)(2,1)} %get-tuple-element.34), channel_id=1, source_target_pairs={{4,0},{8,4},{12,8},{5,1},{9,5},{13,9},{6,2},{10,6},{14,10},{7,3},{... | collective-permute-start | bytes 393224 | tf_op jit(solution)/shard_map/ppermute | solution.py:887
  19.3 1.2 %collective-permute-start.1 = (s32[3,16]{1,0:T(4,128)}, s32[3,16]{1,0:T(4,128)S(1)}, u32[]{:S(2)}, u32[]{:S(2)}) collective-permute-start(s32[3,16]{1,0:T(4,128)} %get-tuple-element.31), channel_id=1, source_target_pairs={{0,16},{16,0},{1,17},{17,1},{2,18},{18,2},{3,19},{19,3},{4,20},{20... | collective-permute-start | bytes 584 | tf_op jit(solution)/shard_map/ppermute | solution.py:873
  20.4 9.5 %conv_inside.2 = (f32[16,128,512]{2,1,0:T(8,128)}, f32[8,128]{1,0:T(8,128)}) custom-call(bf16[16,128,512]{2,1,0:T(8,128)(2,1)} %bitcast.4, f32[16,512]{1,0:T(8,128)} %get-tuple-element.35.refs_1_.left_ref, bf16[2,3,3,512,512]{4,3,2,1,0:T(8,128)(2,1)} %air_hbm.1, bf16[2,3,3,256,256]{4,3,2,1,0:T(8,128)(2,1)} %sea_hbm.1), custom_call_target="tpu_custom_call" | custom-call | flops 4831838208 | bytes 7864320 | tf_op jit(solution)/shard_map/conv_inside/pallas_call | solution.py:529
  29.9 2.7 %collective-permute-done.1.lists_ref = s32[3,16]{1,0:T(4,128)S(1)} collective-permute-done((s32[3,16]{1,0:T(4,128)}, s32[3,16]{1,0:T(4,128)S(1)}, u32[]{:S(2)}, u32[]{:S(2)}) %collective-permute-start.1) | collective-permute-done | bytes 224 | tf_op jit(solution)/shard_map/ppermute | solution.py:873
  32.6 0.0 collective-permute-done.3.above_ref.top_ref
  32.6 0.0 collective-permute-done.4.below_ref.bottom_ref
  32.7 0.0 collective-permute-done.2.dense_ref
  32.7 0.5 copy-done.15
  33.2 0.1 copy-done.11
  33.3 0.0 copy-done.12
  33.3 0.3 copy-done.9
  33.6 2.6 %pack.1 = (bf16[16,192,256]{2,1,0:T(8,128)(2,1)}, f32[18,512]{1,0:T(8,128)}, f32[18,512]{1,0:T(8,128)}) custom-call(s32[3,16]{1,0:T(4,128)} %copy-done.15, bf16[16,96,256]{2,1,0:T(8,128)(2,1)} %copy-done.9, bf16[128,512]{1,0:T(8,128)(2,1)} %copy-done.11, bf16[128,512]{1,0:T(8,128)(2,1)} %copy-done.12, f32[16,512]{1,0:T(8,128)} %get-tuple-element.35.refs_1_.left_ref, ...), custom_call_target="tpu_custom_call" | custom-call | tf_op jit(solution)/shard_map/pack/pallas_call | solution.py:270
  36.2 0.0 all-to-all-done
  36.2 7.0 %all-to-all-start.1 = ((bf16[16,192,256]{2,1,0:T(8,128)(2,1)}), bf16[16,192,256]{2,1,0:T(8,128)(2,1)S(1)}, u32[]{:S(2)}, u32[]{:S(2)}) async-start(bf16[16,192,256]{2,1,0:T(8,128)(2,1)} %get-tuple-element.38), calls=%async_computation.1 | async-start | bytes 3145728 | tf_op jit(solution)/shard_map/all_to_all | solution.py:881
  43.2 0.4 collective-permute-start
  43.6 1.7 %collective-permute-start.5 = (f32[18,512]{1,0:T(8,128)S(1)}, f32[18,512]{1,0:T(8,128)S(1)}, u32[]{:S(2)}, u32[]{:S(2)}) collective-permute-start(f32[18,512]{1,0:T(8,128)S(1)} %copy-done.17), channel_id=1, source_target_pairs={{0,1},{1,2},{2,3},{3,0},{4,5},{5,6},{6,7},{7,4},{8,9},{9,10},{10,1... | collective-permute-start | bytes 110600 | tf_op jit(solution)/shard_map/ppermute | solution.py:893
  45.3 0.0 collective-permute-start.6
  45.3 10.6 %conv_inside.3 = (f32[16,128,512]{2,1,0:T(8,128)}, bf16[3,3,512,512]{3,2,1,0:T(8,128)(2,1)}) custom-call(bf16[16,128,512]{2,1,0:T(8,128)(2,1)} %bitcast.5, f32[16,128,512]{2,1,0:T(8,128)} %get-tuple-element.39.refs_1_, bf16[2,3,3,512,512]{4,3,2,1,0:T(8,128)(2,1)} %air_hbm.1, bf16[2,3,3,256,256]{4,3,2,1,0:T(8,128)(2,1)} %sea_hbm.1), custom_call_target="tpu_custom_call", output_to_operand_aliasing={{0}: (1, {})} | custom-call | flops 4831838208 | bytes 7864320 | tf_op jit(solution)/shard_map/conv_inside/pallas_call | solution.py:529
  55.9 0.0 collective-permute-done.5.left_ref
  55.9 0.0 collective-permute-done.6.right_ref
  55.9 0.6 copy-done.13
  56.5 0.0 copy-done.14
  56.5 5.4 %add_edges.1.refs_2_._ = f32[16,128,512]{2,1,0:T(8,128)} custom-call(f32[16,128,512]{2,1,0:T(8,128)} %get-tuple-element.40.sum_in_hbm, bf16[128,512]{1,0:T(8,128)(2,1)} %copy-done.11, bf16[128,512]{1,0:T(8,128)(2,1)} %copy-done.12, f32[18,512]{1,0:T(8,128)} %copy-done.13, f32[18,512]{1,0:T(8,128)} %copy-done.14, ...), custom_call_target="tpu_custom_call", output_to_operand_aliasing={{}: (0, {})} | custom-call | tf_op jit(solution)/shard_map/add_edges/pallas_call | solution.py:672
  62.0 0.0 collective-permute-done.refs_1_
  62.0 0.1 slice.3
  62.1 0.6 reshape.8.refs_0_
  62.7 0.1 copy-done.10
  62.8 4.3 %update.2 = (bf16[4,128,512]{2,1,0:T(8,128)(2,1)}, bf16[128,512]{1,0:T(8,128)(2,1)}, bf16[128,512]{1,0:T(8,128)(2,1)}) custom-call(s32[32]{0:T(128)} %reshape.8.refs_0_, bf16[16,80,256]{2,1,0:T(8,128)(2,1)} %copy-done.10, f32[16,128,512]{2,1,0:T(8,128)} %add_edges.1.refs_2_._, s32[16,256]{1,0:T(8,128)} %water_ref.5, bf16[256,512]{1,0:T(8,128)(2,1)} %refs_4_.3), custom_call_target="tpu_custom_call" | custom-call | tf_op jit(solution)/shard_map/update/pallas_call | solution.py:824
  67.2 3.1 %collective-permute-start.7 = (bf16[128,512]{1,0:T(8,128)(2,1)}, bf16[128,512]{1,0:T(8,128)(2,1)S(1)}, u32[]{:S(2)}, u32[]{:S(2)}) collective-permute-start(bf16[128,512]{1,0:T(8,128)(2,1)} %get-tuple-element.45), channel_id=1, source_target_pairs={{0,4},{4,8},{8,12},{1,5},{5,9},{9,13},{2,6},{6,10},{10,14},{3,7},{... | collective-permute-start | bytes 393224 | tf_op jit(solution)/shard_map/ppermute | solution.py:886
  70.2 2.2 %collective-permute-start.8 = (bf16[128,512]{1,0:T(8,128)(2,1)}, bf16[128,512]{1,0:T(8,128)(2,1)S(1)}, u32[]{:S(2)}, u32[]{:S(2)}) collective-permute-start(bf16[128,512]{1,0:T(8,128)(2,1)} %get-tuple-element.46), channel_id=1, source_target_pairs={{4,0},{8,4},{12,8},{5,1},{9,5},{13,9},{6,2},{10,6},{14,10},{7,3},{... | collective-permute-start | bytes 393224 | tf_op jit(solution)/shard_map/ppermute | solution.py:887
  72.5 2.2 %copy-done = f32[16,128,512]{2,1,0:T(8,128)S(1)} copy-done((f32[16,128,512]{2,1,0:T(8,128)S(1)}, f32[16,128,512]{2,1,0:T(8,128)}, u32[]{:S(2)}) %copy-start) | copy-done | bytes 4194328
  74.7 1.0 %copy-done.5 = bf16[4,128,512]{2,1,0:T(8,128)(2,1)S(1)} copy-done((bf16[4,128,512]{2,1,0:T(8,128)(2,1)S(1)}, bf16[4,128,512]{2,1,0:T(8,128)(2,1)}, u32[]{:S(2)}) %copy-start.5) | copy-done | bytes 524312
  75.7 2.0 %copy-done.1 = f32[16,128,512]{2,1,0:T(8,128)} copy-done((f32[16,128,512]{2,1,0:T(8,128)}, f32[16,128,512]{2,1,0:T(8,128)S(1)}, u32[]{:S(2)}) %copy-start.1) | copy-done | bytes 4194328
  77.7 2.5 %collective-permute-done.7.refs_6_.above_ref = bf16[128,512]{1,0:T(8,128)(2,1)S(1)} collective-permute-done((bf16[128,512]{1,0:T(8,128)(2,1)}, bf16[128,512]{1,0:T(8,128)(2,1)S(1)}, u32[]{:S(2)}, u32[]{:S(2)}) %collective-permute-start.7) | collective-permute-done | bytes 131104 | tf_op jit(solution)/shard_map/ppermute | solution.py:886
  80.2 1.7 %collective-permute-done.8.refs_7_.below_ref = bf16[128,512]{1,0:T(8,128)(2,1)S(1)} collective-permute-done((bf16[128,512]{1,0:T(8,128)(2,1)}, bf16[128,512]{1,0:T(8,128)(2,1)S(1)}, u32[]{:S(2)}, u32[]{:S(2)}) %collective-permute-start.8) | collective-permute-done | bytes 131104 | tf_op jit(solution)/shard_map/ppermute | solution.py:887
  82.0 0.0 all-to-all-done.1.refs_1_
  82.0 2.2 %copy-done.2 = f32[16,128,512]{2,1,0:T(8,128)S(1)} copy-done((f32[16,128,512]{2,1,0:T(8,128)S(1)}, f32[16,128,512]{2,1,0:T(8,128)}, u32[]{:S(2)}) %copy-start.2) | copy-done | bytes 4194328
  84.2 2.8 %update.3 = (bf16[16,128,512]{2,1,0:T(8,128)(2,1)S(1)}, f32[18,512]{1,0:T(8,128)S(1)}, f32[18,512]{1,0:T(8,128)S(1)}) custom-call(s32[32]{0:T(128)S(1)} %copy-done.8, bf16[16,192,256]{2,1,0:T(8,128)(2,1)S(1)} %all-to-all-done.1.refs_1_, f32[16,128,512]{2,1,0:T(8,128)S(1)} %copy-done.2, s32[16,256]{1,0:T(8,128)S(1)} %copy-done.7, ...), custom_call_target="tpu_custom_call" | custom-call | tf_op jit(solution)/shard_map/update/pallas_call | solution.py:824
  87.0 1.0 collective-permute-start.10
  87.9 1.2 %collective-permute-start.9 = (f32[18,512]{1,0:T(8,128)S(1)}, f32[18,512]{1,0:T(8,128)S(1)}, u32[]{:S(2)}, u32[]{:S(2)}) collective-permute-start(f32[18,512]{1,0:T(8,128)S(1)} %get-tuple-element.53), channel_id=1, source_target_pairs={{0,1},{1,2},{2,3},{3,0},{4,5},{5,6},{6,7},{7,4},{8,9},{9,10},{10,1... | collective-permute-start | bytes 110600 | tf_op jit(solution)/shard_map/ppermute | solution.py:893
  89.2 10.8 %last_conv.1 = (bf16[16,128,512]{2,1,0:T(8,128)(2,1)}, f32[2,16,16,512]{3,2,1,0:T(8,128)S(1)}) custom-call(bf16[16,128,512]{2,1,0:T(8,128)(2,1)S(1)} %get-tuple-element.49.x_ref, bf16[128,512]{1,0:T(8,128)(2,1)S(1)} %collective-permute-done.7.refs_6_.above_ref, bf16[128,512]{1,0:T(8,128)(2,1)S(1)} %collective-permute-done.8.refs_7_.below_ref, ...), custom_call_target="tpu_custom_call" | custom-call | flops 9663676416 | bytes 11010048 | tf_op jit(solution)/shard_map/last_conv/pallas_call | solution.py:487
  100.0 0.0 collective-permute-done.10.right_ref
  100.0 1.3 %fix_sides.1 = bf16[16,128,512]{2,1,0:T(8,128)(2,1)} custom-call(bf16[16,128,512]{2,1,0:T(8,128)(2,1)} %get-tuple-element.51.out_in_hbm, f32[2,16,16,512]{3,2,1,0:T(8,128)S(1)} %get-tuple-element.52.sides_ref, f32[18,512]{1,0:T(8,128)S(1)} %collective-permute-done.9.left_ref, ...), custom_call_target="tpu_custom_call", output_to_operand_aliasing={{}: (0, {})} | custom-call | tf_op jit(solution)/shard_map/fix_sides/pallas_call | solution.py:603
  (28 shorter events, 0.1 us)
Async XLA Ops:
  7.0 29.2 %all-to-all-start = ((bf16[16,80,256]{2,1,0:T(8,128)(2,1)}), bf16[16,80,256]{2,1,0:T(8,128)(2,1)S(1)}, u32[]{:S(2)}, u32[]{:S(2)}) async-start(bf16[16,80,256]{2,1,0:T(8,128)(2,1)} %get-tuple-element.30), calls=%async_computation | async-start | bytes 1310720 | tf_op jit(solution)/shard_map/all_to_all | solution.py:881
  13.6 19.1 %collective-permute-start.2 = (bf16[16,96,256]{2,1,0:T(8,128)(2,1)}, bf16[16,96,256]{2,1,0:T(8,128)(2,1)S(1)}, u32[]{:S(2)}, u32[]{:S(2)}) collective-permute-start(bf16[16,96,256]{2,1,0:T(8,128)(2,1)} %get-tuple-element.32), channel_id=1, source_target_pairs={{0,16},{16,0},{1,17},{17,1},{2,18},{18,2},{3,19},{19,3},{4,20},{20... | collective-permute-start | bytes 2359304 | tf_op jit(solution)/shard_map/ppermute | solution.py:873
  14.0 18.6 %collective-permute-start.3 = (bf16[128,512]{1,0:T(8,128)(2,1)}, bf16[128,512]{1,0:T(8,128)(2,1)S(1)}, u32[]{:S(2)}, u32[]{:S(2)}) collective-permute-start(bf16[128,512]{1,0:T(8,128)(2,1)} %get-tuple-element.33), channel_id=1, source_target_pairs={{0,4},{4,8},{8,12},{1,5},{5,9},{9,13},{2,6},{6,10},{10,14},{3,7},{... | collective-permute-start | bytes 393224 | tf_op jit(solution)/shard_map/ppermute | solution.py:886
  17.1 15.6 %collective-permute-start.4 = (bf16[128,512]{1,0:T(8,128)(2,1)}, bf16[128,512]{1,0:T(8,128)(2,1)S(1)}, u32[]{:S(2)}, u32[]{:S(2)}) collective-permute-start(bf16[128,512]{1,0:T(8,128)(2,1)} %get-tuple-element.34), channel_id=1, source_target_pairs={{4,0},{8,4},{12,8},{5,1},{9,5},{13,9},{6,2},{10,6},{14,10},{7,3},{... | collective-permute-start | bytes 393224 | tf_op jit(solution)/shard_map/ppermute | solution.py:887
  19.3 13.4 %collective-permute-start.1 = (s32[3,16]{1,0:T(4,128)}, s32[3,16]{1,0:T(4,128)S(1)}, u32[]{:S(2)}, u32[]{:S(2)}) collective-permute-start(s32[3,16]{1,0:T(4,128)} %get-tuple-element.31), channel_id=1, source_target_pairs={{0,16},{16,0},{1,17},{17,1},{2,18},{18,2},{3,19},{19,3},{4,20},{20... | collective-permute-start | bytes 584 | tf_op jit(solution)/shard_map/ppermute | solution.py:873
  32.6 0.6 copy-start.15
  32.6 0.7 copy-start.11
  32.7 0.7 copy-start.12
  32.7 0.9 copy-start.9
  36.2 7.4 %copy-start.17 = (f32[18,512]{1,0:T(8,128)S(1)}, f32[18,512]{1,0:T(8,128)}, u32[]{:S(2)}) copy-start(f32[18,512]{1,0:T(8,128)} %get-tuple-element.41) | copy-start | bytes 110596
  36.2 9.1 %copy-start.16 = (f32[18,512]{1,0:T(8,128)S(1)}, f32[18,512]{1,0:T(8,128)}, u32[]{:S(2)}) copy-start(f32[18,512]{1,0:T(8,128)} %get-tuple-element.42) | copy-start | bytes 110596
  36.2 45.8 %all-to-all-start.1 = ((bf16[16,192,256]{2,1,0:T(8,128)(2,1)}), bf16[16,192,256]{2,1,0:T(8,128)(2,1)S(1)}, u32[]{:S(2)}, u32[]{:S(2)}) async-start(bf16[16,192,256]{2,1,0:T(8,128)(2,1)} %get-tuple-element.38), calls=%async_computation.1 | async-start | bytes 3145728 | tf_op jit(solution)/shard_map/all_to_all | solution.py:881
  43.2 18.8 %collective-permute-start = (bf16[16,80,256]{2,1,0:T(8,128)(2,1)S(1)}, bf16[16,80,256]{2,1,0:T(8,128)(2,1)S(1)}, u32[]{:S(2)}, u32[]{:S(2)}) collective-permute-start(bf16[16,80,256]{2,1,0:T(8,128)(2,1)S(1)} %all-to-all-done), channel_id=1, source_target_pairs={{0,16},{16,0},{1,17},{17,1},{2,18},{18,2},{3,19},{19,3},{4,20},{20... | collective-permute-start | bytes 1966088 | tf_op jit(solution)/shard_map/ppermute | solution.py:873
  43.6 12.3 %collective-permute-start.5 = (f32[18,512]{1,0:T(8,128)S(1)}, f32[18,512]{1,0:T(8,128)S(1)}, u32[]{:S(2)}, u32[]{:S(2)}) collective-permute-start(f32[18,512]{1,0:T(8,128)S(1)} %copy-done.17), channel_id=1, source_target_pairs={{0,1},{1,2},{2,3},{3,0},{4,5},{5,6},{6,7},{7,4},{8,9},{9,10},{10,1... | collective-permute-start | bytes 110600 | tf_op jit(solution)/shard_map/ppermute | solution.py:893
  45.3 10.6 %collective-permute-start.6 = (f32[18,512]{1,0:T(8,128)S(1)}, f32[18,512]{1,0:T(8,128)S(1)}, u32[]{:S(2)}, u32[]{:S(2)}) collective-permute-start(f32[18,512]{1,0:T(8,128)S(1)} %copy-done.16), channel_id=1, source_target_pairs={{1,0},{2,1},{3,2},{0,3},{5,4},{6,5},{7,6},{4,7},{9,8},{10,9},{11,1... | collective-permute-start | bytes 110600 | tf_op jit(solution)/shard_map/ppermute | solution.py:894
  55.9 0.6 copy-start.13
  55.9 0.6 copy-start.14
  62.0 0.8 copy-start.10
  62.8 9.6 %copy-start.4 = (bf16[256,512]{1,0:T(8,128)(2,1)S(1)}, bf16[256,512]{1,0:T(8,128)(2,1)}, u32[]{:S(2)}) copy-start(bf16[256,512]{1,0:T(8,128)(2,1)} %refs_4_.3) | copy-start | bytes 786436
  67.2 13.1 %collective-permute-start.7 = (bf16[128,512]{1,0:T(8,128)(2,1)}, bf16[128,512]{1,0:T(8,128)(2,1)S(1)}, u32[]{:S(2)}, u32[]{:S(2)}) collective-permute-start(bf16[128,512]{1,0:T(8,128)(2,1)} %get-tuple-element.45), channel_id=1, source_target_pairs={{0,4},{4,8},{8,12},{1,5},{5,9},{9,13},{2,6},{6,10},{10,14},{3,7},{... | collective-permute-start | bytes 393224 | tf_op jit(solution)/shard_map/ppermute | solution.py:886
  70.2 11.7 %collective-permute-start.8 = (bf16[128,512]{1,0:T(8,128)(2,1)}, bf16[128,512]{1,0:T(8,128)(2,1)S(1)}, u32[]{:S(2)}, u32[]{:S(2)}) collective-permute-start(bf16[128,512]{1,0:T(8,128)(2,1)} %get-tuple-element.46), channel_id=1, source_target_pairs={{4,0},{8,4},{12,8},{5,1},{9,5},{13,9},{6,2},{10,6},{14,10},{7,3},{... | collective-permute-start | bytes 393224 | tf_op jit(solution)/shard_map/ppermute | solution.py:887
  72.5 2.2 %copy-start = (f32[16,128,512]{2,1,0:T(8,128)S(1)}, f32[16,128,512]{2,1,0:T(8,128)}, u32[]{:S(2)}) copy-start(f32[16,128,512]{2,1,0:T(8,128)} %add_edges.1.refs_2_._) | copy-start | bytes 12582916
  74.7 1.0 %copy-start.5 = (bf16[4,128,512]{2,1,0:T(8,128)(2,1)S(1)}, bf16[4,128,512]{2,1,0:T(8,128)(2,1)}, u32[]{:S(2)}) copy-start(bf16[4,128,512]{2,1,0:T(8,128)(2,1)} %get-tuple-element.43.new_ref.refs_5_) | copy-start | bytes 1572868
  75.7 6.3 %copy-start.6 = (bf16[4,128,512]{2,1,0:T(8,128)(2,1)S(1)}, bf16[4,128,512]{2,1,0:T(8,128)(2,1)}, u32[]{:S(2)}) copy-start(bf16[4,128,512]{2,1,0:T(8,128)(2,1)} %get-tuple-element.43.new_ref.refs_5_) | copy-start | bytes 1572868
  75.7 6.3 %copy-start.7 = (s32[16,256]{1,0:T(8,128)S(1)}, s32[16,256]{1,0:T(8,128)}, u32[]{:S(2)}) copy-start(s32[16,256]{1,0:T(8,128)} %water_ref.5) | copy-start | bytes 49156
  75.7 6.3 %copy-start.8 = (s32[32]{0:T(128)S(1)}, s32[32]{0:T(128)}, u32[]{:S(2)}) copy-start(s32[32]{0:T(128)} %reshape.8.refs_0_) | copy-start | bytes 388
  75.7 2.0 %copy-start.1 = (f32[16,128,512]{2,1,0:T(8,128)}, f32[16,128,512]{2,1,0:T(8,128)S(1)}, u32[]{:S(2)}) copy-start(f32[16,128,512]{2,1,0:T(8,128)S(1)} %get-tuple-element.44.refs_2_) | copy-start | bytes 12582916
  82.0 2.2 %copy-start.2 = (f32[16,128,512]{2,1,0:T(8,128)S(1)}, f32[16,128,512]{2,1,0:T(8,128)}, u32[]{:S(2)}) copy-start(f32[16,128,512]{2,1,0:T(8,128)} %copy-done.1) | copy-start | bytes 12582916
  84.2 5.0 %copy-start.3 = (bf16[3,3,512,512]{3,2,1,0:T(8,128)(2,1)S(1)}, bf16[3,3,512,512]{3,2,1,0:T(8,128)(2,1)}, u32[]{:S(2)}) copy-start(bf16[3,3,512,512]{3,2,1,0:T(8,128)(2,1)} %get-tuple-element.50.held) | copy-start | bytes 14155780
  87.0 13.0 %collective-permute-start.10 = (f32[18,512]{1,0:T(8,128)S(1)}, f32[18,512]{1,0:T(8,128)S(1)}, u32[]{:S(2)}, u32[]{:S(2)}) collective-permute-start(f32[18,512]{1,0:T(8,128)S(1)} %get-tuple-element.54), channel_id=1, source_target_pairs={{1,0},{2,1},{3,2},{0,3},{5,4},{6,5},{7,6},{4,7},{9,8},{10,9},{11,1... | collective-permute-start | bytes 110600 | tf_op jit(solution)/shard_map/ppermute | solution.py:894
  87.9 12.1 %collective-permute-start.9 = (f32[18,512]{1,0:T(8,128)S(1)}, f32[18,512]{1,0:T(8,128)S(1)}, u32[]{:S(2)}, u32[]{:S(2)}) collective-permute-start(f32[18,512]{1,0:T(8,128)S(1)} %get-tuple-element.53), channel_id=1, source_target_pairs={{0,1},{1,2},{2,3},{3,0},{4,5},{5,6},{6,7},{7,4},{8,9},{9,10},{10,1... | collective-permute-start | bytes 110600 | tf_op jit(solution)/shard_map/ppermute | solution.py:893
